TPU v7x, 256 devices: a whole 4x4x8 slice. The times are simulated.
256 devices in a mesh: seq: 64 (over z, x, core), head: 4 (over y).
Axes of the slice: x: 4, y: 4, z: 8, core: 2. Of those that a mesh axis runs over, the one named last changes fastest.
Arguments:
- q_in: bfloat16 [8192, 2560], P('seq', 'head'), may hold values from -240 to 240
- k_in: bfloat16 [8192, 512], P('seq', 'head'), may hold values from -4 to 4
- v_in: bfloat16 [8192, 512], P('seq', 'head'), may hold values from -6 to 6
- x_in: bfloat16 [8192, 4096], P('seq', 'head'), may hold values from -400 to 400
- z_in: bfloat16 [8192, 4096], P('seq', 'head'), may hold values from -6 to 6
- b_in: bfloat16 [8192, 256], P('seq'), may hold values from -0.375 to 0.375
- c_in: bfloat16 [8192, 256], P('seq'), may hold values from -0.09375 to 0.09375
- dt_raw: float32 [8192, 64], P('seq', 'head'), may hold values from -4 to 4096
- a_log: float32 [64], P('head'), may hold values from -14 to -1.5
- d_skip: float32 [64], P('head'), may hold values from 0.5 to 1.5
- ssm_gain: float32 [4096], P('head'), may hold values from 0.5 to 1.5
- doc_start: int32 [8192], P('seq'), may hold values from 0 to 8191, as said below
Outputs:
- attn_out: bfloat16 [8192, 2560], P('seq', 'head')
- ssm_out: bfloat16 [8192, 4096], P('seq', 'head')
- attn_range: float32 [2, 2560], P(None, 'head')
- ssm_range: float32 [2, 4096], P(None, 'head')
Inputs may be any that keep to these rules, and one draw needn't show every extreme that they name: doc_start[0] = 0; for every later position t, doc_start[t] is t or doc_start[t - 1].
All inputs are finite; a program needn't handle non-finite values.
Results may differ from a plain program's by a relative error of at most 0.0055.
Values may be sent and summed in bfloat16 or wider, within the bound.
No kernel may reach another device: no remote copies, remote signals or barrier semaphores. Data moves between devices by JAX's collectives and lax.ppermute only.
A program may use at most 256 MiB of HBM per device.

v0:
```python
import math

import jax
import jax.numpy as jnp
from jax import lax
from jax.sharding import PartitionSpec as P

QH = 20
KVH = 4
HD = 128
SH = 64
HP = 64


epsilon = 1e-05
floor_score = -1e30


def carried_in(value, axis, join, neutral):
    count, mine = (lax.axis_size(axis), lax.axis_index(axis))
    pieces = jax.tree.map(lambda part: lax.all_gather(part, axis), value)
    total = jax.tree.map(
        lambda part, zero: jnp.full_like(part, 0) + jnp.asarray(zero, part.dtype), value, neutral
    )

    def hop(position, total):
        longer = join(total, jax.tree.map(lambda part: part[position], pieces))
        return jax.tree.map(lambda new, old: jnp.where(position < mine, new, old), longer, total)

    return lax.fori_loop(0, count - 1, hop, total)


def empty_carry(row_count, kv_heads, group_size, head_width):
    return (
        jnp.full((kv_heads, group_size, row_count), floor_score, jnp.float32),
        jnp.zeros((kv_heads, group_size, row_count), jnp.float32),
        jnp.zeros((row_count, kv_heads, group_size, head_width), jnp.float32),
    )


def absorb_block(carry, member, key_part, value_part, start):
    queries, q_pos, q_doc = member
    count = key_part.shape[0]
    kv_heads = queries.shape[1]
    head_width = queries.shape[3]
    key_pos = start + jnp.arange(count, dtype=jnp.int32)

    def update(state):
        highest, totals, accum = state
        scores = jnp.einsum(
            "rcgd,scd->cgrs",
            queries,
            key_part.reshape(count, kv_heads, head_width),
            preferred_element_type=jnp.float32,
        ) * head_width ** (-0.5)
        visible = (key_pos[None, :] <= q_pos[:, None]) & (key_pos[None, :] >= q_doc[:, None])
        scores = jnp.where(visible, scores, floor_score)
        new_high = jnp.maximum(highest, jnp.max(scores, axis=-1))
        factor = jnp.exp(highest - new_high)
        weights = jnp.where(visible, jnp.exp(scores - new_high[..., None]), 0.0)
        totals = totals * factor + jnp.sum(weights, axis=-1)
        mixed = jnp.einsum(
            "cgrs,scd->rcgd",
            weights.astype(jnp.bfloat16),
            value_part.reshape(count, kv_heads, head_width),
            preferred_element_type=jnp.float32,
        )
        accum = accum * jnp.transpose(factor, (2, 0, 1))[..., None] + mixed
        return (new_high, totals, accum)

    active = (start <= q_pos[-1]) & (start + count > q_doc[0])
    return lax.cond(active, update, lambda state: state, carry)


def absorb_keys(carries, members, key_rows, value_rows):
    count = key_rows.shape[0]
    size_step = math.gcd(count, 2048)

    def absorb_all(state, key_part, value_part, begin_at):
        return tuple(
            (
                absorb_block(state[number], members[number], key_part, value_part, begin_at)
                for number in range(len(members))
            )
        )

    split_keys = key_rows.reshape(count // size_step, size_step, key_rows.shape[1])
    split_values = value_rows.reshape(count // size_step, size_step, value_rows.shape[1])

    def stepper(state, bundle):
        index_value, key_part, value_part = bundle
        return (absorb_all(state, key_part, value_part, index_value * size_step), None)

    steps_index = jnp.arange(count // size_step, dtype=jnp.int32)
    carries, _ = lax.scan(stepper, carries, (steps_index, split_keys, split_values))
    return carries


def finish_rows(carry):
    highest, totals, accum = carry
    result = accum / jnp.transpose(totals, (2, 0, 1))[..., None]
    return result.reshape(result.shape[0], -1).astype(jnp.bfloat16)


def block_summands(x_blk, b_blk, c_blk, dt_blk, a_log, doc_blk, begin):
    tok_rows = x_blk.shape[0]
    head_count = dt_blk.shape[1]
    step_len = jax.nn.softplus(dt_blk)
    log_decay = -step_len * jnp.exp(a_log)[None, :]
    running = jnp.cumsum(log_decay, axis=0)
    offsets = jnp.arange(tok_rows, dtype=jnp.int32)
    same_doc = (offsets[None, :] <= offsets[:, None]) & (
        begin + offsets[None, :] >= doc_blk[:, None]
    )
    spread = jnp.where(same_doc[:, :, None], running[:, None, :] - running[None, :, :], 0.0)
    decay = jnp.where(same_doc[:, :, None], jnp.exp(spread), 0.0)
    inner = jnp.dot(c_blk, b_blk.T, preferred_element_type=jnp.float32)
    mixing = inner[:, :, None] * decay * step_len[None, :, :]
    values = x_blk.astype(jnp.float32).reshape(tok_rows, head_count, -1)
    intra = jnp.einsum("ijh,jhp->ihp", mixing, values, precision=lax.Precision.HIGHEST)
    reach = jnp.where(
        (begin + offsets >= doc_blk[tok_rows - 1])[:, None],
        jnp.exp(running[tok_rows - 1][None, :] - running) * step_len,
        0.0,
    )
    local_state = jnp.dot(
        b_blk.astype(jnp.float32).T,
        (values * reach[:, :, None]).reshape(tok_rows, -1),
        precision=lax.Precision.HIGHEST,
    )
    through = jnp.where(doc_blk[tok_rows - 1] < begin, jnp.exp(running[tok_rows - 1]), 0.0)
    entering = jnp.where((doc_blk < begin)[:, None], jnp.exp(running), 0.0)
    return (values, intra, local_state, through, entering)


def chain_combine(earlier, later):
    return (earlier[0] * later[0], earlier[1] * later[0][None, :] + later[1])


def body(q_in, k_in, v_in, x_in, z_in, b_in, c_in, dt_raw, a_log, d_skip, ssm_gain, doc_start):
    tok_rows = q_in.shape[0]
    kv_heads = k_in.shape[1] // HD
    group_size = QH // KVH
    begin = lax.axis_index("seq") * tok_rows
    queries = q_in.reshape(tok_rows, kv_heads, group_size, HD)
    positions = begin + jnp.arange(tok_rows, dtype=jnp.int32)
    members = [(queries, positions, doc_start)]
    initial = tuple(
        (empty_carry(member[0].shape[0], kv_heads, group_size, HD) for member in members)
    )
    carries = absorb_keys(
        initial,
        members,
        lax.all_gather(k_in, "seq", axis=0, tiled=True),
        lax.all_gather(v_in, "seq", axis=0, tiled=True),
    )
    attn_out = finish_rows(carries[0])
    values, intra, local_state, through, entering = block_summands(
        x_in, b_in, c_in, dt_raw, a_log, doc_start, begin
    )
    head_width = values.shape[2]
    through_wide = jnp.repeat(through, head_width)
    identity = (jnp.ones_like(through_wide), jnp.zeros_like(local_state))
    _, state_in = carried_in((through_wide, local_state), "seq", chain_combine, identity)
    carried = jnp.dot(c_in.astype(jnp.float32), state_in, precision=lax.Precision.HIGHEST)
    carried = carried.reshape(tok_rows, values.shape[1], head_width) * entering[:, :, None]
    mixed = intra + carried + d_skip[None, :, None] * values
    gated = mixed.reshape(tok_rows, -1) * jax.nn.silu(z_in.astype(jnp.float32))
    square_sum = lax.psum(jnp.sum(gated * gated, axis=1), "head")
    ssm_out = (
        gated * lax.rsqrt(square_sum[:, None] / (SH * HP) + epsilon) * ssm_gain[None, :]
    ).astype(jnp.bfloat16)
    attn_wide = attn_out.astype(jnp.float32)
    ssm_wide = ssm_out.astype(jnp.float32)
    lowest = lax.pmin((jnp.min(attn_wide, axis=0), jnp.min(ssm_wide, axis=0)), "seq")
    largest = lax.pmax((jnp.max(attn_wide, axis=0), jnp.max(ssm_wide, axis=0)), "seq")
    attn_range = jnp.stack([lowest[0], largest[0]])
    ssm_range = jnp.stack([lowest[1], largest[1]])
    return (attn_out, ssm_out, attn_range, ssm_range)


def solution(mesh):
    return jax.shard_map(
        body,
        mesh=mesh,
        in_specs=(
            P("seq", "head"),
            P("seq", "head"),
            P("seq", "head"),
            P("seq", "head"),
            P("seq", "head"),
            P("seq", None),
            P("seq", None),
            P("seq", "head"),
            P("head"),
            P("head"),
            P("head"),
            P("seq"),
        ),
        out_specs=(P("seq", "head"), P("seq", "head"), P(None, "head"), P(None, "head")),
        check_vma=False,
    )
```

profile of v0, /device:TPU:1, one launch (start us, length us, event | category | flops | bytes accessed | tf_op | source)
XLA Modules:
  0.0 949.0 jit_solution(1375596253418774121)
XLA Ops:
  16.8 48.6 %all-gather.1 = f32[64,1,1024]{2,1,0:T(1,128)S(1)} all-gather(f32[1,1,1024]{2,1,0:T(1,128)S(1)} %reshape.177), channel_id=1, replica_groups=mesh['seq'=64,'head'=4] {'seq'}, dimensions={0}, use_global_device_ids=true | all-gather | bytes 266240 | tf_op jit(solution)/shard_map/all_gather | solution.py:21
  68.1 24.2 %all-gather.8.cloned.1.call-done = bf16[8192,128]{1,0:T(8,128)(2,1)} async-done(((bf16[128,128]{1,0:T(8,128)(2,1)}), bf16[8192,128]{1,0:T(8,128)(2,1)}) %all-gather.8.cloned.1.call-update) | async-done | bytes 2097168 | tf_op jit(solution)/shard_map/all_gather | solution.py:155
  92.3 2.9 copy.53
  95.2 74.8 %all-gather.6.cloned.1.call-done = bf16[8192,128]{1,0:T(8,128)(2,1)} async-done(((bf16[128,128]{1,0:T(8,128)(2,1)}), bf16[8192,128]{1,0:T(8,128)(2,1)}) %all-gather.6.cloned.1.call-update) | async-done | bytes 2097168 | tf_op jit(solution)/shard_map/all_gather | solution.py:154
  171.3 18.9 %while.28 = (s32[]{:T(128)}, f32[1,5,128]{2,1,0:T(8,128)S(1)}, f32[1,5,128]{2,1,0:T(8,128)S(1)}, f32[128,1,5,128]{0,3,2,1:T(8,128)}, s32[4]{0:T(128)}, /*index=5...) while((s32[]{:T(128)}, f32[1,5,128]{2,1,0:T(8,128)S(1)}, ...), condition=%wide.region_5.6_spmd, body=%wide.region_0.5_spmd.sunk | while | flops 689082240 | bytes 21345172 | solution.py:95
  174.5 6.0 conditional.2
  192.4 233.1 %all-gather.10.cloned.1.call-done = f32[16384,1024]{0,1:T(8,128)} async-done(((f32[256,1024]{0,1:T(8,128)}), f32[16384,1024]{0,1:T(8,128)}) %all-gather.10.cloned.1.call-update) | async-done | bytes 67108880 | tf_op jit(solution)/shard_map/all_gather | solution.py:21
  425.5 65.8 %copy.70 = f32[16384,1024]{1,0:T(8,128)} copy(f32[16384,1024]{0,1:T(8,128)} %all-gather.10.cloned.1.call-done) | data formatting | bytes 134217728
  491.4 183.9 %while.29 = (s32[]{:T(128)}, f32[256,1024]{1,0:T(8,128)S(1)}, s32[]{:T(128)}, f32[64,1024]{1,0:T(8,128)}, f32[64,256,1024]{2,1,0:T(8,128)}, /*index=5*/s32[]{:T(128)}, s32[]{:T(128)}) while((s32[]{:T(128)}, f32[256,1024]{1,0:T(8,128)S(1)}, s32[]{:T(128)}, f32[64,1024]{1,0:T(8,128)}, f32[64,256,1024]{2,1,0:T(8,128)}, ...), condition=%wide.region_8.9_spmd.clone, body=%wide.region_7.8_spmd.clone.sunk | while | flops 1048580 | bytes 3158121 | solution.py:30
  495.1 2.1 fusion.56
  498.0 2.1 fusion.56
  503.8 2.1 fusion.56
  512.6 2.1 fusion.56
  518.4 2.1 fusion.56
  521.4 2.1 fusion.56
  527.2 2.1 fusion.56
  536.0 2.1 fusion.56
  541.8 2.1 fusion.56
  544.7 2.1 fusion.56
  550.6 2.1 fusion.56
  553.5 2.1 fusion.56
  678.2 8.4 psum.7
  687.0 127.7 %all-reduce.1 = (f32[1,640]{1,0:T(1,128)S(1)}, f32[1,1024]{1,0:T(1,128)S(1)}) all-reduce(f32[1,640]{1,0:T(1,128)S(1)} %bitcast.147, f32[1,1024]{1,0:T(1,128)S(1)} %bitcast.144), channel_id=1, replica_groups=mesh['seq'=64,'head'=4] {'seq'}, use_global_device_ids=true, to_apply=%region_12.13 | all-reduce | flops 1664 | bytes 13312 | tf_op jit(solution)/shard_map/pmin | solution.py:175
  814.7 126.6 %all-reduce = (f32[1,640]{1,0:T(1,128)S(1)}, f32[1,1024]{1,0:T(1,128)S(1)}) all-reduce(f32[1,640]{1,0:T(1,128)S(1)} %bitcast.148, f32[1,1024]{1,0:T(1,128)S(1)} %bitcast.146), channel_id=1, replica_groups=mesh['seq'=64,'head'=4] {'seq'}, use_global_device_ids=true, to_apply=%region_14.15 | all-reduce | flops 1664 | bytes 13312 | tf_op jit(solution)/shard_map/pmax | solution.py:176
  (216 shorter events, 190.1 us)
Async XLA Ops:
  7.2 7.2 copy-start
  7.2 60.6 %copy-start.9 = (s32[128]{0:T(128)S(1)}, s32[128]{0:T(128)}, u32[]{:S(2)}) copy-start(s32[128]{0:T(128)} %param.29) | copy-start | bytes 1540
  7.2 60.3 %copy-start.8 = (bf16[128,640]{1,0:T(8,128)(2,1)S(1)}, bf16[128,640]{1,0:T(8,128)(2,1)}, u32[]{:S(2)}) copy-start(bf16[128,640]{1,0:T(8,128)(2,1)} %param.18) | copy-start | bytes 491524
  7.2 60.7 %copy-start.7 = (bf16[128,256]{1,0:T(8,128)(2,1)S(1)}, bf16[128,256]{1,0:T(8,128)(2,1)}, u32[]{:S(2)}) copy-start(bf16[128,256]{1,0:T(8,128)(2,1)} %param.24) | copy-start | bytes 196612
  7.2 85.1 %all-gather.8.cloned.1.call-start = ((), (), s32[]{:S(2)}) async-start(), calls=%async_computation.1 | async-start | bytes 2129920 | tf_op jit(solution)/shard_map/all_gather | solution.py:155
  7.9 162.1 %all-gather.6.cloned.1.call-start = ((), (), s32[]{:S(2)}) async-start(), calls=%async_computation | async-start | bytes 2129920 | tf_op jit(solution)/shard_map/all_gather | solution.py:154
  8.7 416.8 %all-gather.10.cloned.1.call-start = ((), (), s32[]{:S(2)}) async-start(), calls=%async_computation.2 | async-start | bytes 68157440 | tf_op jit(solution)/shard_map/all_gather | solution.py:21
  14.3 1.6 copy-start.3
  174.9 3.4 copy-start.1
  179.7 0.7 copy-start.2
  491.3 185.0 %copy-start.4 = (bf16[128,1024]{0,1:T(8,128)(2,1)S(1)}, bf16[128,1024]{0,1:T(8,128)(2,1)}, u32[]{:S(2)}) copy-start(bf16[128,1024]{0,1:T(8,128)(2,1)} %copy-done.3) | copy-start | bytes 786436
  491.3 185.0 %copy-start.10 = (f32[128,16]{0,1:T(8,128)S(1)}, f32[128,16]{0,1:T(8,128)}, u32[]{:S(2)}) copy-start(f32[128,16]{0,1:T(8,128)} %copy.61) | copy-start | bytes 24580
  491.3 185.0 %copy-start.11 = (f32[128,16]{0,1:T(8,128)S(1)}, f32[128,16]{0,1:T(8,128)}, u32[]{:S(2)}) copy-start(f32[128,16]{0,1:T(8,128)} %copy.66) | copy-start | bytes 24580
  491.3 185.0 %copy-start.13 = (f32[16]{0:T(128)S(1)}, f32[16]{0:T(128)}, u32[]{:S(2)}) copy-start(f32[16]{0:T(128)} %param.27) | copy-start | bytes 196
  675.3 2.7 copy-start.6
  675.3 11.4 %copy-start.12 = (f32[1024]{0:T(1024)S(1)}, f32[1024]{0:T(1024)}, u32[]{:S(2)}) copy-start(f32[1024]{0:T(1024)} %param.28) | copy-start | bytes 12292
  686.9 255.6 %copy-start.5 = (bf16[128,1024]{1,0:T(8,128)(2,1)}, bf16[128,1024]{1,0:T(8,128)(2,1)S(1)}, u32[]{:S(2)}) copy-start(bf16[128,1024]{1,0:T(8,128)(2,1)S(1)} %get-tuple-element.351) | copy-start | bytes 786436
Sparse Core Ops, SparseCore 0:
  10.8 81.4 all-gather.7
  95.1 74.9 all-gather.5
  172.7 252.8 all-gather.9
where the time goes:
time: 957 us; the launch traced here: 949 us
  waiting for transfers between devices  334 us (35%)
  blocking collectives  311 us (32%)
  other arithmetic  141 us (15%)
  local copies, waits for them, and re-layouts  134 us (14%)
  between operations  14.7 us (2%)
    all_gather x1, waiting for transfers between devices, carried_in(): pieces = jax.tree.map(lambda part: lax.all_gather(part, axis), value)  233 us
    select_n x63, other arithmetic, hop(): jnp.where(position < mine, new, old)  134 us
    pmin x1, blocking collectives, body(): lax.pmin((jnp.min(attn_wide, axis=0), jnp.min(ssm_wide, axis=0)), 'seq')  128 us
    pmax x1, blocking collectives, body(): lax.pmax((jnp.max(attn_wide, axis=0), jnp.max(ssm_wide, axis=0)), 'seq')  127 us
    all_gather x1, waiting for transfers between devices, body(): lax.all_gather(k_in, 'seq', axis=0, tiled=True)  74.8 us
    unnamed x33, local copies, waits for them, and re-layouts  69.6 us
    all_gather x1, blocking collectives, carried_in(): pieces = jax.tree.map(lambda part: lax.all_gather(part, axis), value)  48.6 us
    dynamic_slice x63, local copies, waits for them, and re-layouts, hop(): longer = join(total, jax.tree.map(lambda part: part[position], pieces))  48.4 us
  transfers between devices with their start and end apart: 3, of which 3 were waited for; matrix products, arithmetic and copies ran while one was open for 3% of the time, Pallas kernels for 0%

commit v1 on v0

v1 whole, which is shorter than its diff:
```python
import functools
import math

import jax
import jax.numpy as jnp
from jax import lax
from jax.experimental import pallas as pl
from jax.experimental.pallas import tpu as pltpu
from jax.sharding import PartitionSpec as P

TOK = 128
GROUP = 5
HD = 128
HEADS = 16
HP = 64
NS = 256
COLS = 1024
HALF = 512
HALF_HEADS = 8
ALL_COLS = 4096
CHIPS = 32
EPSILON = 1e-05
FLOOR = -1e30
SCORE_SCALE = math.log2(math.e) / math.sqrt(HD)
F32 = jnp.float32
BF16 = jnp.bfloat16
HIGH = lax.Precision.HIGHEST

VMEM = pl.BlockSpec(memory_space=pltpu.VMEM)
SMEM = pl.BlockSpec(memory_space=pltpu.SMEM)
ANY = pl.BlockSpec(memory_space=pl.ANY)


def mm(a, b, dims=((1,), (0,)), precision=None):
    return lax.dot_general(a, b, (dims, ((), ())), precision=precision, preferred_element_type=F32)


def split_mm(a, b, dims=((1,), (0,)), which=0):
    wide = (a, b)[which]
    top = wide.astype(BF16)
    rest = (wide - top.astype(F32)).astype(BF16)
    if which == 0:
        return mm(top, b, dims) + mm(rest, b, dims)
    return mm(a, top, dims) + mm(a, rest, dims)


def iota(shape, dim):
    return lax.broadcasted_iota(jnp.int32, shape, dim)


def spread_heads(first_head, width):
    return jnp.where(
        iota((HEADS, width), 0) == first_head + iota((HEADS, width), 1) // HP, 1.0, 0.0
    ).astype(F32)


def step_sizes(dt_ref, a_ref):
    raw = dt_ref[...]
    step_t = jnp.maximum(raw, 0.0) + jnp.log1p(jnp.exp(-jnp.abs(raw)))
    rows, cols = iota((TOK, TOK), 0), iota((TOK, TOK), 1)
    eye = jnp.where(rows == cols, 1.0, 0.0).astype(F32)
    rate = jnp.exp(jnp.transpose(jnp.broadcast_to(a_ref[...], (TOK, HEADS))))
    upper = jnp.where(rows <= cols, 1.0, 0.0).astype(F32)
    running_t = mm(-step_t * rate, upper, precision=HIGH)
    both = mm(eye, jnp.concatenate([step_t, running_t], axis=0), ((1,), (1,)), precision=HIGH)
    return step_t, running_t, both[:, :HEADS], both[:, HEADS : 2 * HEADS]


def position(doc_smem):
    return lax.axis_index("seq"), doc_smem[0, 0], doc_smem[0, TOK - 1]


def local_kernel(scal, x_ref, b_ref, dt_ref, a_ref, keep_ref, send_ref):
    me, _, last_doc = position(scal)
    begin = me * TOK
    core = me % 2
    _, _, step_len, running = step_sizes(dt_ref, a_ref)
    last = running[TOK - 1 : TOK, :]
    live = begin + iota((TOK, HEADS), 0) >= last_doc
    reach = jnp.where(live, jnp.exp(last - running) * step_len, 0.0)
    through = jnp.where(last_doc < begin, jnp.exp(last), 0.0)
    stacked = jnp.concatenate([reach, jnp.broadcast_to(through, (8, HEADS))], axis=0)
    for half, out in ((core, keep_ref), (1 - core, send_ref)):
        wide = mm(stacked, spread_heads(half * HALF_HEADS, HALF), precision=HIGH)
        values = x_ref[:, pl.ds(pl.multiple_of(half * HALF, HALF), HALF)].astype(F32)
        out[0:NS, :] = split_mm(b_ref[...], values * wide[:TOK], ((0,), (0,)), which=1)
        out[NS : NS + 8, :] = wide[TOK:]


def intra_kernel(x_ref, b_ref, c_ref, dt_ref, a_ref, skip_ref, doc_ref, y_ref, enter_ref):
    begin = lax.axis_index("seq") * TOK
    step_t, running_t, _, running = step_sizes(dt_ref, a_ref)
    rows, cols = iota((TOK, TOK), 0), iota((TOK, TOK), 1)
    doc = jnp.transpose(jnp.broadcast_to(doc_ref[...], (TOK, TOK)).astype(F32)).astype(jnp.int32)
    same_doc = (cols <= rows) & (begin + cols >= doc)
    earlier = same_doc & (cols < rows)
    enter_ref[...] = jnp.where(doc[:, :HEADS] < begin, jnp.exp(running), 0.0)
    inner = jnp.where(same_doc, mm(c_ref[...], b_ref[...], ((1,), (1,))), 0.0)
    skip = mm(
        jnp.broadcast_to(skip_ref[...], (8, HEADS)), spread_heads(0, COLS), precision=HIGH
    )[0:1]
    left = iota((TOK, 2 * HP), 1) < HP
    for pair in range(HEADS // 2):
        parts = []
        for h in (2 * pair, 2 * pair + 1):
            gap = jnp.where(earlier, running[:, h : h + 1] - running_t[h : h + 1, :], 0.0)
            parts.append(inner * jnp.exp(gap) * step_t[h : h + 1, :])
        at = slice(pair * 2 * HP, (pair + 1) * 2 * HP)
        values = x_ref[:, at]
        both = split_mm(jnp.concatenate(parts, axis=0), values)
        y_ref[:, at] = jnp.where(left, both[:TOK], both[TOK:]) + skip[:, at] * values.astype(F32)


def chip_kernel(keep_ref, got_ref, out_ref):
    core = lax.axis_index("seq") % 2
    first = core == 0
    t_own, t_other = keep_ref[NS : NS + 1, :], got_ref[NS : NS + 1, :]
    f_own = jnp.where(first, t_other, 1.0)
    f_other = jnp.where(first, 1.0, t_own)
    through = t_own * t_other
    lines = [through[:, tile * 128 : tile * 128 + 128] for tile in range(4)]
    lines = jnp.concatenate(lines + [jnp.zeros((4, 128), F32)], axis=0)
    for chip in range(CHIPS):
        rows = slice(chip * 8, chip * 8 + 8)
        out_ref[chip, :, 0:HALF] = keep_ref[rows, :] * f_own + got_ref[rows, :] * f_other
        out_ref[chip, :, HALF : HALF + 128] = lines


def prefix_kernel(in_ref, out_ref):
    total = jnp.zeros((8, HALF), F32)
    for chip in range(CHIPS):
        out_ref[chip] = total
        if chip < CHIPS - 1:
            lines = in_ref[chip, :, HALF : HALF + 128]
            through = jnp.concatenate([lines[n : n + 1] for n in range(4)], axis=1)
            total = total * through + in_ref[chip, :, 0:HALF]


def enter_kernel(pre_ref, keep_ref, got_ref, mine_ref, send_ref):
    core = lax.axis_index("seq") % 2
    first = core == 0
    t_first = jnp.where(first, keep_ref[NS : NS + 1, :], got_ref[NS : NS + 1, :])
    for chip in range(CHIPS):
        rows = slice(chip * 8, chip * 8 + 8)
        before = pre_ref[chip]
        state = jnp.where(first, keep_ref[rows, :], got_ref[rows, :])
        after = before * t_first + state
        mine_ref[rows, :] = jnp.where(first, before, after)
        send_ref[rows, :] = jnp.where(first, after, before)


def mix_kernel(y_ref, enter_ref, c_ref, z_ref, mine_ref, got_ref, gated_ref, sq_ref):
    core = lax.axis_index("seq") % 2
    squares = jnp.zeros((TOK, 128), F32)
    for half, state in ((core, mine_ref), (1 - core, got_ref)):
        at = pl.ds(pl.multiple_of(half * HALF, HALF), HALF)
        wide = mm(enter_ref[...], spread_heads(half * HALF_HEADS, HALF), precision=HIGH)
        mixed = y_ref[:, at] + split_mm(c_ref[...], state[...], which=1) * wide
        gate = z_ref[:, at].astype(F32)
        gated = mixed * (gate / (1.0 + jnp.exp(-gate)))
        gated_ref[:, at] = gated
        power = gated * gated
        for tile in range(HALF // 128):
            squares += power[:, tile * 128 : tile * 128 + 128]
    ones = jnp.ones((8, 128), F32)
    sq_ref[...] = mm(ones, squares, ((1,), (1,)), precision=HIGH)


def finish_kernel(gated_ref, s0, s1, s2, s3, gain_ref, attn_rng, out_ref, rng_ref, lines):
    total = s0[...] + s1[...] + s2[...] + s3[...]
    scale = lax.rsqrt(total[0:1, :] / ALL_COLS + EPSILON)
    scale = jnp.transpose(jnp.broadcast_to(scale, (TOK, TOK)))
    lines[16:32, :] = attn_rng[...]
    for tile in range(COLS // 128):
        at = slice(tile * 128, tile * 128 + 128)
        out = (gated_ref[:, at] * scale * gain_ref[:, at]).astype(BF16)
        out_ref[:, at] = out
        wide = out.astype(F32)
        lines[tile : tile + 1, :] = jnp.min(wide, axis=0, keepdims=True)
        lines[8 + tile : 9 + tile, :] = jnp.min(-wide, axis=0, keepdims=True)
    packed = lines[...].astype(BF16)
    for dest in range(8):
        rng_ref[dest] = packed


def least_kernel(in_ref, out_ref):
    least = in_ref[0].astype(F32)
    for part in range(1, 8):
        least = jnp.minimum(least, in_ref[part].astype(F32))
    for dest in range(8):
        out_ref[dest] = least.astype(BF16)


def range_kernel(in_ref, attn_ref, ssm_ref):
    least = in_ref[0].astype(F32)
    for part in range(1, 8):
        least = jnp.minimum(least, in_ref[part].astype(F32))
    for tile in range(COLS // 128):
        at = slice(tile * 128, tile * 128 + 128)
        ssm_ref[0:1, at] = least[tile : tile + 1]
        ssm_ref[1:2, at] = -least[8 + tile : 9 + tile]
    for tile in range(GROUP):
        at = slice(tile * 128, tile * 128 + 128)
        attn_ref[0:1, at] = least[16 + tile : 17 + tile]
        attn_ref[1:2, at] = -least[21 + tile : 22 + tile]


def attn_kernel(scal, q_ref, doc_ref, *rest):
    parts, (out_ref, rng_ref, held, highest, totals, accum, sems) = rest[:8], rest[8:]
    copies = [
        pltpu.make_async_copy(part, held.at[n // 4, pl.ds((n % 4) * 8, 8)], sems.at[n])
        for n, part in enumerate(parts)
    ]
    for copy in copies:
        copy.start()
    me, first_doc, last_doc = position(scal)
    core, mine = me % 2, me // 2
    z_mine, x_mine = mine // 4, mine % 4
    doc = jnp.transpose(jnp.broadcast_to(doc_ref[...], (TOK, TOK)).astype(F32)).astype(jnp.int32)
    doc = jnp.concatenate([doc, doc], axis=1)
    q_pos = me * TOK + iota((TOK, 2 * TOK), 0)
    lane = iota((TOK, 2 * TOK), 1)
    key_lane = jnp.where(lane < TOK, core * TOK + lane, (1 - core) * TOK + lane - TOK)
    highest[...] = jnp.full(highest.shape, FLOOR, F32)
    totals[...] = jnp.zeros(totals.shape, F32)
    accum[...] = jnp.zeros(accum.shape, F32)
    for copy in copies:
        copy.wait()

    def absorb(chip, masked):
        flip = z_mine ^ (chip // 4)
        place = (flip % 2) * 4 + (flip // 2 % 2) * 2 + flip // 4
        slot = (x_mine ^ (chip % 4)) * 8 + place
        near, far = held[0, slot], held[1, slot]
        keys = jnp.concatenate([near[:, :HD], far[:, :HD]], axis=0)
        vals = jnp.concatenate([near[:, HD:], far[:, HD:]], axis=0)
        if masked:
            key_pos = chip * 2 * TOK + key_lane
            visible = (key_pos <= q_pos) & (key_pos >= doc)
        for g in range(GROUP):
            scores = mm(q_ref[:, g * HD : (g + 1) * HD], keys, ((1,), (1,)))
            if masked:
                scores = jnp.where(visible, scores, FLOOR)
            old = highest[g]
            new = jnp.maximum(old, jnp.max(scores, axis=1, keepdims=True))
            factor = jnp.exp2((old - new) * SCORE_SCALE)
            wide = jnp.concatenate([new, new], axis=1)
            weights = jnp.exp2((scores - wide) * SCORE_SCALE)
            if masked:
                weights = jnp.where(visible, weights, 0.0)
            highest[g] = new
            totals[g] = totals[g] * factor + (weights[:, :TOK] + weights[:, TOK:])
            accum[g] = accum[g] * factor + mm(weights.astype(BF16), vals)

    low = first_doc // (2 * TOK)
    middle = jnp.minimum((last_doc + 2 * TOK - 1) // (2 * TOK), mine)

    def edge(n, _):
        absorb(jnp.where(n == 0, mine, low + n - 1), True)
        return 0

    def inside(chip, _):
        absorb(chip, False)
        return 0

    lax.fori_loop(0, middle - low + 1, edge, 0)
    lax.fori_loop(middle, mine, inside, 0)
    rng_ref[...] = jnp.zeros(rng_ref.shape, F32)
    for g in range(GROUP):
        total = jnp.sum(totals[g], axis=1, keepdims=True)
        out = (accum[g] / total).astype(BF16)
        out_ref[:, g * HD : (g + 1) * HD] = out
        wide = out.astype(F32)
        rng_ref[g : g + 1, :] = jnp.min(wide, axis=0, keepdims=True)
        rng_ref[GROUP + g : GROUP + g + 1, :] = jnp.min(-wide, axis=0, keepdims=True)


def call(kernel, outs, specs, name, flops=0, data=0, exps=0, scratch=()):
    return pl.pallas_call(
        kernel,
        out_shape=[jax.ShapeDtypeStruct(shape, dtype) for shape, dtype in outs],
        in_specs=list(specs),
        out_specs=[VMEM] * len(outs),
        scratch_shapes=list(scratch),
        compiler_params=pltpu.CompilerParams(vmem_limit_bytes=40 * 2**20),
        cost_estimate=pl.CostEstimate(flops=flops, bytes_accessed=data, transcendentals=exps),
        name=name,
    )


def swap(value, bit):
    count = lax.axis_size("seq")
    return lax.ppermute(value, "seq", [(i, i ^ bit) for i in range(count)])


def body(q_in, k_in, v_in, x_in, z_in, b_in, c_in, dt_raw, a_log, d_skip, ssm_gain, doc_start):
    dt_t = dt_raw.T
    doc_row = doc_start[None, :]
    a_row, skip_row, gain_row = a_log[None, :], d_skip[None, :], ssm_gain[None, :]
    same_core = [[i for i in range(64) if i % 2 == core] for core in range(2)]
    plane = [[z * 8 + n for n in range(8)] for z in range(8)]
    column = [[z * 8 + n for z in range(8)] for n in range(8)]

    near = jnp.concatenate([k_in, v_in], axis=1)[None]
    for bit in (32, 16, 8):
        near = jnp.concatenate([near, swap(near, bit)], axis=0)
    own = [near] + [swap(near, bit) for bit in (2, 4, 6)]
    other = [swap(part, 1) for part in own]

    keep, send = call(
        local_kernel, [((NS + 8, HALF), F32)] * 2, [SMEM] + [VMEM] * 4, "local_state",
        flops=2 * 2 * TOK * NS * COLS, data=2**21,
    )(doc_row, x_in, b_in, dt_t, a_row)
    got = swap(send, 1)
    (chunks,) = call(
        chip_kernel, [((CHIPS, 8, HALF + 128), F32)], [VMEM] * 2, "chip_state", data=2**20
    )(keep, got)
    chunks = lax.all_to_all(chunks, "seq", 0, 0, tiled=True, axis_index_groups=same_core)
    (prefix,) = call(prefix_kernel, [((CHIPS, 8, HALF), F32)], [VMEM], "prefix", data=2**19)(chunks)
    prefix = lax.all_to_all(prefix, "seq", 0, 0, tiled=True, axis_index_groups=same_core)
    mine, theirs = call(
        enter_kernel, [((NS, HALF), F32)] * 2, [VMEM] * 3, "state_in", data=2**20
    )(prefix, keep, got)
    got_state = swap(theirs, 1)
    y_part, enter = call(
        intra_kernel, [((TOK, COLS), F32), ((TOK, HEADS), F32)], [VMEM] * 7, "intra",
        flops=4 * TOK * TOK * COLS * 2, data=2**20, exps=TOK * TOK * HEADS,
    )(x_in, b_in, c_in, dt_t, a_row, skip_row, doc_row)
    gated, square = call(
        mix_kernel, [((TOK, COLS), F32), ((8, TOK), F32)], [VMEM] * 6, "mix",
        flops=2 * TOK * NS * COLS, data=2**21,
    )(y_part, enter, c_in, z_in, mine, got_state)
    squares = [square] + [
        lax.ppermute(square, "head", [(i, i ^ bit) for i in range(4)]) for bit in (1, 2, 3)
    ]

    attn_out, attn_rng = call(
        attn_kernel, [((TOK, GROUP * HD), BF16), ((16, 128), F32)],
        [SMEM] + [VMEM] * 2 + [ANY] * 8, "attention",
        flops=4 * TOK * GROUP * HD * 8192, data=2**23, exps=TOK * GROUP * 8192,
        scratch=[
            pltpu.VMEM((2, CHIPS, TOK, 2 * HD), BF16),
            pltpu.VMEM((GROUP, TOK, HD), F32),
            pltpu.VMEM((GROUP, TOK, HD), F32),
            pltpu.VMEM((GROUP, TOK, HD), F32),
            pltpu.SemaphoreType.DMA((8,)),
        ],
    )(doc_row, q_in, doc_row, *own, *other)

    ssm_out, rng = call(
        finish_kernel, [((TOK, COLS), BF16), ((8, 32, 128), BF16)], [VMEM] * 7, "finish",
        data=2**20, scratch=[pltpu.VMEM((32, 128), F32)],
    )(gated, *squares, gain_row, attn_rng)
    rng = lax.all_to_all(rng, "seq", 0, 0, tiled=True, axis_index_groups=plane)
    (rng,) = call(least_kernel, [((8, 32, 128), BF16)], [VMEM], "least")(rng)
    rng = lax.all_to_all(rng, "seq", 0, 0, tiled=True, axis_index_groups=column)
    attn_range, ssm_range = call(
        range_kernel, [((2, GROUP * HD), F32), ((2, COLS), F32)], [VMEM], "ranges"
    )(rng)
    return (attn_out, ssm_out, attn_range, ssm_range)


def solution(mesh):
    return jax.shard_map(
        body,
        mesh=mesh,
        in_specs=(
            P("seq", "head"),
            P("seq", "head"),
            P("seq", "head"),
            P("seq", "head"),
            P("seq", "head"),
            P("seq", None),
            P("seq", None),
            P("seq", "head"),
            P("head"),
            P("head"),
            P("head"),
            P("seq"),
        ),
        out_specs=(P("seq", "head"), P("seq", "head"), P(None, "head"), P(None, "head")),
        check_vma=False,
    )
```

time: 957 us -> 142 us (0.15)
  waiting for transfers between devices: 334 us -> 51.8 us
  blocking collectives: 311 us -> 33.8 us
  other arithmetic: 141 us -> 0.11 us
  local copies, waits for them, and re-layouts: 134 us -> 4.78 us
  starting transfers between devices: 0.11 us -> 40.8 us
  between operations: 14.7 us -> 0.87 us
  Pallas kernels: 0 us -> 11.2 us
    all_gather x3 -> x0, waiting for transfers between devices: 332 us -> none  [the longest x1 233 us: carried_in(): pieces = jax.tree.map(lambda part: lax.all_gather(part, axis), value)]
    select_n x65 -> x0, other arithmetic: 135 us -> none  [the longest x63 134 us: hop(): jnp.where(position < mine, new, old)]
    pmin x1 -> x0, blocking collectives: 128 us -> none  [body(): lax.pmin((jnp.min(attn_wide, axis=0), jnp.min(ssm_wide, axis=0)), 'seq')]
    pmax x1 -> x0, blocking collectives: 127 us -> none  [body(): lax.pmax((jnp.max(attn_wide, axis=0), jnp.max(ssm_wide, axis=0)), 'seq')]
    unnamed x33 -> x30, local copies, waits for them, and re-layouts: 69.6 us -> 4.78 us
    dynamic_slice x67 -> x0, local copies, waits for them, and re-layouts: 53.4 us -> none  [the longest x63 48.4 us: hop(): longer = join(total, jax.tree.map(lambda part: part[position], pieces))]
    ppermute x0 -> x15, waiting for transfers between devices: none -> 51.8 us  [the longest x12 51.8 us: swap(): return lax.ppermute(value, 'seq', [(i, i ^ bit) for i in range(count)])]
    all_gather x1 -> x0, blocking collectives: 48.6 us -> none  [carried_in(): pieces = jax.tree.map(lambda part: lax.all_gather(part, axis), value)]
  transfers between devices with their start and end apart: 3 -> 17, of which waited for: 3 -> 4; matrix products, arithmetic and copies ran while one was open for 3% -> 0% of each run, Pallas kernels for 0% -> 5%
where the time goes in v1:
time: 142 us; the launch traced here: 143 us
  waiting for transfers between devices  51.8 us (36%)
  starting transfers between devices  40.8 us (29%)
  blocking collectives  33.8 us (24%)
  Pallas kernels  11.2 us (8%)
  local copies, waits for them, and re-layouts  4.78 us (3%)
    ppermute x12, waiting for transfers between devices, swap(): return lax.ppermute(value, 'seq', [(i, i ^ bit) for i in range(count)])  51.8 us
    all_to_all x1, blocking collectives, body(): rng = lax.all_to_all(rng, 'seq', 0, 0, tiled=True, axis_index_groups=column)  22.9 us
    ppermute x12, starting transfers between devices, swap(): return lax.ppermute(value, 'seq', [(i, i ^ bit) for i in range(count)])  20 us
    all_to_all x1, blocking collectives, body(): rng = lax.all_to_all(rng, 'seq', 0, 0, tiled=True, axis_index_groups=plane)  10.9 us
    all_to_all x1, starting transfers between devices, body(): lax.all_to_all(chunks, 'seq', 0, 0, tiled=True, axis_index_groups=same_core)  9.43 us
    all_to_all x1, starting transfers between devices, body(): lax.all_to_all(prefix, 'seq', 0, 0, tiled=True, axis_index_groups=same_core)  7.94 us
    unnamed x30, local copies, waits for them, and re-layouts  4.78 us
    ppermute x3, starting transfers between devices, body(): lax.ppermute(square, 'head', [(i, i ^ bit) for i in range(4)])  3.41 us
  transfers between devices with their start and end apart: 17, of which 4 were waited for; matrix products, arithmetic and copies ran while one was open for 0% of the time, Pallas kernels for 5%

profile of v1, /device:TPU:1, one launch (start us, length us, event | category | flops | bytes accessed | tf_op | source)
XLA Modules:
  0.0 143.4 jit_solution(16575918709781338438)
XLA Ops:
  1.3 0.9 copy-done.3
  3.8 2.3 %local_state.1 = (f32[264,512]{1,0:T(8,128)S(1)}, f32[264,512]{1,0:T(8,128)S(1)}) custom-call(s32[1,128]{1,0:T(1,128)S(1)} %bitcast.13, bf16[128,1024]{1,0:T(8,128)(2,1)S(1)} %copy-done.3, bf16[128,256]{1,0:T(8,128)(2,1)S(1)} %copy-done.6, f32[16,128]{1,0:T(8,128)S(1)} %bitcast.8, f32[1,16]{1,0:T(1,128)S(1)} %bitcast.10), custom_call_target="tpu_custom_call" | custom-call | flops 134217728 | bytes 2097152 | tf_op jit(solution)/shard_map/local_state/pallas_call | solution.py:310
  6.1 3.3 %collective-permute-start.10 = (f32[264,512]{1,0:T(8,128)S(1)}, f32[264,512]{1,0:T(8,128)S(1)}, u32[]{:S(2)}, u32[]{:S(2)}) collective-permute-start(f32[264,512]{1,0:T(8,128)S(1)} %get-tuple-element.22), channel_id=1, source_target_pairs={{0,4},{4,0},{8,12},{12,8},{16,20},{20,16},{24,28},{28,24},{32,36},... | collective-permute-start | bytes 1622024 | tf_op jit(solution)/shard_map/ppermute | solution.py:293
  9.4 1.6 %collective-permute-done.10.got_ref = f32[264,512]{1,0:T(8,128)S(1)} collective-permute-done((f32[264,512]{1,0:T(8,128)S(1)}, f32[264,512]{1,0:T(8,128)S(1)}, u32[]{:S(2)}, u32[]{:S(2)}) %collective-permute-start.10) | collective-permute-done | bytes 540704 | tf_op jit(solution)/shard_map/ppermute | solution.py:293
  11.0 0.9 chip_state.1
  11.9 9.4 %all-to-all-start = ((f32[32,8,640]{2,1,0:T(8,128)}), f32[32,8,640]{2,1,0:T(8,128)S(1)}, u32[]{:S(2)}, u32[]{:S(2)}) async-start(f32[32,8,640]{2,1,0:T(8,128)} %chip_state.1), calls=%async_computation | async-start | bytes 1310720 | tf_op jit(solution)/shard_map/all_to_all | solution.py:318
  21.4 5.2 %collective-permute-start = (bf16[1,128,256]{2,1,0:T(8,128)(2,1)S(1)}, bf16[1,128,256]{2,1,0:T(8,128)(2,1)S(1)}, u32[]{:S(2)}, u32[]{:S(2)}) collective-permute-start(bf16[1,128,256]{2,1,0:T(8,128)(2,1)S(1)} %maximum_bitcast_fusion), channel_id=1, source_target_pairs={{0,128},{4,132},{8,136},{12,140},{16,144},{20,148},{24,152},{28,15... | collective-permute-start | bytes 196616 | tf_op jit(solution)/shard_map/ppermute | solution.py:293
  26.6 14.9 %collective-permute-done = bf16[1,128,256]{2,1,0:T(8,128)(2,1)S(1)} collective-permute-done((bf16[1,128,256]{2,1,0:T(8,128)(2,1)S(1)}, bf16[1,128,256]{2,1,0:T(8,128)(2,1)S(1)}, u32[]{:S(2)}, u32[]{:S(2)}) %collective-permute-start) | collective-permute-done | bytes 65568 | tf_op jit(solution)/shard_map/ppermute | solution.py:293
  41.5 1.3 collective-permute-start.1
  43.7 7.9 %all-to-all-start.1 = ((f32[32,8,512]{2,1,0:T(8,128)}), f32[32,8,512]{2,1,0:T(8,128)S(1)}, u32[]{:S(2)}, u32[]{:S(2)}) async-start(f32[32,8,512]{2,1,0:T(8,128)} %prefix.1), calls=%async_computation.1 | async-start | bytes 1048576 | tf_op jit(solution)/shard_map/all_to_all | solution.py:320
  51.7 1.3 collective-permute-start.2
  53.0 16.7 %collective-permute-done.2 = bf16[4,128,256]{2,1,0:T(8,128)(2,1)S(1)} collective-permute-done((bf16[4,128,256]{2,1,0:T(8,128)(2,1)S(1)}, bf16[4,128,256]{2,1,0:T(8,128)(2,1)S(1)}, u32[]{:S(2)}, u32[]{:S(2)}) %collective-permute-start.2) | collective-permute-done | bytes 262176 | tf_op jit(solution)/shard_map/ppermute | solution.py:293
  69.8 2.5 %collective-permute-start.5 = (bf16[8,128,256]{2,1,0:T(8,128)(2,1)S(1)}, bf16[8,128,256]{2,1,0:T(8,128)(2,1)S(1)}, u32[]{:S(2)}, u32[]{:S(2)}) collective-permute-start(bf16[8,128,256]{2,1,0:T(8,128)(2,1)S(1)} %pad_maximum_fusion.rest_0_), channel_id=1, source_target_pairs={{0,24},{4,28},{8,16},{12,20},{16,8},{20,12},{24,0},{28,4},{32,56},... | collective-permute-start | bytes 1572872 | tf_op jit(solution)/shard_map/ppermute | solution.py:293
  73.3 2.6 %collective-permute-start.11 = (f32[256,512]{1,0:T(8,128)S(1)}, f32[256,512]{1,0:T(8,128)S(1)}, u32[]{:S(2)}, u32[]{:S(2)}) collective-permute-start(f32[256,512]{1,0:T(8,128)S(1)} %get-tuple-element.24), channel_id=1, source_target_pairs={{0,4},{4,0},{8,12},{12,8},{16,20},{20,16},{24,28},{28,24},{32,36},... | collective-permute-start | bytes 1572872 | tf_op jit(solution)/shard_map/ppermute | solution.py:293
  76.1 18.6 %collective-permute-done.5.rest_3_ = bf16[8,128,256]{2,1,0:T(8,128)(2,1)S(1)} collective-permute-done((bf16[8,128,256]{2,1,0:T(8,128)(2,1)S(1)}, bf16[8,128,256]{2,1,0:T(8,128)(2,1)S(1)}, u32[]{:S(2)}, u32[]{:S(2)}) %collective-permute-start.5) | collective-permute-done | bytes 524320 | tf_op jit(solution)/shard_map/ppermute | solution.py:293
  94.7 2.0 %collective-permute-start.9 = (bf16[8,128,256]{2,1,0:T(8,128)(2,1)S(1)}, bf16[8,128,256]{2,1,0:T(8,128)(2,1)S(1)}, u32[]{:S(2)}, u32[]{:S(2)}) collective-permute-start(bf16[8,128,256]{2,1,0:T(8,128)(2,1)S(1)} %collective-permute-done.5.rest_3_), channel_id=1, source_target_pairs={{0,4},{4,0},{8,12},{12,8},{16,20},{20,16},{24,28},{28,24},{32,36},... | collective-permute-start | bytes 1572872 | tf_op jit(solution)/shard_map/ppermute | solution.py:293
  97.5 0.9 copy-done.4
  98.4 1.2 intra.1
  99.6 1.0 mix.1
  100.6 2.8 %collective-permute-start.14 = (f32[8,128]{1,0:T(8,128)S(1)}, f32[8,128]{1,0:T(8,128)S(1)}, u32[]{:S(2)}, u32[]{:S(2)}) collective-permute-start(f32[8,128]{1,0:T(8,128)S(1)} %get-tuple-element.26.s0), channel_id=1, source_target_pairs={{0,3},{1,2},{2,1},{3,0},{4,7},{5,6},{6,5},{7,4},{8,11},{9,10},{10,... | collective-permute-start | bytes 12296 | tf_op jit(solution)/shard_map/ppermute | solution.py:334
  104.1 3.3 %attention.1 = (bf16[128,640]{1,0:T(8,128)(2,1)}, f32[16,128]{1,0:T(8,128)S(1)}) custom-call(s32[1,128]{1,0:T(1,128)S(1)} %bitcast.15, bf16[128,640]{1,0:T(8,128)(2,1)S(1)} %copy-done.5, s32[1,128]{1,0:T(1,128)S(1)} %bitcast.16, bf16[8,128,256]{2,1,0:T(8,128)(2,1)S(1)} %pad_maximum_fusion.rest_0_, bf16[8,128,256]{2,1,0:T(8,128)(2,1)} %collective-permute-done.3.rest_1_, ...), custom_call_target="tpu_custom_call" | custom-call | flops 2684354560 | bytes 8388608 | tf_op jit(solution)/shard_map/attention/pallas_call | solution.py:337
  108.1 0.9 finish.1
  109.0 10.9 %all_to_all.20.in_ref = bf16[8,32,128]{2,1,0:T(8,128)(2,1)S(1)} all-to-all(bf16[8,32,128]{2,1,0:T(8,128)(2,1)S(1)} %get-tuple-element.29), channel_id=1, replica_groups={{0,4,8,12,16,20,24,28},{32,36,40,44,48,52,56,60},{64,68,72,76,80,84,88,..., dimensions={0} | all-to-all | bytes 131072 | tf_op jit(solution)/shard_map/all_to_all | solution.py:354
  119.9 22.9 %all_to_all.21.in_ref = bf16[8,32,128]{2,1,0:T(8,128)(2,1)S(1)} all-to-all(bf16[8,32,128]{2,1,0:T(8,128)(2,1)S(1)} %least.1), channel_id=1, replica_groups={{0,32,64,96,128,160,192,224},{4,36,68,100,132,164,196,228},{8,40,72,104..., dimensions={0} | all-to-all | bytes 131072 | tf_op jit(solution)/shard_map/all_to_all | solution.py:356
  (56 shorter events, 6.9 us)
Async XLA Ops:
  6.1 4.9 %collective-permute-start.10 = (f32[264,512]{1,0:T(8,128)S(1)}, f32[264,512]{1,0:T(8,128)S(1)}, u32[]{:S(2)}, u32[]{:S(2)}) collective-permute-start(f32[264,512]{1,0:T(8,128)S(1)} %get-tuple-element.22), channel_id=1, source_target_pairs={{0,4},{4,0},{8,12},{12,8},{16,20},{20,16},{24,28},{28,24},{32,36},... | collective-permute-start | bytes 1622024 | tf_op jit(solution)/shard_map/ppermute | solution.py:293
  11.9 9.4 %copy-start.13 = (bf16[128,128]{1,0:T(8,128)(2,1)S(1)}, bf16[128,128]{1,0:T(8,128)(2,1)}, u32[]{:S(2)}) copy-start(bf16[128,128]{1,0:T(8,128)(2,1)} %param.14) | copy-start | bytes 98308
  11.9 9.4 %copy-start.14 = (bf16[128,128]{1,0:T(8,128)(2,1)S(1)}, bf16[128,128]{1,0:T(8,128)(2,1)}, u32[]{:S(2)}) copy-start(bf16[128,128]{1,0:T(8,128)(2,1)} %param.13) | copy-start | bytes 98308
  11.9 30.9 %all-to-all-start = ((f32[32,8,640]{2,1,0:T(8,128)}), f32[32,8,640]{2,1,0:T(8,128)S(1)}, u32[]{:S(2)}, u32[]{:S(2)}) async-start(f32[32,8,640]{2,1,0:T(8,128)} %chip_state.1), calls=%async_computation | async-start | bytes 1310720 | tf_op jit(solution)/shard_map/all_to_all | solution.py:318
  21.4 20.1 %collective-permute-start = (bf16[1,128,256]{2,1,0:T(8,128)(2,1)S(1)}, bf16[1,128,256]{2,1,0:T(8,128)(2,1)S(1)}, u32[]{:S(2)}, u32[]{:S(2)}) collective-permute-start(bf16[1,128,256]{2,1,0:T(8,128)(2,1)S(1)} %maximum_bitcast_fusion), channel_id=1, source_target_pairs={{0,128},{4,132},{8,136},{12,140},{16,144},{20,148},{24,152},{28,15... | collective-permute-start | bytes 196616 | tf_op jit(solution)/shard_map/ppermute | solution.py:293
  41.5 10.1 %collective-permute-start.1 = (bf16[2,128,256]{2,1,0:T(8,128)(2,1)S(1)}, bf16[2,128,256]{2,1,0:T(8,128)(2,1)S(1)}, u32[]{:S(2)}, u32[]{:S(2)}) collective-permute-start(bf16[2,128,256]{2,1,0:T(8,128)(2,1)S(1)} %pad_maximum_fusion.2), channel_id=1, source_target_pairs={{0,64},{4,68},{8,72},{12,76},{16,80},{20,84},{24,88},{28,92},{32,9... | collective-permute-start | bytes 393224 | tf_op jit(solution)/shard_map/ppermute | solution.py:293
  43.7 29.5 %all-to-all-start.1 = ((f32[32,8,512]{2,1,0:T(8,128)}), f32[32,8,512]{2,1,0:T(8,128)S(1)}, u32[]{:S(2)}, u32[]{:S(2)}) async-start(f32[32,8,512]{2,1,0:T(8,128)} %prefix.1), calls=%async_computation.1 | async-start | bytes 1048576 | tf_op jit(solution)/shard_map/all_to_all | solution.py:320
  51.7 18.1 %collective-permute-start.2 = (bf16[4,128,256]{2,1,0:T(8,128)(2,1)S(1)}, bf16[4,128,256]{2,1,0:T(8,128)(2,1)S(1)}, u32[]{:S(2)}, u32[]{:S(2)}) collective-permute-start(bf16[4,128,256]{2,1,0:T(8,128)(2,1)S(1)} %pad_maximum_fusion.1), channel_id=1, source_target_pairs={{0,32},{4,36},{8,40},{12,44},{16,48},{20,52},{24,56},{28,60},{32,0... | collective-permute-start | bytes 786440 | tf_op jit(solution)/shard_map/ppermute | solution.py:293
  69.8 27.6 %copy-start.1 = (bf16[128,256]{1,0:T(8,128)(2,1)S(1)}, bf16[128,256]{1,0:T(8,128)(2,1)}, u32[]{:S(2)}) copy-start(bf16[128,256]{1,0:T(8,128)(2,1)} %c_ref.3) | copy-start | bytes 196612
  69.8 27.6 %copy-start.7 = (bf16[128,256]{1,0:T(8,128)(2,1)S(1)}, bf16[128,256]{1,0:T(8,128)(2,1)}, u32[]{:S(2)}) copy-start(bf16[128,256]{1,0:T(8,128)(2,1)} %b_ref.3) | copy-start | bytes 196612
  69.8 27.6 %copy-start.9 = (f32[128,16]{0,1:T(8,128)S(1)}, f32[128,16]{0,1:T(8,128)}, u32[]{:S(2)}) copy-start(f32[128,16]{0,1:T(8,128)} %param.19) | copy-start | bytes 24580
  69.8 24.8 %collective-permute-start.5 = (bf16[8,128,256]{2,1,0:T(8,128)(2,1)S(1)}, bf16[8,128,256]{2,1,0:T(8,128)(2,1)S(1)}, u32[]{:S(2)}, u32[]{:S(2)}) collective-permute-start(bf16[8,128,256]{2,1,0:T(8,128)(2,1)S(1)} %pad_maximum_fusion.rest_0_), channel_id=1, source_target_pairs={{0,24},{4,28},{8,16},{12,20},{16,8},{20,12},{24,0},{28,4},{32,56},... | collective-permute-start | bytes 1572872 | tf_op jit(solution)/shard_map/ppermute | solution.py:293
  72.4 24.3 %collective-permute-start.4 = (bf16[8,128,256]{2,1,0:T(8,128)(2,1)S(1)}, bf16[8,128,256]{2,1,0:T(8,128)(2,1)S(1)}, u32[]{:S(2)}, u32[]{:S(2)}) collective-permute-start(bf16[8,128,256]{2,1,0:T(8,128)(2,1)S(1)} %pad_maximum_fusion.rest_0_), channel_id=1, source_target_pairs={{0,16},{4,20},{8,24},{12,28},{16,0},{20,4},{24,8},{28,12},{32,48},... | collective-permute-start | bytes 1572872 | tf_op jit(solution)/shard_map/ppermute | solution.py:293
  72.8 23.9 %collective-permute-start.3 = (bf16[8,128,256]{2,1,0:T(8,128)(2,1)S(1)}, bf16[8,128,256]{2,1,0:T(8,128)(2,1)}, u32[]{:S(2)}, u32[]{:S(2)}) collective-permute-start(bf16[8,128,256]{2,1,0:T(8,128)(2,1)S(1)} %pad_maximum_fusion.rest_0_), channel_id=1, source_target_pairs={{0,8},{4,12},{8,0},{12,4},{16,24},{20,28},{24,16},{28,20},{32,40},... | collective-permute-start | bytes 1572872 | tf_op jit(solution)/shard_map/ppermute | solution.py:293
  73.2 24.3 %copy-start.11 = (f32[16]{0:T(128)S(1)}, f32[16]{0:T(128)}, u32[]{:S(2)}) copy-start(f32[16]{0:T(128)} %param.21) | copy-start | bytes 196
  73.3 26.3 %copy-start = (bf16[128,1024]{1,0:T(8,128)(2,1)S(1)}, bf16[128,1024]{1,0:T(8,128)(2,1)}, u32[]{:S(2)}) copy-start(bf16[128,1024]{1,0:T(8,128)(2,1)} %z_ref.1) | copy-start | bytes 786436
  73.3 26.3 %collective-permute-start.11 = (f32[256,512]{1,0:T(8,128)S(1)}, f32[256,512]{1,0:T(8,128)S(1)}, u32[]{:S(2)}, u32[]{:S(2)}) collective-permute-start(f32[256,512]{1,0:T(8,128)S(1)} %get-tuple-element.24), channel_id=1, source_target_pairs={{0,4},{4,0},{8,12},{12,8},{16,20},{20,16},{24,28},{28,24},{32,36},... | collective-permute-start | bytes 1572872 | tf_op jit(solution)/shard_map/ppermute | solution.py:293
  76.0 27.4 %collective-permute-start.6 = (bf16[8,128,256]{2,1,0:T(8,128)(2,1)S(1)}, bf16[8,128,256]{2,1,0:T(8,128)(2,1)S(1)}, u32[]{:S(2)}, u32[]{:S(2)}) collective-permute-start(bf16[8,128,256]{2,1,0:T(8,128)(2,1)S(1)} %pad_maximum_fusion.rest_0_), channel_id=1, source_target_pairs={{0,4},{4,0},{8,12},{12,8},{16,20},{20,16},{24,28},{28,24},{32,36},... | collective-permute-start | bytes 1572872 | tf_op jit(solution)/shard_map/ppermute | solution.py:293
  94.7 9.1 %collective-permute-start.9 = (bf16[8,128,256]{2,1,0:T(8,128)(2,1)S(1)}, bf16[8,128,256]{2,1,0:T(8,128)(2,1)S(1)}, u32[]{:S(2)}, u32[]{:S(2)}) collective-permute-start(bf16[8,128,256]{2,1,0:T(8,128)(2,1)S(1)} %collective-permute-done.5.rest_3_), channel_id=1, source_target_pairs={{0,4},{4,0},{8,12},{12,8},{16,20},{20,16},{24,28},{28,24},{32,36},... | collective-permute-start | bytes 1572872 | tf_op jit(solution)/shard_map/ppermute | solution.py:293
  96.7 7.3 %collective-permute-start.8 = (bf16[8,128,256]{2,1,0:T(8,128)(2,1)S(1)}, bf16[8,128,256]{2,1,0:T(8,128)(2,1)S(1)}, u32[]{:S(2)}, u32[]{:S(2)}) collective-permute-start(bf16[8,128,256]{2,1,0:T(8,128)(2,1)S(1)} %collective-permute-done.4.rest_2_), channel_id=1, source_target_pairs={{0,4},{4,0},{8,12},{12,8},{16,20},{20,16},{24,28},{28,24},{32,36},... | collective-permute-start | bytes 1572872 | tf_op jit(solution)/shard_map/ppermute | solution.py:293
  96.7 7.3 %collective-permute-start.7 = (bf16[8,128,256]{2,1,0:T(8,128)(2,1)}, bf16[8,128,256]{2,1,0:T(8,128)(2,1)S(1)}, u32[]{:S(2)}, u32[]{:S(2)}) collective-permute-start(bf16[8,128,256]{2,1,0:T(8,128)(2,1)} %collective-permute-done.3.rest_1_), channel_id=1, source_target_pairs={{0,4},{4,0},{8,12},{12,8},{16,20},{20,16},{24,28},{28,24},{32,36},... | collective-permute-start | bytes 1572872 | tf_op jit(solution)/shard_map/ppermute | solution.py:293
  100.6 6.8 %collective-permute-start.14 = (f32[8,128]{1,0:T(8,128)S(1)}, f32[8,128]{1,0:T(8,128)S(1)}, u32[]{:S(2)}, u32[]{:S(2)}) collective-permute-start(f32[8,128]{1,0:T(8,128)S(1)} %get-tuple-element.26.s0), channel_id=1, source_target_pairs={{0,3},{1,2},{2,1},{3,0},{4,7},{5,6},{6,5},{7,4},{8,11},{9,10},{10,... | collective-permute-start | bytes 12296 | tf_op jit(solution)/shard_map/ppermute | solution.py:334
  103.4 4.0 %collective-permute-start.13 = (f32[8,128]{1,0:T(8,128)S(1)}, f32[8,128]{1,0:T(8,128)S(1)}, u32[]{:S(2)}, u32[]{:S(2)}) collective-permute-start(f32[8,128]{1,0:T(8,128)S(1)} %get-tuple-element.26.s0), channel_id=1, source_target_pairs={{0,2},{1,3},{2,0},{3,1},{4,6},{5,7},{6,4},{7,5},{8,10},{9,11},{10,... | collective-permute-start | bytes 12296 | tf_op jit(solution)/shard_map/ppermute | solution.py:334
  103.7 3.7 %collective-permute-start.12 = (f32[8,128]{1,0:T(8,128)S(1)}, f32[8,128]{1,0:T(8,128)S(1)}, u32[]{:S(2)}, u32[]{:S(2)}) collective-permute-start(f32[8,128]{1,0:T(8,128)S(1)} %get-tuple-element.26.s0), channel_id=1, source_target_pairs={{0,1},{1,0},{2,3},{3,2},{4,5},{5,4},{6,7},{7,6},{8,9},{9,8},{10,11... | collective-permute-start | bytes 12296 | tf_op jit(solution)/shard_map/ppermute | solution.py:334
  (8 other events, 9.9 us)

commit v2 on v1

--- a/solution.py
+++ b/solution.py
@@ -178,22 +178,18 @@
         wide = out.astype(F32)
         lines[tile : tile + 1, :] = jnp.min(wide, axis=0, keepdims=True)
         lines[8 + tile : 9 + tile, :] = jnp.min(-wide, axis=0, keepdims=True)
-    packed = lines[...].astype(BF16)
-    for dest in range(8):
-        rng_ref[dest] = packed
-
-
-def least_kernel(in_ref, out_ref):
-    least = in_ref[0].astype(F32)
-    for part in range(1, 8):
-        least = jnp.minimum(least, in_ref[part].astype(F32))
-    for dest in range(8):
-        out_ref[dest] = least.astype(BF16)
+    rng_ref[...] = lines[...].astype(BF16)
+
+
+def least_kernel(own_ref, got_ref, out_ref):
+    least = jnp.minimum(own_ref[...].astype(F32), got_ref[...].astype(F32)).astype(BF16)
+    for dest in range(CHIPS):
+        out_ref[dest] = least
 
 
 def range_kernel(in_ref, attn_ref, ssm_ref):
     least = in_ref[0].astype(F32)
-    for part in range(1, 8):
+    for part in range(1, CHIPS):
         least = jnp.minimum(least, in_ref[part].astype(F32))
     for tile in range(COLS // 128):
         at = slice(tile * 128, tile * 128 + 128)
@@ -205,77 +201,118 @@
         attn_ref[1:2, at] = -least[21 + tile : 22 + tile]
 
 
-def attn_kernel(scal, q_ref, doc_ref, *rest):
-    parts, (out_ref, rng_ref, held, highest, totals, accum, sems) = rest[:8], rest[8:]
-    copies = [
-        pltpu.make_async_copy(part, held.at[n // 4, pl.ds((n % 4) * 8, 8)], sems.at[n])
-        for n, part in enumerate(parts)
-    ]
-    for copy in copies:
-        copy.start()
-    me, first_doc, last_doc = position(scal)
-    core, mine = me % 2, me // 2
-    z_mine, x_mine = mine // 4, mine % 4
-    doc = jnp.transpose(jnp.broadcast_to(doc_ref[...], (TOK, TOK)).astype(F32)).astype(jnp.int32)
-    doc = jnp.concatenate([doc, doc], axis=1)
-    q_pos = me * TOK + iota((TOK, 2 * TOK), 0)
-    lane = iota((TOK, 2 * TOK), 1)
-    key_lane = jnp.where(lane < TOK, core * TOK + lane, (1 - core) * TOK + lane - TOK)
-    highest[...] = jnp.full(highest.shape, FLOOR, F32)
-    totals[...] = jnp.zeros(totals.shape, F32)
-    accum[...] = jnp.zeros(accum.shape, F32)
-    for copy in copies:
-        copy.wait()
-
-    def absorb(chip, masked):
-        flip = z_mine ^ (chip // 4)
-        place = (flip % 2) * 4 + (flip // 2 % 2) * 2 + flip // 4
-        slot = (x_mine ^ (chip % 4)) * 8 + place
-        near, far = held[0, slot], held[1, slot]
-        keys = jnp.concatenate([near[:, :HD], far[:, :HD]], axis=0)
-        vals = jnp.concatenate([near[:, HD:], far[:, HD:]], axis=0)
-        if masked:
-            key_pos = chip * 2 * TOK + key_lane
-            visible = (key_pos <= q_pos) & (key_pos >= doc)
-        for g in range(GROUP):
-            scores = mm(q_ref[:, g * HD : (g + 1) * HD], keys, ((1,), (1,)))
-            if masked:
-                scores = jnp.where(visible, scores, FLOOR)
-            old = highest[g]
-            new = jnp.maximum(old, jnp.max(scores, axis=1, keepdims=True))
-            factor = jnp.exp2((old - new) * SCORE_SCALE)
-            wide = jnp.concatenate([new, new], axis=1)
-            weights = jnp.exp2((scores - wide) * SCORE_SCALE)
-            if masked:
-                weights = jnp.where(visible, weights, 0.0)
-            highest[g] = new
-            totals[g] = totals[g] * factor + (weights[:, :TOK] + weights[:, TOK:])
-            accum[g] = accum[g] * factor + mm(weights.astype(BF16), vals)
-
-    low = first_doc // (2 * TOK)
-    middle = jnp.minimum((last_doc + 2 * TOK - 1) // (2 * TOK), mine)
-
-    def edge(n, _):
-        absorb(jnp.where(n == 0, mine, low + n - 1), True)
-        return 0
-
-    def inside(chip, _):
-        absorb(chip, False)
-        return 0
-
-    lax.fori_loop(0, middle - low + 1, edge, 0)
-    lax.fori_loop(middle, mine, inside, 0)
+ROWS = GROUP * TOK
+
+
+def attn_kernel(flips, span, first, final, doc_smem, q_ref, doc_ref, *rest):
+    sides, rest = rest[: 4 * len(flips)], rest[4 * len(flips) :]
+    if not first:
+        (old_highest, old_totals, old_accum), rest = [rest[0].at[n] for n in range(3)], rest[1:]
+    if final:
+        out_ref, rng_ref, carry, q_rows = rest
+    else:
+        carry, q_rows = rest
+    highest, totals, accum = [carry.at[n] for n in range(3)]
+    me, first_doc, last_doc = position(doc_smem)
+    core, z_mine, x_mine = me % 2, me // 8, me // 2 % 4
+    wide = span * TOK
+    width = 2 * len(flips) * wide
+    lane = iota((TOK, wide), 1)
+    lane = lane // TOK * (8 * TOK) + lane % TOK
+    for g in range(GROUP):
+        q_rows[g * TOK : (g + 1) * TOK, :] = q_ref[:, g * HD : (g + 1) * HD]
+
+    def load(planes, which):
+        refs = [sides[2 * n + which] for n in range(2 * len(flips))]
+        at = [slice(0, HD) if ref.shape[2] == HD or which == 0 else slice(HD, 2 * HD) for ref in refs]
+        return jnp.concatenate(
+            [ref[planes, :, cols].reshape(wide, HD) for ref, cols in zip(refs, at)], axis=0
+        )
+
+    def hide(block, values):
+        begins = [
+            ((block * span * 4 + (x_mine ^ flip)) * 2 + side) * TOK
+            for flip in flips
+            for side in (core, 1 - core)
+        ]
+        key_pos = jnp.concatenate([begin + lane for begin in begins], axis=1)
+        doc = jnp.transpose(jnp.broadcast_to(doc_ref[...], (TOK, TOK)).astype(F32))
+        doc = jnp.concatenate([doc.astype(jnp.int32)] * (width // TOK), axis=1)
+        q_pos = me * TOK + iota((TOK, width), 0)
+        visible = (key_pos <= q_pos) & (key_pos >= doc)
+        return jnp.where(jnp.concatenate([visible] * GROUP, axis=0), values, FLOOR)
+
+    def score(block, masked):
+        keys = load(pl.ds(block * span, span), 0)
+        scores = mm(q_rows[...], keys, ((1,), (1,)))
+        return hide(block, scores) if masked else scores
+
+    def fold(join, values):
+        total = values[:, :TOK]
+        for n in range(1, width // TOK):
+            total = join(total, values[:, n * TOK : (n + 1) * TOK])
+        return total
+
+    def find(block, masked):
+        highest[...] = jnp.maximum(highest[...], fold(jnp.maximum, score(block, masked)))
+
+    def add(block, masked):
+        vals = load(pl.ds(block * span, span), 1)
+        gap = score(block, masked) - jnp.concatenate([highest[...]] * (width // TOK), axis=1)
+        weights = jnp.exp2(gap * SCORE_SCALE)
+        totals[...] += fold(jnp.add, weights)
+        accum[...] += mm(weights.astype(BF16), vals)
+
+    size = span * 8 * TOK
+    low, last = first_doc // size, z_mine // span
+    inner = jnp.minimum((last_doc + size - 1) // size, last)
+
+    def sweep(absorb):
+        def edge(n, _):
+            absorb(jnp.where(n == 0, last, low + n - 1), True)
+            return 0
+
+        def inside(block, _):
+            absorb(block, False)
+            return 0
+
+        lax.fori_loop(0, inner - low + 1, edge, 0)
+        lax.fori_loop(inner, last, inside, 0)
+
+    highest[...] = jnp.full((ROWS, HD), FLOOR, F32) if first else old_highest[...]
+    sweep(find)
+    highest[...] = jnp.broadcast_to(jnp.max(highest[...], axis=1, keepdims=True), (ROWS, HD))
+    if first:
+        totals[...] = jnp.zeros((ROWS, HD), F32)
+        accum[...] = jnp.zeros((ROWS, HD), F32)
+    else:
+        factor = jnp.exp2((old_highest[...] - highest[...]) * SCORE_SCALE)
+        totals[...] = old_totals[...] * factor
+        accum[...] = old_accum[...] * factor
+    sweep(add)
+    if not final:
+        return
     rng_ref[...] = jnp.zeros(rng_ref.shape, F32)
     for g in range(GROUP):
-        total = jnp.sum(totals[g], axis=1, keepdims=True)
-        out = (accum[g] / total).astype(BF16)
+        rows = slice(g * TOK, (g + 1) * TOK)
+        total = jnp.sum(totals[rows, :], axis=1, keepdims=True)
+        out = (accum[rows, :] / total).astype(BF16)
         out_ref[:, g * HD : (g + 1) * HD] = out
-        wide = out.astype(F32)
-        rng_ref[g : g + 1, :] = jnp.min(wide, axis=0, keepdims=True)
-        rng_ref[GROUP + g : GROUP + g + 1, :] = jnp.min(-wide, axis=0, keepdims=True)
-
-
-def call(kernel, outs, specs, name, flops=0, data=0, exps=0, scratch=()):
+        values = out.astype(F32)
+        rng_ref[g : g + 1, :] = jnp.min(values, axis=0, keepdims=True)
+        rng_ref[GROUP + g : GROUP + g + 1, :] = jnp.min(-values, axis=0, keepdims=True)
+
+
+def copies_kernel(k_ref, v_ref, out_ref):
+    for dest in range(8):
+        out_ref[dest, :, 0:HD] = k_ref[...]
+        out_ref[dest, :, HD:] = v_ref[...]
+
+
+ATTN_COST = 10**10
+
+
+def call(kernel, outs, specs, name, scratch=(), flops=0):
     return pl.pallas_call(
         kernel,
         out_shape=[jax.ShapeDtypeStruct(shape, dtype) for shape, dtype in outs],
@@ -283,7 +320,7 @@
         out_specs=[VMEM] * len(outs),
         scratch_shapes=list(scratch),
         compiler_params=pltpu.CompilerParams(vmem_limit_bytes=40 * 2**20),
-        cost_estimate=pl.CostEstimate(flops=flops, bytes_accessed=data, transcendentals=exps),
+        cost_estimate=pl.CostEstimate(flops=flops, bytes_accessed=0, transcendentals=0),
         name=name,
     )
 
@@ -298,62 +335,62 @@
     doc_row = doc_start[None, :]
     a_row, skip_row, gain_row = a_log[None, :], d_skip[None, :], ssm_gain[None, :]
     same_core = [[i for i in range(64) if i % 2 == core] for core in range(2)]
-    plane = [[z * 8 + n for n in range(8)] for z in range(8)]
     column = [[z * 8 + n for z in range(8)] for n in range(8)]
 
-    near = jnp.concatenate([k_in, v_in], axis=1)[None]
-    for bit in (32, 16, 8):
-        near = jnp.concatenate([near, swap(near, bit)], axis=0)
-    own = [near] + [swap(near, bit) for bit in (2, 4, 6)]
-    other = [swap(part, 1) for part in own]
+    (near,) = call(copies_kernel, [((8, TOK, 2 * HD), BF16)], [VMEM] * 2, "copies")(k_in, v_in)
+    near = lax.all_to_all(near, "seq", 0, 0, tiled=True, axis_index_groups=column)
+
+    def attend(parts, flips, span, first, final, carry, name):
+        scratch = [pltpu.VMEM((ROWS, HD), BF16)]
+        if final:
+            outs = [((TOK, GROUP * HD), BF16), ((16, 128), F32)]
+            scratch = [pltpu.VMEM((3, ROWS, HD), F32)] + scratch
+        else:
+            outs = [((3, ROWS, HD), F32)]
+        refs = []
+        for part in parts:
+            other = [swap(value, 1) for value in part]
+            refs += [part[0], part[-1], other[0], other[-1]]
+        return call(
+            functools.partial(attn_kernel, flips, span, first, final), outs,
+            [SMEM] + [VMEM] * (2 + len(refs) + len(carry)), name, scratch=scratch, flops=ATTN_COST,
+        )(doc_row, q_in, doc_row, *refs, *carry)
 
     keep, send = call(
-        local_kernel, [((NS + 8, HALF), F32)] * 2, [SMEM] + [VMEM] * 4, "local_state",
-        flops=2 * 2 * TOK * NS * COLS, data=2**21,
+        local_kernel, [((NS + 8, HALF), F32)] * 2, [SMEM] + [VMEM] * 4, "local_state"
     )(doc_row, x_in, b_in, dt_t, a_row)
     got = swap(send, 1)
-    (chunks,) = call(
-        chip_kernel, [((CHIPS, 8, HALF + 128), F32)], [VMEM] * 2, "chip_state", data=2**20
-    )(keep, got)
+    y_part, enter = call(
+        intra_kernel, [((TOK, COLS), F32), ((TOK, HEADS), F32)], [VMEM] * 7, "intra"
+    )(x_in, b_in, c_in, dt_t, a_row, skip_row, doc_row)
+    (chunks,) = call(chip_kernel, [((CHIPS, 8, HALF + 128), F32)], [VMEM] * 2, "chip_state")(keep, got)
     chunks = lax.all_to_all(chunks, "seq", 0, 0, tiled=True, axis_index_groups=same_core)
-    (prefix,) = call(prefix_kernel, [((CHIPS, 8, HALF), F32)], [VMEM], "prefix", data=2**19)(chunks)
+    side1, side3 = swap(near, 2), swap(near, 6)
+    carry = attend([[near]], (0,), 4, True, False, [], "attention_near")
+    carry = attend([[side1], [side3]], (1, 3), 2, False, False, carry, "attention_sides")
+    chunks, carry, y_part = lax.optimization_barrier((chunks, carry, y_part))
+    far = [swap(side1[:, :, :HD], 6), swap(side3[:, :, HD:], 2)]
+    (prefix,) = call(prefix_kernel, [((CHIPS, 8, HALF), F32)], [VMEM], "prefix")(chunks)
     prefix = lax.all_to_all(prefix, "seq", 0, 0, tiled=True, axis_index_groups=same_core)
-    mine, theirs = call(
-        enter_kernel, [((NS, HALF), F32)] * 2, [VMEM] * 3, "state_in", data=2**20
-    )(prefix, keep, got)
+    attn_out, attn_rng = attend([far], (2,), 4, False, True, carry, "attention_far")
+    prefix, attn_rng = lax.optimization_barrier((prefix, attn_rng))
+    mine, theirs = call(enter_kernel, [((NS, HALF), F32)] * 2, [VMEM] * 3, "state_in")(
+        prefix, keep, got
+    )
     got_state = swap(theirs, 1)
-    y_part, enter = call(
-        intra_kernel, [((TOK, COLS), F32), ((TOK, HEADS), F32)], [VMEM] * 7, "intra",
-        flops=4 * TOK * TOK * COLS * 2, data=2**20, exps=TOK * TOK * HEADS,
-    )(x_in, b_in, c_in, dt_t, a_row, skip_row, doc_row)
-    gated, square = call(
-        mix_kernel, [((TOK, COLS), F32), ((8, TOK), F32)], [VMEM] * 6, "mix",
-        flops=2 * TOK * NS * COLS, data=2**21,
-    )(y_part, enter, c_in, z_in, mine, got_state)
+    gated, square = call(mix_kernel, [((TOK, COLS), F32), ((8, TOK), F32)], [VMEM] * 6, "mix")(
+        y_part, enter, c_in, z_in, mine, got_state
+    )
     squares = [square] + [
         lax.ppermute(square, "head", [(i, i ^ bit) for i in range(4)]) for bit in (1, 2, 3)
     ]
 
-    attn_out, attn_rng = call(
-        attn_kernel, [((TOK, GROUP * HD), BF16), ((16, 128), F32)],
-        [SMEM] + [VMEM] * 2 + [ANY] * 8, "attention",
-        flops=4 * TOK * GROUP * HD * 8192, data=2**23, exps=TOK * GROUP * 8192,
-        scratch=[
-            pltpu.VMEM((2, CHIPS, TOK, 2 * HD), BF16),
-            pltpu.VMEM((GROUP, TOK, HD), F32),
-            pltpu.VMEM((GROUP, TOK, HD), F32),
-            pltpu.VMEM((GROUP, TOK, HD), F32),
-            pltpu.SemaphoreType.DMA((8,)),
-        ],
-    )(doc_row, q_in, doc_row, *own, *other)
-
     ssm_out, rng = call(
-        finish_kernel, [((TOK, COLS), BF16), ((8, 32, 128), BF16)], [VMEM] * 7, "finish",
-        data=2**20, scratch=[pltpu.VMEM((32, 128), F32)],
+        finish_kernel, [((TOK, COLS), BF16), ((32, 128), BF16)], [VMEM] * 7, "finish",
+        scratch=[pltpu.VMEM((32, 128), F32)],
     )(gated, *squares, gain_row, attn_rng)
-    rng = lax.all_to_all(rng, "seq", 0, 0, tiled=True, axis_index_groups=plane)
-    (rng,) = call(least_kernel, [((8, 32, 128), BF16)], [VMEM], "least")(rng)
-    rng = lax.all_to_all(rng, "seq", 0, 0, tiled=True, axis_index_groups=column)
+    (rng,) = call(least_kernel, [((CHIPS, 32, 128), BF16)], [VMEM] * 2, "least")(rng, swap(rng, 1))
+    rng = lax.all_to_all(rng, "seq", 0, 0, tiled=True, axis_index_groups=same_core)
     attn_range, ssm_range = call(
         range_kernel, [((2, GROUP * HD), F32), ((2, COLS), F32)], [VMEM], "ranges"
     )(rng)

time: 142 us -> 121 us (0.85)
  blocking collectives: 33.8 us -> 15.8 us
  waiting for transfers between devices: 51.8 us -> 37.2 us
  Pallas kernels: 11.2 us -> 19.8 us
    ppermute x12, waiting for transfers between devices: 51.8 us -> 8.44 us  [swap(): return lax.ppermute(value, 'seq', [(i, i ^ bit) for i in range(count)])]
    all_to_all x2 -> x1, blocking collectives: 33.8 us -> 15.8 us  [body(): lax.all_to_all(rng, 'seq', 0, 0, tiled=True, axis_index_groups=same_core)]
    all_to_all x0 -> x1, waiting for transfers between devices: none -> 13.2 us  [body(): lax.all_to_all(near, 'seq', 0, 0, tiled=True, axis_index_groups=column)]
    all_to_all x1, waiting for transfers between devices: 0.01 us -> 11.8 us  [body(): lax.all_to_all(prefix, 'seq', 0, 0, tiled=True, axis_index_groups=same_core)]
    all_to_all x0 -> x1, starting transfers between devices: none -> 9.15 us  [body(): lax.all_to_all(near, 'seq', 0, 0, tiled=True, axis_index_groups=column)]
    pallas_call x7 -> x10, Pallas kernels: 7.18 us -> 14.9 us  [the longest x3 10.2 us: attend(): call(functools.partial(attn_kernel, flips, span, first, final), outs, [SM...]
    all_to_all x1, starting transfers between devices: 9.43 us -> 3.9 us  [body(): lax.all_to_all(chunks, 'seq', 0, 0, tiled=True, axis_index_groups=same_core)]
    ppermute x3, waiting for transfers between devices: 0.01 us -> 3.66 us  [body(): lax.ppermute(square, 'head', [(i, i ^ bit) for i in range(4)])]
  transfers between devices with their start and end apart: 17 -> 18, of which waited for: 4 -> 8; matrix products, arithmetic and copies ran while one was open for 0% -> 1% of each run, Pallas kernels for 5% -> 13%
where the time goes in v2:
time: 121 us
  starting transfers between devices  42.2 us (35%)
  waiting for transfers between devices  37.2 us (31%)
  Pallas kernels  19.8 us (16%)
  blocking collectives  15.8 us (13%)
  local copies, waits for them, and re-layouts  5.32 us (4%)
    ppermute x12, starting transfers between devices, swap(): return lax.ppermute(value, 'seq', [(i, i ^ bit) for i in range(count)])  17.8 us
    all_to_all x1, blocking collectives, body(): lax.all_to_all(rng, 'seq', 0, 0, tiled=True, axis_index_groups=same_core)  15.8 us
    all_to_all x1, waiting for transfers between devices, body(): lax.all_to_all(near, 'seq', 0, 0, tiled=True, axis_index_groups=column)  13.2 us
    all_to_all x1, waiting for transfers between devices, body(): lax.all_to_all(prefix, 'seq', 0, 0, tiled=True, axis_index_groups=same_core)  11.8 us
    pallas_call x3, Pallas kernels, attend(): call(functools.partial(attn_kernel, flips, span, first, final), outs, [SM...  10.2 us
    all_to_all x1, starting transfers between devices, body(): lax.all_to_all(near, 'seq', 0, 0, tiled=True, axis_index_groups=column)  9.15 us
    ppermute x12, waiting for transfers between devices, swap(): return lax.ppermute(value, 'seq', [(i, i ^ bit) for i in range(count)])  8.44 us
    all_to_all x1, starting transfers between devices, body(): lax.all_to_all(prefix, 'seq', 0, 0, tiled=True, axis_index_groups=same_core)  7.36 us
  transfers between devices with their start and end apart: 18, of which 8 were waited for; matrix products, arithmetic and copies ran while one was open for 1% of the time, Pallas kernels for 13%

profile of v2, /device:TPU:1, one launch (start us, length us, event | category | flops | bytes accessed | tf_op | source)
XLA Modules:
  0.0 121.1 jit_solution(18325473688375918305)
XLA Ops:
  3.0 9.1 %all-to-all-start = ((bf16[8,128,256]{2,1,0:T(8,128)(2,1)}), bf16[8,128,256]{2,1,0:T(8,128)(2,1)S(1)}, u32[]{:S(2)}, u32[]{:S(2)}) async-start(bf16[8,128,256]{2,1,0:T(8,128)(2,1)} %copies.1), calls=%async_computation | async-start | bytes 1048576 | tf_op jit(solution)/shard_map/all_to_all | solution.py:341
  12.8 3.1 %local_state.1 = (f32[264,512]{1,0:T(8,128)S(1)}, f32[264,512]{1,0:T(8,128)}) custom-call(s32[1,128]{1,0:T(1,128)S(1)} %bitcast.10, bf16[128,1024]{1,0:T(8,128)(2,1)S(1)} %copy-done, bf16[128,256]{1,0:T(8,128)(2,1)S(1)} %copy-done.3, f32[16,128]{1,0:T(8,128)S(1)} %bitcast.5, f32[1,16]{1,0:T(1,128)S(1)} %bitcast.8), custom_call_target="tpu_custom_call" | custom-call | tf_op jit(solution)/shard_map/local_state/pallas_call | solution.py:359
  16.9 13.2 %all-to-all-done.rest_0_.rest_1_ = bf16[8,128,256]{2,1,0:T(8,128)(2,1)S(1)} async-done(((bf16[8,128,256]{2,1,0:T(8,128)(2,1)}), bf16[8,128,256]{2,1,0:T(8,128)(2,1)S(1)}, u32[]{:S(2)}, u32[]{:S(2)}) %all-to-all-start) | async-done | bytes 524320 | tf_op jit(solution)/shard_map/all_to_all | solution.py:341
  30.1 1.2 collective-permute-start
  31.3 1.8 %collective-permute-start.2 = (bf16[8,128,256]{2,1,0:T(8,128)(2,1)S(1)}, bf16[8,128,256]{2,1,0:T(8,128)(2,1)}, u32[]{:S(2)}, u32[]{:S(2)}) collective-permute-start(bf16[8,128,256]{2,1,0:T(8,128)(2,1)S(1)} %all-to-all-done.rest_0_.rest_1_), channel_id=1, source_target_pairs={{0,24},{4,28},{8,16},{12,20},{16,8},{20,12},{24,0},{28,4},{32,56},... | collective-permute-start | bytes 1572872 | tf_op jit(solution)/shard_map/ppermute | solution.py:330
  36.3 3.9 %all-to-all-start.1 = ((f32[32,8,640]{2,1,0:T(8,128)}), f32[32,8,640]{2,1,0:T(8,128)S(1)}, u32[]{:S(2)}, u32[]{:S(2)}) async-start(f32[32,8,640]{2,1,0:T(8,128)} %chip_state.1), calls=%async_computation.1 | async-start | bytes 1310720 | tf_op jit(solution)/shard_map/all_to_all | solution.py:367
  40.2 3.0 %collective-permute-done.rest_0_.rest_1_ = bf16[8,128,256]{2,1,0:T(8,128)(2,1)S(1)} collective-permute-done((bf16[8,128,256]{2,1,0:T(8,128)(2,1)S(1)}, bf16[8,128,256]{2,1,0:T(8,128)(2,1)S(1)}, u32[]{:S(2)}, u32[]{:S(2)}) %collective-permute-start) | collective-permute-done | bytes 524320 | tf_op jit(solution)/shard_map/ppermute | solution.py:330
  43.3 2.8 %collective-permute-start.1 = (bf16[8,128,128]{2,1,0:T(8,128)(2,1)S(1)}, bf16[8,128,128]{2,1,0:T(8,128)(2,1)}, u32[]{:S(2)}, u32[]{:S(2)}) collective-permute-start(bf16[8,128,128]{2,1,0:T(8,128)(2,1)S(1)} %slice.8), channel_id=1, source_target_pairs={{0,24},{4,28},{8,16},{12,20},{16,8},{20,12},{24,0},{28,4},{32,56},... | collective-permute-start | bytes 786440 | tf_op jit(solution)/shard_map/ppermute | solution.py:330
  47.1 3.4 %collective-permute-start.7 = (bf16[8,128,256]{2,1,0:T(8,128)(2,1)S(1)}, bf16[8,128,256]{2,1,0:T(8,128)(2,1)S(1)}, u32[]{:S(2)}, u32[]{:S(2)}) collective-permute-start(bf16[8,128,256]{2,1,0:T(8,128)(2,1)S(1)} %collective-permute-done.rest_0_.rest_1_), channel_id=1, source_target_pairs={{0,4},{4,0},{8,12},{12,8},{16,20},{20,16},{24,28},{28,24},{32,36},... | collective-permute-start | bytes 1572872 | tf_op jit(solution)/shard_map/ppermute | solution.py:330
  50.6 3.1 %attention_near.1.rest_8_ = f32[3,640,128]{2,1,0:T(8,128)S(1)} custom-call(s32[1,128]{1,0:T(1,128)S(1)} %bitcast.12, bf16[128,640]{1,0:T(8,128)(2,1)S(1)} %copy-done.11, s32[1,128]{1,0:T(1,128)S(1)} %bitcast.13, bf16[8,128,256]{2,1,0:T(8,128)(2,1)S(1)} %all-to-all-done.rest_0_.rest_1_, bf16[8,128,256]{2,1,0:T(8,128)(2,1)S(1)} %all-to-all-done.rest_0_.rest_1_, ...), custom_call_target="tpu_custom_call" | custom-call | flops 10000000000 | tf_op jit(solution)/shard_map/attention_near/pallas_call | solution.py:354
  53.7 3.0 %collective-permute-done.1.rest_0_ = bf16[8,128,128]{2,1,0:T(8,128)(2,1)} collective-permute-done((bf16[8,128,128]{2,1,0:T(8,128)(2,1)S(1)}, bf16[8,128,128]{2,1,0:T(8,128)(2,1)}, u32[]{:S(2)}, u32[]{:S(2)}) %collective-permute-start.1) | collective-permute-done | bytes 262176 | tf_op jit(solution)/shard_map/ppermute | solution.py:330
  56.8 2.4 %collective-permute-start.4 = (bf16[8,128,128]{2,1,0:T(8,128)(2,1)}, bf16[8,128,128]{2,1,0:T(8,128)(2,1)S(1)}, u32[]{:S(2)}, u32[]{:S(2)}) collective-permute-start(bf16[8,128,128]{2,1,0:T(8,128)(2,1)} %collective-permute-done.1.rest_0_), channel_id=1, source_target_pairs={{0,4},{4,0},{8,12},{12,8},{16,20},{20,16},{24,28},{28,24},{32,36},... | collective-permute-start | bytes 786440 | tf_op jit(solution)/shard_map/ppermute | solution.py:330
  59.2 3.3 %attention_sides.1.rest_4_ = f32[3,640,128]{2,1,0:T(8,128)S(1)} custom-call(s32[1,128]{1,0:T(1,128)S(1)} %bitcast.14, bf16[128,640]{1,0:T(8,128)(2,1)S(1)} %copy-done.11, s32[1,128]{1,0:T(1,128)S(1)} %bitcast.15, bf16[8,128,256]{2,1,0:T(8,128)(2,1)S(1)} %collective-permute-done.rest_0_.rest_1_, ...), custom_call_target="tpu_custom_call" | custom-call | flops 10000000000 | tf_op jit(solution)/shard_map/attention_sides/pallas_call | solution.py:354
  64.4 7.4 %all-to-all-start.2 = ((f32[32,8,512]{2,1,0:T(8,128)}), f32[32,8,512]{2,1,0:T(8,128)S(1)}, u32[]{:S(2)}, u32[]{:S(2)}) async-start(f32[32,8,512]{2,1,0:T(8,128)} %prefix.1), calls=%async_computation.2 | async-start | bytes 1048576 | tf_op jit(solution)/shard_map/all_to_all | solution.py:374
  73.0 3.7 %attention_far.1 = (bf16[128,640]{1,0:T(8,128)(2,1)}, f32[16,128]{1,0:T(8,128)S(1)}) custom-call(s32[1,128]{1,0:T(1,128)S(1)} %bitcast.16, bf16[128,640]{1,0:T(8,128)(2,1)S(1)} %copy-done.12, s32[1,128]{1,0:T(1,128)S(1)} %bitcast.17, bf16[8,128,128]{2,1,0:T(8,128)(2,1)} %collective-permute-done.1.rest_0_, ...), custom_call_target="tpu_custom_call" | custom-call | flops 10000000000 | tf_op jit(solution)/shard_map/attention_far/pallas_call | solution.py:354
  76.7 11.8 %all-to-all-done.2.pre_ref = f32[32,8,512]{2,1,0:T(8,128)S(1)} async-done(((f32[32,8,512]{2,1,0:T(8,128)}), f32[32,8,512]{2,1,0:T(8,128)S(1)}, u32[]{:S(2)}, u32[]{:S(2)}) %all-to-all-start.2) | async-done | bytes 524320 | tf_op jit(solution)/shard_map/all_to_all | solution.py:374
  88.7 2.0 %collective-permute-start.10 = (f32[256,512]{1,0:T(8,128)S(1)}, f32[256,512]{1,0:T(8,128)S(1)}, u32[]{:S(2)}, u32[]{:S(2)}) collective-permute-start(f32[256,512]{1,0:T(8,128)S(1)} %get-tuple-element.34), channel_id=1, source_target_pairs={{0,4},{4,0},{8,12},{12,8},{16,20},{20,16},{24,28},{28,24},{32,36},... | collective-permute-start | bytes 1572872 | tf_op jit(solution)/shard_map/ppermute | solution.py:330
  90.7 1.5 %collective-permute-done.10.got_ref = f32[256,512]{1,0:T(8,128)S(1)} collective-permute-done((f32[256,512]{1,0:T(8,128)S(1)}, f32[256,512]{1,0:T(8,128)S(1)}, u32[]{:S(2)}, u32[]{:S(2)}) %collective-permute-start.10) | collective-permute-done | bytes 524320 | tf_op jit(solution)/shard_map/ppermute | solution.py:330
  93.2 1.3 %collective-permute-start.11 = (f32[8,128]{1,0:T(8,128)S(1)}, f32[8,128]{1,0:T(8,128)S(1)}, u32[]{:S(2)}, u32[]{:S(2)}) collective-permute-start(f32[8,128]{1,0:T(8,128)S(1)} %get-tuple-element.36.s0), channel_id=1, source_target_pairs={{0,1},{1,0},{2,3},{3,2},{4,5},{5,4},{6,7},{7,6},{8,9},{9,8},{10,11... | collective-permute-start | bytes 12296 | tf_op jit(solution)/shard_map/ppermute | solution.py:385
  94.5 2.6 %collective-permute-start.12 = (f32[8,128]{1,0:T(8,128)S(1)}, f32[8,128]{1,0:T(8,128)S(1)}, u32[]{:S(2)}, u32[]{:S(2)}) collective-permute-start(f32[8,128]{1,0:T(8,128)S(1)} %get-tuple-element.36.s0), channel_id=1, source_target_pairs={{0,2},{1,3},{2,0},{3,1},{4,6},{5,7},{6,4},{7,5},{8,10},{9,11},{10,... | collective-permute-start | bytes 12296 | tf_op jit(solution)/shard_map/ppermute | solution.py:385
  97.1 1.3 %collective-permute-done.12.s2 = f32[8,128]{1,0:T(8,128)S(1)} collective-permute-done((f32[8,128]{1,0:T(8,128)S(1)}, f32[8,128]{1,0:T(8,128)S(1)}, u32[]{:S(2)}, u32[]{:S(2)}) %collective-permute-start.12) | collective-permute-done | bytes 4128 | tf_op jit(solution)/shard_map/ppermute | solution.py:385
  98.5 2.3 %collective-permute-done.13.s3 = f32[8,128]{1,0:T(8,128)S(1)} collective-permute-done((f32[8,128]{1,0:T(8,128)S(1)}, f32[8,128]{1,0:T(8,128)S(1)}, u32[]{:S(2)}, u32[]{:S(2)}) %collective-permute-start.13) | collective-permute-done | bytes 4128 | tf_op jit(solution)/shard_map/ppermute | solution.py:385
  101.7 2.1 %collective-permute-start.14 = (bf16[32,128]{1,0:T(8,128)(2,1)S(1)}, bf16[32,128]{1,0:T(8,128)(2,1)S(1)}, u32[]{:S(2)}, u32[]{:S(2)}) collective-permute-start(bf16[32,128]{1,0:T(8,128)(2,1)S(1)} %get-tuple-element.39.own_ref), channel_id=1, source_target_pairs={{0,4},{4,0},{8,12},{12,8},{16,20},{20,16},{24,28},{28,24},{32,36},... | collective-permute-start | bytes 24584 | tf_op jit(solution)/shard_map/ppermute | solution.py:330
  104.7 15.8 %all_to_all.20.in_ref = bf16[32,32,128]{2,1,0:T(8,128)(2,1)S(1)} all-to-all(bf16[32,32,128]{2,1,0:T(8,128)(2,1)S(1)} %least.1), channel_id=1, replica_groups={{0,8,16,24,32,40,48,56,64,72,80,88,96,104,112,120,128,136,144,152,160,1..., dimensions={0} | all-to-all | bytes 524288 | tf_op jit(solution)/shard_map/all_to_all | solution.py:393
  (58 shorter events, 14.9 us)
Async XLA Ops:
  3.0 9.2 %copy-start = (bf16[128,1024]{1,0:T(8,128)(2,1)S(1)}, bf16[128,1024]{1,0:T(8,128)(2,1)}, u32[]{:S(2)}) copy-start(bf16[128,1024]{1,0:T(8,128)(2,1)} %x_ref.3) | copy-start | bytes 786436
  3.0 9.2 %copy-start.3 = (bf16[128,256]{1,0:T(8,128)(2,1)S(1)}, bf16[128,256]{1,0:T(8,128)(2,1)}, u32[]{:S(2)}) copy-start(bf16[128,256]{1,0:T(8,128)(2,1)} %b_ref.3) | copy-start | bytes 196612
  3.0 9.2 %copy-start.6 = (f32[128,16]{0,1:T(8,128)S(1)}, f32[128,16]{0,1:T(8,128)}, u32[]{:S(2)}) copy-start(f32[128,16]{0,1:T(8,128)} %param.19) | copy-start | bytes 24580
  3.0 27.1 %all-to-all-start = ((bf16[8,128,256]{2,1,0:T(8,128)(2,1)}), bf16[8,128,256]{2,1,0:T(8,128)(2,1)S(1)}, u32[]{:S(2)}, u32[]{:S(2)}) async-start(bf16[8,128,256]{2,1,0:T(8,128)(2,1)} %copies.1), calls=%async_computation | async-start | bytes 1048576 | tf_op jit(solution)/shard_map/all_to_all | solution.py:341
  12.8 21.4 %copy-start.2 = (bf16[128,256]{1,0:T(8,128)(2,1)S(1)}, bf16[128,256]{1,0:T(8,128)(2,1)}, u32[]{:S(2)}) copy-start(bf16[128,256]{1,0:T(8,128)(2,1)} %c_ref.3) | copy-start | bytes 196612
  15.9 18.3 %copy-start.10 = (f32[16]{0:T(128)S(1)}, f32[16]{0:T(128)}, u32[]{:S(2)}) copy-start(f32[16]{0:T(128)} %param.21) | copy-start | bytes 196
  15.9 19.5 %collective-permute-start.6 = (f32[264,512]{1,0:T(8,128)}, f32[264,512]{1,0:T(8,128)S(1)}, u32[]{:S(2)}, u32[]{:S(2)}) collective-permute-start(f32[264,512]{1,0:T(8,128)} %get-tuple-element.24), channel_id=1, source_target_pairs={{0,4},{4,0},{8,12},{12,8},{16,20},{20,16},{24,28},{28,24},{32,36},... | collective-permute-start | bytes 1622024 | tf_op jit(solution)/shard_map/ppermute | solution.py:330
  30.1 13.1 %collective-permute-start = (bf16[8,128,256]{2,1,0:T(8,128)(2,1)S(1)}, bf16[8,128,256]{2,1,0:T(8,128)(2,1)S(1)}, u32[]{:S(2)}, u32[]{:S(2)}) collective-permute-start(bf16[8,128,256]{2,1,0:T(8,128)(2,1)S(1)} %all-to-all-done.rest_0_.rest_1_), channel_id=1, source_target_pairs={{0,8},{4,12},{8,0},{12,4},{16,24},{20,28},{24,16},{28,20},{32,40},... | collective-permute-start | bytes 1572872 | tf_op jit(solution)/shard_map/ppermute | solution.py:330
  31.3 14.7 %collective-permute-start.2 = (bf16[8,128,256]{2,1,0:T(8,128)(2,1)S(1)}, bf16[8,128,256]{2,1,0:T(8,128)(2,1)}, u32[]{:S(2)}, u32[]{:S(2)}) collective-permute-start(bf16[8,128,256]{2,1,0:T(8,128)(2,1)S(1)} %all-to-all-done.rest_0_.rest_1_), channel_id=1, source_target_pairs={{0,24},{4,28},{8,16},{12,20},{16,8},{20,12},{24,0},{28,4},{32,56},... | collective-permute-start | bytes 1572872 | tf_op jit(solution)/shard_map/ppermute | solution.py:330
  33.1 17.5 %collective-permute-start.9 = (bf16[8,128,256]{2,1,0:T(8,128)(2,1)S(1)}, bf16[8,128,256]{2,1,0:T(8,128)(2,1)}, u32[]{:S(2)}, u32[]{:S(2)}) collective-permute-start(bf16[8,128,256]{2,1,0:T(8,128)(2,1)S(1)} %all-to-all-done.rest_0_.rest_1_), channel_id=1, source_target_pairs={{0,4},{4,0},{8,12},{12,8},{16,20},{20,16},{24,28},{28,24},{32,36},... | collective-permute-start | bytes 1572872 | tf_op jit(solution)/shard_map/ppermute | solution.py:330
  36.3 27.2 %all-to-all-start.1 = ((f32[32,8,640]{2,1,0:T(8,128)}), f32[32,8,640]{2,1,0:T(8,128)S(1)}, u32[]{:S(2)}, u32[]{:S(2)}) async-start(f32[32,8,640]{2,1,0:T(8,128)} %chip_state.1), calls=%async_computation.1 | async-start | bytes 1310720 | tf_op jit(solution)/shard_map/all_to_all | solution.py:367
  43.3 13.5 %collective-permute-start.1 = (bf16[8,128,128]{2,1,0:T(8,128)(2,1)S(1)}, bf16[8,128,128]{2,1,0:T(8,128)(2,1)}, u32[]{:S(2)}, u32[]{:S(2)}) collective-permute-start(bf16[8,128,128]{2,1,0:T(8,128)(2,1)S(1)} %slice.8), channel_id=1, source_target_pairs={{0,24},{4,28},{8,16},{12,20},{16,8},{20,12},{24,0},{28,4},{32,56},... | collective-permute-start | bytes 786440 | tf_op jit(solution)/shard_map/ppermute | solution.py:330
  47.0 12.1 %collective-permute-start.3 = (bf16[8,128,128]{2,1,0:T(8,128)(2,1)S(1)}, bf16[8,128,128]{2,1,0:T(8,128)(2,1)}, u32[]{:S(2)}, u32[]{:S(2)}) collective-permute-start(bf16[8,128,128]{2,1,0:T(8,128)(2,1)S(1)} %slice.9), channel_id=1, source_target_pairs={{0,8},{4,12},{8,0},{12,4},{16,24},{20,28},{24,16},{28,20},{32,40},... | collective-permute-start | bytes 786440 | tf_op jit(solution)/shard_map/ppermute | solution.py:330
  47.1 12.1 %collective-permute-start.7 = (bf16[8,128,256]{2,1,0:T(8,128)(2,1)S(1)}, bf16[8,128,256]{2,1,0:T(8,128)(2,1)S(1)}, u32[]{:S(2)}, u32[]{:S(2)}) collective-permute-start(bf16[8,128,256]{2,1,0:T(8,128)(2,1)S(1)} %collective-permute-done.rest_0_.rest_1_), channel_id=1, source_target_pairs={{0,4},{4,0},{8,12},{12,8},{16,20},{20,16},{24,28},{28,24},{32,36},... | collective-permute-start | bytes 1572872 | tf_op jit(solution)/shard_map/ppermute | solution.py:330
  50.5 8.7 %collective-permute-start.8 = (bf16[8,128,256]{2,1,0:T(8,128)(2,1)}, bf16[8,128,256]{2,1,0:T(8,128)(2,1)S(1)}, u32[]{:S(2)}, u32[]{:S(2)}) collective-permute-start(bf16[8,128,256]{2,1,0:T(8,128)(2,1)} %collective-permute-done.2.rest_4_.rest_5_), channel_id=1, source_target_pairs={{0,4},{4,0},{8,12},{12,8},{16,20},{20,16},{24,28},{28,24},{32,36},... | collective-permute-start | bytes 1572872 | tf_op jit(solution)/shard_map/ppermute | solution.py:330
  56.8 15.0 %collective-permute-start.4 = (bf16[8,128,128]{2,1,0:T(8,128)(2,1)}, bf16[8,128,128]{2,1,0:T(8,128)(2,1)S(1)}, u32[]{:S(2)}, u32[]{:S(2)}) collective-permute-start(bf16[8,128,128]{2,1,0:T(8,128)(2,1)} %collective-permute-done.1.rest_0_), channel_id=1, source_target_pairs={{0,4},{4,0},{8,12},{12,8},{16,20},{20,16},{24,28},{28,24},{32,36},... | collective-permute-start | bytes 786440 | tf_op jit(solution)/shard_map/ppermute | solution.py:330
  59.2 12.6 %collective-permute-start.5 = (bf16[8,128,128]{2,1,0:T(8,128)(2,1)}, bf16[8,128,128]{2,1,0:T(8,128)(2,1)S(1)}, u32[]{:S(2)}, u32[]{:S(2)}) collective-permute-start(bf16[8,128,128]{2,1,0:T(8,128)(2,1)} %collective-permute-done.3.rest_1_), channel_id=1, source_target_pairs={{0,4},{4,0},{8,12},{12,8},{16,20},{20,16},{24,28},{28,24},{32,36},... | collective-permute-start | bytes 786440 | tf_op jit(solution)/shard_map/ppermute | solution.py:330
  64.4 24.2 %all-to-all-start.2 = ((f32[32,8,512]{2,1,0:T(8,128)}), f32[32,8,512]{2,1,0:T(8,128)S(1)}, u32[]{:S(2)}, u32[]{:S(2)}) async-start(f32[32,8,512]{2,1,0:T(8,128)} %prefix.1), calls=%async_computation.2 | async-start | bytes 1048576 | tf_op jit(solution)/shard_map/all_to_all | solution.py:374
  88.7 3.5 %collective-permute-start.10 = (f32[256,512]{1,0:T(8,128)S(1)}, f32[256,512]{1,0:T(8,128)S(1)}, u32[]{:S(2)}, u32[]{:S(2)}) collective-permute-start(f32[256,512]{1,0:T(8,128)S(1)} %get-tuple-element.34), channel_id=1, source_target_pairs={{0,4},{4,0},{8,12},{12,8},{16,20},{20,16},{24,28},{28,24},{32,36},... | collective-permute-start | bytes 1572872 | tf_op jit(solution)/shard_map/ppermute | solution.py:330
  93.2 7.6 %copy-start.7 = (f32[1024]{0:T(1024)S(1)}, f32[1024]{0:T(1024)}, u32[]{:S(2)}) copy-start(f32[1024]{0:T(1024)} %param.22) | copy-start | bytes 12292
  93.2 3.9 %collective-permute-start.11 = (f32[8,128]{1,0:T(8,128)S(1)}, f32[8,128]{1,0:T(8,128)S(1)}, u32[]{:S(2)}, u32[]{:S(2)}) collective-permute-start(f32[8,128]{1,0:T(8,128)S(1)} %get-tuple-element.36.s0), channel_id=1, source_target_pairs={{0,1},{1,0},{2,3},{3,2},{4,5},{5,4},{6,7},{7,6},{8,9},{9,8},{10,11... | collective-permute-start | bytes 12296 | tf_op jit(solution)/shard_map/ppermute | solution.py:385
  94.5 4.0 %collective-permute-start.12 = (f32[8,128]{1,0:T(8,128)S(1)}, f32[8,128]{1,0:T(8,128)S(1)}, u32[]{:S(2)}, u32[]{:S(2)}) collective-permute-start(f32[8,128]{1,0:T(8,128)S(1)} %get-tuple-element.36.s0), channel_id=1, source_target_pairs={{0,2},{1,3},{2,0},{3,1},{4,6},{5,7},{6,4},{7,5},{8,10},{9,11},{10,... | collective-permute-start | bytes 12296 | tf_op jit(solution)/shard_map/ppermute | solution.py:385
  97.1 3.7 %collective-permute-start.13 = (f32[8,128]{1,0:T(8,128)S(1)}, f32[8,128]{1,0:T(8,128)S(1)}, u32[]{:S(2)}, u32[]{:S(2)}) collective-permute-start(f32[8,128]{1,0:T(8,128)S(1)} %get-tuple-element.36.s0), channel_id=1, source_target_pairs={{0,3},{1,2},{2,1},{3,0},{4,7},{5,6},{6,5},{7,4},{8,11},{9,10},{10,... | collective-permute-start | bytes 12296 | tf_op jit(solution)/shard_map/ppermute | solution.py:385
  101.7 2.9 %collective-permute-start.14 = (bf16[32,128]{1,0:T(8,128)(2,1)S(1)}, bf16[32,128]{1,0:T(8,128)(2,1)S(1)}, u32[]{:S(2)}, u32[]{:S(2)}) collective-permute-start(bf16[32,128]{1,0:T(8,128)(2,1)S(1)} %get-tuple-element.39.own_ref), channel_id=1, source_target_pairs={{0,4},{4,0},{8,12},{12,8},{16,20},{20,16},{24,28},{28,24},{32,36},... | collective-permute-start | bytes 24584 | tf_op jit(solution)/shard_map/ppermute | solution.py:330
  (9 other events, 23.4 us)

commit v3 on v2

--- a/solution.py
+++ b/solution.py
@@ -253,43 +253,40 @@
             total = join(total, values[:, n * TOK : (n + 1) * TOK])
         return total
 
-    def find(block, masked):
-        highest[...] = jnp.maximum(highest[...], fold(jnp.maximum, score(block, masked)))
-
-    def add(block, masked):
+    def absorb(block, masked):
         vals = load(pl.ds(block * span, span), 1)
-        gap = score(block, masked) - jnp.concatenate([highest[...]] * (width // TOK), axis=1)
+        scores = score(block, masked)
+        old = highest[...]
+        new = jnp.maximum(old, jnp.max(fold(jnp.maximum, scores), axis=1, keepdims=True))
+        factor = jnp.exp2((old - new) * SCORE_SCALE)
+        gap = scores - jnp.concatenate([new] * (width // TOK), axis=1)
         weights = jnp.exp2(gap * SCORE_SCALE)
-        totals[...] += fold(jnp.add, weights)
-        accum[...] += mm(weights.astype(BF16), vals)
+        highest[...] = new
+        totals[...] = totals[...] * factor + fold(jnp.add, weights)
+        accum[...] = accum[...] * factor + mm(weights.astype(BF16), vals)
 
     size = span * 8 * TOK
     low, last = first_doc // size, z_mine // span
     inner = jnp.minimum((last_doc + size - 1) // size, last)
 
-    def sweep(absorb):
-        def edge(n, _):
-            absorb(jnp.where(n == 0, last, low + n - 1), True)
-            return 0
-
-        def inside(block, _):
-            absorb(block, False)
-            return 0
-
-        lax.fori_loop(0, inner - low + 1, edge, 0)
-        lax.fori_loop(inner, last, inside, 0)
-
-    highest[...] = jnp.full((ROWS, HD), FLOOR, F32) if first else old_highest[...]
-    sweep(find)
-    highest[...] = jnp.broadcast_to(jnp.max(highest[...], axis=1, keepdims=True), (ROWS, HD))
+    def edge(n, _):
+        absorb(jnp.where(n == 0, last, low + n - 1), True)
+        return 0
+
+    def inside(block, _):
+        absorb(block, False)
+        return 0
+
     if first:
+        highest[...] = jnp.full((ROWS, HD), 0.1 * FLOOR, F32)
         totals[...] = jnp.zeros((ROWS, HD), F32)
         accum[...] = jnp.zeros((ROWS, HD), F32)
     else:
-        factor = jnp.exp2((old_highest[...] - highest[...]) * SCORE_SCALE)
-        totals[...] = old_totals[...] * factor
-        accum[...] = old_accum[...] * factor
-    sweep(add)
+        highest[...] = old_highest[...]
+        totals[...] = old_totals[...]
+        accum[...] = old_accum[...]
+    lax.fori_loop(0, inner - low + 1, edge, 0)
+    lax.fori_loop(inner, last, inside, 0)
     if not final:
         return
     rng_ref[...] = jnp.zeros(rng_ref.shape, F32)
@@ -364,12 +361,13 @@
         intra_kernel, [((TOK, COLS), F32), ((TOK, HEADS), F32)], [VMEM] * 7, "intra"
     )(x_in, b_in, c_in, dt_t, a_row, skip_row, doc_row)
     (chunks,) = call(chip_kernel, [((CHIPS, 8, HALF + 128), F32)], [VMEM] * 2, "chip_state")(keep, got)
+    near, chunks, y_part = lax.optimization_barrier((near, chunks, y_part))
     chunks = lax.all_to_all(chunks, "seq", 0, 0, tiled=True, axis_index_groups=same_core)
     side1, side3 = swap(near, 2), swap(near, 6)
     carry = attend([[near]], (0,), 4, True, False, [], "attention_near")
+    far = [swap(side1[:, :, :HD], 6), swap(side3[:, :, HD:], 2)]
+    chunks, _, _ = lax.optimization_barrier((chunks, carry, far))
     carry = attend([[side1], [side3]], (1, 3), 2, False, False, carry, "attention_sides")
-    chunks, carry, y_part = lax.optimization_barrier((chunks, carry, y_part))
-    far = [swap(side1[:, :, :HD], 6), swap(side3[:, :, HD:], 2)]
     (prefix,) = call(prefix_kernel, [((CHIPS, 8, HALF), F32)], [VMEM], "prefix")(chunks)
     prefix = lax.all_to_all(prefix, "seq", 0, 0, tiled=True, axis_index_groups=same_core)
     attn_out, attn_rng = attend([far], (2,), 4, False, True, carry, "attention_far")

time: 121 us -> 116 us (0.959)
  waiting for transfers between devices: 37.2 us -> 32.5 us
  Pallas kernels: 19.8 us -> 18 us
    all_to_all x1, waiting for transfers between devices: 11.8 us -> 8.02 us  [body(): lax.all_to_all(prefix, 'seq', 0, 0, tiled=True, axis_index_groups=same_core)]
    all_to_all x1, starting transfers between devices: 7.36 us -> 5.49 us  [body(): lax.all_to_all(prefix, 'seq', 0, 0, tiled=True, axis_index_groups=same_core)]
    all_to_all x1, waiting for transfers between devices: 13.2 us -> 11.5 us  [body(): lax.all_to_all(near, 'seq', 0, 0, tiled=True, axis_index_groups=column)]
    ppermute x12, starting transfers between devices: 17.8 us -> 19.5 us  [swap(): return lax.ppermute(value, 'seq', [(i, i ^ bit) for i in range(count)])]
  transfers between devices with their start and end apart: 18 -> 18, of which waited for: 8 -> 10; matrix products, arithmetic and copies ran while one was open for 1% -> 1% of each run, Pallas kernels for 13% -> 12%
where the time goes in v3:
time: 116 us; the launch traced here: 115 us
  starting transfers between devices  42 us (36%)
  waiting for transfers between devices  32.5 us (28%)
  Pallas kernels  18 us (16%)
  blocking collectives  15.8 us (14%)
  local copies, waits for them, and re-layouts  6.24 us (5%)
    ppermute x12, starting transfers between devices, swap(): return lax.ppermute(value, 'seq', [(i, i ^ bit) for i in range(count)])  19.5 us
    all_to_all x1, blocking collectives, body(): lax.all_to_all(rng, 'seq', 0, 0, tiled=True, axis_index_groups=same_core)  15.8 us
    all_to_all x1, waiting for transfers between devices, body(): lax.all_to_all(near, 'seq', 0, 0, tiled=True, axis_index_groups=column)  11.5 us
    ppermute x12, waiting for transfers between devices, swap(): return lax.ppermute(value, 'seq', [(i, i ^ bit) for i in range(count)])  9.34 us
    pallas_call x3, Pallas kernels, attend(): call(functools.partial(attn_kernel, flips, span, first, final), outs, [SM...  9.21 us
    all_to_all x1, starting transfers between devices, body(): lax.all_to_all(near, 'seq', 0, 0, tiled=True, axis_index_groups=column)  9.15 us
    all_to_all x1, waiting for transfers between devices, body(): lax.all_to_all(prefix, 'seq', 0, 0, tiled=True, axis_index_groups=same_core)  8.02 us
    all_to_all x1, starting transfers between devices, body(): lax.all_to_all(prefix, 'seq', 0, 0, tiled=True, axis_index_groups=same_core)  5.49 us
  transfers between devices with their start and end apart: 18, of which 10 were waited for; matrix products, arithmetic and copies ran while one was open for 1% of the time, Pallas kernels for 12%

profile of v3, /device:TPU:1, one launch (start us, length us, event | category | flops | bytes accessed | tf_op | source)
XLA Modules:
  0.0 115.4 jit_solution(6141420759749403344)
XLA Ops:
  3.0 9.1 %all-to-all-start = ((bf16[8,128,256]{2,1,0:T(8,128)(2,1)}), bf16[8,128,256]{2,1,0:T(8,128)(2,1)S(1)}, u32[]{:S(2)}, u32[]{:S(2)}) async-start(bf16[8,128,256]{2,1,0:T(8,128)(2,1)} %copies.1), calls=%async_computation | async-start | bytes 1048576 | tf_op jit(solution)/shard_map/all_to_all | solution.py:338
  12.8 2.3 %local_state.1 = (f32[264,512]{1,0:T(8,128)S(1)}, f32[264,512]{1,0:T(8,128)S(1)}) custom-call(s32[1,128]{1,0:T(1,128)S(1)} %bitcast.10, bf16[128,1024]{1,0:T(8,128)(2,1)S(1)} %copy-done, bf16[128,256]{1,0:T(8,128)(2,1)S(1)} %copy-done.3, f32[16,128]{1,0:T(8,128)S(1)} %bitcast.5, f32[1,16]{1,0:T(1,128)S(1)} %bitcast.8), custom_call_target="tpu_custom_call" | custom-call | tf_op jit(solution)/shard_map/local_state/pallas_call | solution.py:356
  18.6 11.5 %all-to-all-done.rest_0_.rest_1_ = bf16[8,128,256]{2,1,0:T(8,128)(2,1)S(1)} async-done(((bf16[8,128,256]{2,1,0:T(8,128)(2,1)}), bf16[8,128,256]{2,1,0:T(8,128)(2,1)S(1)}, u32[]{:S(2)}, u32[]{:S(2)}) %all-to-all-start) | async-done | bytes 524320 | tf_op jit(solution)/shard_map/all_to_all | solution.py:338
  30.1 1.2 %collective-permute-start.1 = (bf16[8,128,256]{2,1,0:T(8,128)(2,1)S(1)}, bf16[8,128,256]{2,1,0:T(8,128)(2,1)S(1)}, u32[]{:S(2)}, u32[]{:S(2)}) collective-permute-start(bf16[8,128,256]{2,1,0:T(8,128)(2,1)S(1)} %all-to-all-done.rest_0_.rest_1_), channel_id=1, source_target_pairs={{0,8},{4,12},{8,0},{12,4},{16,24},{20,28},{24,16},{28,20},{32,40},... | collective-permute-start | bytes 1572872 | tf_op jit(solution)/shard_map/ppermute | solution.py:327
  31.3 1.8 %collective-permute-start.3 = (bf16[8,128,256]{2,1,0:T(8,128)(2,1)S(1)}, bf16[8,128,256]{2,1,0:T(8,128)(2,1)}, u32[]{:S(2)}, u32[]{:S(2)}) collective-permute-start(bf16[8,128,256]{2,1,0:T(8,128)(2,1)S(1)} %all-to-all-done.rest_0_.rest_1_), channel_id=1, source_target_pairs={{0,24},{4,28},{8,16},{12,20},{16,8},{20,12},{24,0},{28,4},{32,56},... | collective-permute-start | bytes 1572872 | tf_op jit(solution)/shard_map/ppermute | solution.py:327
  34.2 3.9 %all-to-all-start.1 = ((f32[32,8,640]{2,1,0:T(8,128)}), f32[32,8,640]{2,1,0:T(8,128)S(1)}, u32[]{:S(2)}, u32[]{:S(2)}) async-start(f32[32,8,640]{2,1,0:T(8,128)} %chip_state.1), calls=%async_computation.1 | async-start | bytes 1310720 | tf_op jit(solution)/shard_map/all_to_all | solution.py:365
  38.1 5.6 %collective-permute-done.1.rest_0_.rest_1_ = bf16[8,128,256]{2,1,0:T(8,128)(2,1)S(1)} collective-permute-done((bf16[8,128,256]{2,1,0:T(8,128)(2,1)S(1)}, bf16[8,128,256]{2,1,0:T(8,128)(2,1)S(1)}, u32[]{:S(2)}, u32[]{:S(2)}) %collective-permute-start.1) | collective-permute-done | bytes 524320 | tf_op jit(solution)/shard_map/ppermute | solution.py:327
  43.7 2.8 %collective-permute-start.2 = (bf16[8,128,128]{2,1,0:T(8,128)(2,1)S(1)}, bf16[8,128,128]{2,1,0:T(8,128)(2,1)}, u32[]{:S(2)}, u32[]{:S(2)}) collective-permute-start(bf16[8,128,128]{2,1,0:T(8,128)(2,1)S(1)} %slice.8), channel_id=1, source_target_pairs={{0,24},{4,28},{8,16},{12,20},{16,8},{20,12},{24,0},{28,4},{32,56},... | collective-permute-start | bytes 786440 | tf_op jit(solution)/shard_map/ppermute | solution.py:327
  48.1 5.0 %collective-permute-start.7 = (bf16[8,128,256]{2,1,0:T(8,128)(2,1)S(1)}, bf16[8,128,256]{2,1,0:T(8,128)(2,1)}, u32[]{:S(2)}, u32[]{:S(2)}) collective-permute-start(bf16[8,128,256]{2,1,0:T(8,128)(2,1)S(1)} %collective-permute-done.1.rest_0_.rest_1_), channel_id=1, source_target_pairs={{0,4},{4,0},{8,12},{12,8},{16,20},{20,16},{24,28},{28,24},{32,36},... | collective-permute-start | bytes 1572872 | tf_op jit(solution)/shard_map/ppermute | solution.py:327
  53.2 2.6 %attention_near.1.rest_8_ = f32[3,640,128]{2,1,0:T(8,128)S(1)} custom-call(s32[1,128]{1,0:T(1,128)S(1)} %bitcast.12, bf16[128,640]{1,0:T(8,128)(2,1)S(1)} %copy-done.11, s32[1,128]{1,0:T(1,128)S(1)} %bitcast.13, bf16[8,128,256]{2,1,0:T(8,128)(2,1)S(1)} %all-to-all-done.rest_0_.rest_1_, bf16[8,128,256]{2,1,0:T(8,128)(2,1)S(1)} %all-to-all-done.rest_0_.rest_1_, ...), custom_call_target="tpu_custom_call" | custom-call | flops 10000000000 | tf_op jit(solution)/shard_map/attention_near/pallas_call | solution.py:351
  57.3 2.4 %collective-permute-start.5 = (bf16[8,128,128]{2,1,0:T(8,128)(2,1)}, bf16[8,128,128]{2,1,0:T(8,128)(2,1)S(1)}, u32[]{:S(2)}, u32[]{:S(2)}) collective-permute-start(bf16[8,128,128]{2,1,0:T(8,128)(2,1)} %collective-permute-done.2.rest_0_), channel_id=1, source_target_pairs={{0,4},{4,0},{8,12},{12,8},{16,20},{20,16},{24,28},{28,24},{32,36},... | collective-permute-start | bytes 786440 | tf_op jit(solution)/shard_map/ppermute | solution.py:327
  60.5 5.5 %all-to-all-start.2 = ((f32[32,8,512]{2,1,0:T(8,128)}), f32[32,8,512]{2,1,0:T(8,128)S(1)}, u32[]{:S(2)}, u32[]{:S(2)}) async-start(f32[32,8,512]{2,1,0:T(8,128)} %prefix.1), calls=%async_computation.2 | async-start | bytes 1048576 | tf_op jit(solution)/shard_map/all_to_all | solution.py:372
  66.9 1.2 %copy-done.14 = f32[3,640,128]{2,1,0:T(8,128)S(1)} copy-done((f32[3,640,128]{2,1,0:T(8,128)S(1)}, f32[3,640,128]{2,1,0:T(8,128)}, u32[]{:S(2)}) %copy-start.14) | copy-done | bytes 983064
  68.1 3.4 %attention_sides.1.rest_4_ = f32[3,640,128]{2,1,0:T(8,128)S(1)} custom-call(s32[1,128]{1,0:T(1,128)S(1)} %bitcast.14, bf16[128,640]{1,0:T(8,128)(2,1)S(1)} %copy-done.12, s32[1,128]{1,0:T(1,128)S(1)} %bitcast.15, bf16[8,128,256]{2,1,0:T(8,128)(2,1)S(1)} %collective-permute-done.1.rest_0_.rest_1_, ...), custom_call_target="tpu_custom_call" | custom-call | flops 10000000000 | tf_op jit(solution)/shard_map/attention_sides/pallas_call | solution.py:351
  71.6 3.2 %attention_far.1 = (bf16[128,640]{1,0:T(8,128)(2,1)}, f32[16,128]{1,0:T(8,128)S(1)}) custom-call(s32[1,128]{1,0:T(1,128)S(1)} %bitcast.16, bf16[128,640]{1,0:T(8,128)(2,1)S(1)} %copy-done.12, s32[1,128]{1,0:T(1,128)S(1)} %bitcast.17, bf16[8,128,128]{2,1,0:T(8,128)(2,1)} %collective-permute-done.2.rest_0_, ...), custom_call_target="tpu_custom_call" | custom-call | flops 10000000000 | tf_op jit(solution)/shard_map/attention_far/pallas_call | solution.py:351
  74.8 8.0 %all-to-all-done.2.pre_ref = f32[32,8,512]{2,1,0:T(8,128)S(1)} async-done(((f32[32,8,512]{2,1,0:T(8,128)}), f32[32,8,512]{2,1,0:T(8,128)S(1)}, u32[]{:S(2)}, u32[]{:S(2)}) %all-to-all-start.2) | async-done | bytes 524320 | tf_op jit(solution)/shard_map/all_to_all | solution.py:372
  82.9 2.0 %collective-permute-start.10 = (f32[256,512]{1,0:T(8,128)S(1)}, f32[256,512]{1,0:T(8,128)S(1)}, u32[]{:S(2)}, u32[]{:S(2)}) collective-permute-start(f32[256,512]{1,0:T(8,128)S(1)} %get-tuple-element.36), channel_id=1, source_target_pairs={{0,4},{4,0},{8,12},{12,8},{16,20},{20,16},{24,28},{28,24},{32,36},... | collective-permute-start | bytes 1572872 | tf_op jit(solution)/shard_map/ppermute | solution.py:327
  84.9 1.5 %collective-permute-done.10.got_ref = f32[256,512]{1,0:T(8,128)S(1)} collective-permute-done((f32[256,512]{1,0:T(8,128)S(1)}, f32[256,512]{1,0:T(8,128)S(1)}, u32[]{:S(2)}, u32[]{:S(2)}) %collective-permute-start.10) | collective-permute-done | bytes 524320 | tf_op jit(solution)/shard_map/ppermute | solution.py:327
  87.4 1.3 %collective-permute-start.11 = (f32[8,128]{1,0:T(8,128)S(1)}, f32[8,128]{1,0:T(8,128)S(1)}, u32[]{:S(2)}, u32[]{:S(2)}) collective-permute-start(f32[8,128]{1,0:T(8,128)S(1)} %get-tuple-element.38.s0), channel_id=1, source_target_pairs={{0,1},{1,0},{2,3},{3,2},{4,5},{5,4},{6,7},{7,6},{8,9},{9,8},{10,11... | collective-permute-start | bytes 12296 | tf_op jit(solution)/shard_map/ppermute | solution.py:383
  88.8 2.6 %collective-permute-start.12 = (f32[8,128]{1,0:T(8,128)S(1)}, f32[8,128]{1,0:T(8,128)S(1)}, u32[]{:S(2)}, u32[]{:S(2)}) collective-permute-start(f32[8,128]{1,0:T(8,128)S(1)} %get-tuple-element.38.s0), channel_id=1, source_target_pairs={{0,2},{1,3},{2,0},{3,1},{4,6},{5,7},{6,4},{7,5},{8,10},{9,11},{10,... | collective-permute-start | bytes 12296 | tf_op jit(solution)/shard_map/ppermute | solution.py:383
  91.4 1.3 %collective-permute-done.12.s2 = f32[8,128]{1,0:T(8,128)S(1)} collective-permute-done((f32[8,128]{1,0:T(8,128)S(1)}, f32[8,128]{1,0:T(8,128)S(1)}, u32[]{:S(2)}, u32[]{:S(2)}) %collective-permute-start.12) | collective-permute-done | bytes 4128 | tf_op jit(solution)/shard_map/ppermute | solution.py:383
  92.7 2.3 %collective-permute-done.13.s3 = f32[8,128]{1,0:T(8,128)S(1)} collective-permute-done((f32[8,128]{1,0:T(8,128)S(1)}, f32[8,128]{1,0:T(8,128)S(1)}, u32[]{:S(2)}, u32[]{:S(2)}) %collective-permute-start.13) | collective-permute-done | bytes 4128 | tf_op jit(solution)/shard_map/ppermute | solution.py:383
  96.0 2.1 %collective-permute-start.14 = (bf16[32,128]{1,0:T(8,128)(2,1)S(1)}, bf16[32,128]{1,0:T(8,128)(2,1)S(1)}, u32[]{:S(2)}, u32[]{:S(2)}) collective-permute-start(bf16[32,128]{1,0:T(8,128)(2,1)S(1)} %get-tuple-element.41.own_ref), channel_id=1, source_target_pairs={{0,4},{4,0},{8,12},{12,8},{16,20},{20,16},{24,28},{28,24},{32,36},... | collective-permute-start | bytes 24584 | tf_op jit(solution)/shard_map/ppermute | solution.py:327
  98.9 15.8 %all_to_all.20.in_ref = bf16[32,32,128]{2,1,0:T(8,128)(2,1)S(1)} all-to-all(bf16[32,32,128]{2,1,0:T(8,128)(2,1)S(1)} %least.1), channel_id=1, replica_groups={{0,8,16,24,32,40,48,56,64,72,80,88,96,104,112,120,128,136,144,152,160,1..., dimensions={0} | all-to-all | bytes 524288 | tf_op jit(solution)/shard_map/all_to_all | solution.py:391
  (58 shorter events, 16.1 us)
Async XLA Ops:
  3.0 9.2 %copy-start = (bf16[128,1024]{1,0:T(8,128)(2,1)S(1)}, bf16[128,1024]{1,0:T(8,128)(2,1)}, u32[]{:S(2)}) copy-start(bf16[128,1024]{1,0:T(8,128)(2,1)} %x_ref.3) | copy-start | bytes 786436
  3.0 9.2 %copy-start.3 = (bf16[128,256]{1,0:T(8,128)(2,1)S(1)}, bf16[128,256]{1,0:T(8,128)(2,1)}, u32[]{:S(2)}) copy-start(bf16[128,256]{1,0:T(8,128)(2,1)} %b_ref.3) | copy-start | bytes 196612
  3.0 9.2 %copy-start.6 = (f32[128,16]{0,1:T(8,128)S(1)}, f32[128,16]{0,1:T(8,128)}, u32[]{:S(2)}) copy-start(f32[128,16]{0,1:T(8,128)} %param.19) | copy-start | bytes 24580
  3.0 27.1 %all-to-all-start = ((bf16[8,128,256]{2,1,0:T(8,128)(2,1)}), bf16[8,128,256]{2,1,0:T(8,128)(2,1)S(1)}, u32[]{:S(2)}, u32[]{:S(2)}) async-start(bf16[8,128,256]{2,1,0:T(8,128)(2,1)} %copies.1), calls=%async_computation | async-start | bytes 1048576 | tf_op jit(solution)/shard_map/all_to_all | solution.py:338
  15.1 2.6 %collective-permute-start = (f32[264,512]{1,0:T(8,128)S(1)}, f32[264,512]{1,0:T(8,128)S(1)}, u32[]{:S(2)}, u32[]{:S(2)}) collective-permute-start(f32[264,512]{1,0:T(8,128)S(1)} %get-tuple-element.25), channel_id=1, source_target_pairs={{0,4},{4,0},{8,12},{12,8},{16,20},{20,16},{24,28},{28,24},{32,36},... | collective-permute-start | bytes 1622024 | tf_op jit(solution)/shard_map/ppermute | solution.py:327
  30.1 13.5 %collective-permute-start.1 = (bf16[8,128,256]{2,1,0:T(8,128)(2,1)S(1)}, bf16[8,128,256]{2,1,0:T(8,128)(2,1)S(1)}, u32[]{:S(2)}, u32[]{:S(2)}) collective-permute-start(bf16[8,128,256]{2,1,0:T(8,128)(2,1)S(1)} %all-to-all-done.rest_0_.rest_1_), channel_id=1, source_target_pairs={{0,8},{4,12},{8,0},{12,4},{16,24},{20,28},{24,16},{28,20},{32,40},... | collective-permute-start | bytes 1572872 | tf_op jit(solution)/shard_map/ppermute | solution.py:327
  31.3 15.7 %collective-permute-start.3 = (bf16[8,128,256]{2,1,0:T(8,128)(2,1)S(1)}, bf16[8,128,256]{2,1,0:T(8,128)(2,1)}, u32[]{:S(2)}, u32[]{:S(2)}) collective-permute-start(bf16[8,128,256]{2,1,0:T(8,128)(2,1)S(1)} %all-to-all-done.rest_0_.rest_1_), channel_id=1, source_target_pairs={{0,24},{4,28},{8,16},{12,20},{16,8},{20,12},{24,0},{28,4},{32,56},... | collective-permute-start | bytes 1572872 | tf_op jit(solution)/shard_map/ppermute | solution.py:327
  33.1 20.1 %collective-permute-start.9 = (bf16[8,128,256]{2,1,0:T(8,128)(2,1)S(1)}, bf16[8,128,256]{2,1,0:T(8,128)(2,1)}, u32[]{:S(2)}, u32[]{:S(2)}) collective-permute-start(bf16[8,128,256]{2,1,0:T(8,128)(2,1)S(1)} %all-to-all-done.rest_0_.rest_1_), channel_id=1, source_target_pairs={{0,4},{4,0},{8,12},{12,8},{16,20},{20,16},{24,28},{28,24},{32,36},... | collective-permute-start | bytes 1572872 | tf_op jit(solution)/shard_map/ppermute | solution.py:327
  34.2 25.4 %all-to-all-start.1 = ((f32[32,8,640]{2,1,0:T(8,128)}), f32[32,8,640]{2,1,0:T(8,128)S(1)}, u32[]{:S(2)}, u32[]{:S(2)}) async-start(f32[32,8,640]{2,1,0:T(8,128)} %chip_state.1), calls=%async_computation.1 | async-start | bytes 1310720 | tf_op jit(solution)/shard_map/all_to_all | solution.py:365
  43.7 9.5 %copy-start.11 = (bf16[128,640]{1,0:T(8,128)(2,1)S(1)}, bf16[128,640]{1,0:T(8,128)(2,1)}, u32[]{:S(2)}) copy-start(bf16[128,640]{1,0:T(8,128)(2,1)} %q_ref.5) | copy-start | bytes 491524
  43.7 13.5 %collective-permute-start.2 = (bf16[8,128,128]{2,1,0:T(8,128)(2,1)S(1)}, bf16[8,128,128]{2,1,0:T(8,128)(2,1)}, u32[]{:S(2)}, u32[]{:S(2)}) collective-permute-start(bf16[8,128,128]{2,1,0:T(8,128)(2,1)S(1)} %slice.8), channel_id=1, source_target_pairs={{0,24},{4,28},{8,16},{12,20},{16,8},{20,12},{24,0},{28,4},{32,56},... | collective-permute-start | bytes 786440 | tf_op jit(solution)/shard_map/ppermute | solution.py:327
  48.0 11.6 %collective-permute-start.4 = (bf16[8,128,128]{2,1,0:T(8,128)(2,1)S(1)}, bf16[8,128,128]{2,1,0:T(8,128)(2,1)}, u32[]{:S(2)}, u32[]{:S(2)}) collective-permute-start(bf16[8,128,128]{2,1,0:T(8,128)(2,1)S(1)} %slice.9), channel_id=1, source_target_pairs={{0,8},{4,12},{8,0},{12,4},{16,24},{20,28},{24,16},{28,20},{32,40},... | collective-permute-start | bytes 786440 | tf_op jit(solution)/shard_map/ppermute | solution.py:327
  48.1 17.9 %collective-permute-start.7 = (bf16[8,128,256]{2,1,0:T(8,128)(2,1)S(1)}, bf16[8,128,256]{2,1,0:T(8,128)(2,1)}, u32[]{:S(2)}, u32[]{:S(2)}) collective-permute-start(bf16[8,128,256]{2,1,0:T(8,128)(2,1)S(1)} %collective-permute-done.1.rest_0_.rest_1_), channel_id=1, source_target_pairs={{0,4},{4,0},{8,12},{12,8},{16,20},{20,16},{24,28},{28,24},{32,36},... | collective-permute-start | bytes 1572872 | tf_op jit(solution)/shard_map/ppermute | solution.py:327
  53.1 12.9 %collective-permute-start.8 = (bf16[8,128,256]{2,1,0:T(8,128)(2,1)}, bf16[8,128,256]{2,1,0:T(8,128)(2,1)}, u32[]{:S(2)}, u32[]{:S(2)}) collective-permute-start(bf16[8,128,256]{2,1,0:T(8,128)(2,1)} %collective-permute-done.3.rest_4_.rest_5_), channel_id=1, source_target_pairs={{0,4},{4,0},{8,12},{12,8},{16,20},{20,16},{24,28},{28,24},{32,36},... | collective-permute-start | bytes 1572872 | tf_op jit(solution)/shard_map/ppermute | solution.py:327
  57.3 14.3 %collective-permute-start.5 = (bf16[8,128,128]{2,1,0:T(8,128)(2,1)}, bf16[8,128,128]{2,1,0:T(8,128)(2,1)S(1)}, u32[]{:S(2)}, u32[]{:S(2)}) collective-permute-start(bf16[8,128,128]{2,1,0:T(8,128)(2,1)} %collective-permute-done.2.rest_0_), channel_id=1, source_target_pairs={{0,4},{4,0},{8,12},{12,8},{16,20},{20,16},{24,28},{28,24},{32,36},... | collective-permute-start | bytes 786440 | tf_op jit(solution)/shard_map/ppermute | solution.py:327
  59.6 11.9 %collective-permute-start.6 = (bf16[8,128,128]{2,1,0:T(8,128)(2,1)}, bf16[8,128,128]{2,1,0:T(8,128)(2,1)S(1)}, u32[]{:S(2)}, u32[]{:S(2)}) collective-permute-start(bf16[8,128,128]{2,1,0:T(8,128)(2,1)} %collective-permute-done.4.rest_1_), channel_id=1, source_target_pairs={{0,4},{4,0},{8,12},{12,8},{16,20},{20,16},{24,28},{28,24},{32,36},... | collective-permute-start | bytes 786440 | tf_op jit(solution)/shard_map/ppermute | solution.py:327
  60.5 22.3 %all-to-all-start.2 = ((f32[32,8,512]{2,1,0:T(8,128)}), f32[32,8,512]{2,1,0:T(8,128)S(1)}, u32[]{:S(2)}, u32[]{:S(2)}) async-start(f32[32,8,512]{2,1,0:T(8,128)} %prefix.1), calls=%async_computation.2 | async-start | bytes 1048576 | tf_op jit(solution)/shard_map/all_to_all | solution.py:372
  82.8 3.6 %copy-start.1 = (bf16[128,1024]{1,0:T(8,128)(2,1)S(1)}, bf16[128,1024]{1,0:T(8,128)(2,1)}, u32[]{:S(2)}) copy-start(bf16[128,1024]{1,0:T(8,128)(2,1)} %z_ref.1) | copy-start | bytes 786436
  82.9 3.5 %collective-permute-start.10 = (f32[256,512]{1,0:T(8,128)S(1)}, f32[256,512]{1,0:T(8,128)S(1)}, u32[]{:S(2)}, u32[]{:S(2)}) collective-permute-start(f32[256,512]{1,0:T(8,128)S(1)} %get-tuple-element.36), channel_id=1, source_target_pairs={{0,4},{4,0},{8,12},{12,8},{16,20},{20,16},{24,28},{28,24},{32,36},... | collective-permute-start | bytes 1572872 | tf_op jit(solution)/shard_map/ppermute | solution.py:327
  87.4 7.6 %copy-start.7 = (f32[1024]{0:T(1024)S(1)}, f32[1024]{0:T(1024)}, u32[]{:S(2)}) copy-start(f32[1024]{0:T(1024)} %param.22) | copy-start | bytes 12292
  87.4 4.0 %collective-permute-start.11 = (f32[8,128]{1,0:T(8,128)S(1)}, f32[8,128]{1,0:T(8,128)S(1)}, u32[]{:S(2)}, u32[]{:S(2)}) collective-permute-start(f32[8,128]{1,0:T(8,128)S(1)} %get-tuple-element.38.s0), channel_id=1, source_target_pairs={{0,1},{1,0},{2,3},{3,2},{4,5},{5,4},{6,7},{7,6},{8,9},{9,8},{10,11... | collective-permute-start | bytes 12296 | tf_op jit(solution)/shard_map/ppermute | solution.py:383
  88.8 4.0 %collective-permute-start.12 = (f32[8,128]{1,0:T(8,128)S(1)}, f32[8,128]{1,0:T(8,128)S(1)}, u32[]{:S(2)}, u32[]{:S(2)}) collective-permute-start(f32[8,128]{1,0:T(8,128)S(1)} %get-tuple-element.38.s0), channel_id=1, source_target_pairs={{0,2},{1,3},{2,0},{3,1},{4,6},{5,7},{6,4},{7,5},{8,10},{9,11},{10,... | collective-permute-start | bytes 12296 | tf_op jit(solution)/shard_map/ppermute | solution.py:383
  91.4 3.7 %collective-permute-start.13 = (f32[8,128]{1,0:T(8,128)S(1)}, f32[8,128]{1,0:T(8,128)S(1)}, u32[]{:S(2)}, u32[]{:S(2)}) collective-permute-start(f32[8,128]{1,0:T(8,128)S(1)} %get-tuple-element.38.s0), channel_id=1, source_target_pairs={{0,3},{1,2},{2,1},{3,0},{4,7},{5,6},{6,5},{7,4},{8,11},{9,10},{10,... | collective-permute-start | bytes 12296 | tf_op jit(solution)/shard_map/ppermute | solution.py:383
  96.0 2.9 %collective-permute-start.14 = (bf16[32,128]{1,0:T(8,128)(2,1)S(1)}, bf16[32,128]{1,0:T(8,128)(2,1)S(1)}, u32[]{:S(2)}, u32[]{:S(2)}) collective-permute-start(bf16[32,128]{1,0:T(8,128)(2,1)S(1)} %get-tuple-element.41.own_ref), channel_id=1, source_target_pairs={{0,4},{4,0},{8,12},{12,8},{16,20},{20,16},{24,28},{28,24},{32,36},... | collective-permute-start | bytes 24584 | tf_op jit(solution)/shard_map/ppermute | solution.py:327
  (9 other events, 10.3 us)

commit v4 on v3

--- a/solution.py
+++ b/solution.py
@@ -300,12 +300,6 @@
         rng_ref[GROUP + g : GROUP + g + 1, :] = jnp.min(-values, axis=0, keepdims=True)
 
 
-def copies_kernel(k_ref, v_ref, out_ref):
-    for dest in range(8):
-        out_ref[dest, :, 0:HD] = k_ref[...]
-        out_ref[dest, :, HD:] = v_ref[...]
-
-
 ATTN_COST = 10**10
 
 
@@ -334,7 +328,8 @@
     same_core = [[i for i in range(64) if i % 2 == core] for core in range(2)]
     column = [[z * 8 + n for z in range(8)] for n in range(8)]
 
-    (near,) = call(copies_kernel, [((8, TOK, 2 * HD), BF16)], [VMEM] * 2, "copies")(k_in, v_in)
+    near = jnp.concatenate([k_in, v_in], axis=1)[None]
+    near = jnp.broadcast_to(near, (8, TOK, 2 * HD))
     near = lax.all_to_all(near, "seq", 0, 0, tiled=True, axis_index_groups=column)
 
     def attend(parts, flips, span, first, final, carry, name):
@@ -350,7 +345,7 @@
             refs += [part[0], part[-1], other[0], other[-1]]
         return call(
             functools.partial(attn_kernel, flips, span, first, final), outs,
-            [SMEM] + [VMEM] * (2 + len(refs) + len(carry)), name, scratch=scratch, flops=ATTN_COST,
+            [SMEM] + [VMEM] * (2 + len(refs) + len(carry)), name, scratch=scratch, flops=9*10**9 if first else ATTN_COST,
         )(doc_row, q_in, doc_row, *refs, *carry)
 
     keep, send = call(

time: 116 us -> 115 us (level)
    unnamed x30 -> x26, local copies, waits for them, and re-layouts: 5.23 us -> 3.74 us
  transfers between devices with their start and end apart: 18 -> 18, of which waited for: 10 -> 10; matrix products, arithmetic and copies ran while one was open for 1% -> 1% of each run, Pallas kernels for 12% -> 13%
where the time goes in v4:
time: 115 us
  starting transfers between devices  42 us (37%)
  waiting for transfers between devices  32.5 us (28%)
  Pallas kernels  17.1 us (15%)
  blocking collectives  15.8 us (14%)
  local copies, waits for them, and re-layouts  5.58 us (5%)
    ppermute x12, starting transfers between devices, swap(): return lax.ppermute(value, 'seq', [(i, i ^ bit) for i in range(count)])  19.5 us
    all_to_all x1, blocking collectives, body(): lax.all_to_all(rng, 'seq', 0, 0, tiled=True, axis_index_groups=same_core)  15.8 us
    all_to_all x1, waiting for transfers between devices, body(): lax.all_to_all(near, 'seq', 0, 0, tiled=True, axis_index_groups=column)  11.5 us
    ppermute x12, waiting for transfers between devices, swap(): return lax.ppermute(value, 'seq', [(i, i ^ bit) for i in range(count)])  9.35 us
    pallas_call x3, Pallas kernels, attend(): call(functools.partial(attn_kernel, flips, span, first, final), outs, [SM...  9.19 us
    all_to_all x1, starting transfers between devices, body(): lax.all_to_all(near, 'seq', 0, 0, tiled=True, axis_index_groups=column)  9.15 us
    all_to_all x1, waiting for transfers between devices, body(): lax.all_to_all(prefix, 'seq', 0, 0, tiled=True, axis_index_groups=same_core)  8.02 us
    all_to_all x1, starting transfers between devices, body(): lax.all_to_all(prefix, 'seq', 0, 0, tiled=True, axis_index_groups=same_core)  5.49 us
  transfers between devices with their start and end apart: 18, of which 10 were waited for; matrix products, arithmetic and copies ran while one was open for 1% of the time, Pallas kernels for 13%

profile of v4, /device:TPU:1, one launch (start us, length us, event | category | flops | bytes accessed | tf_op | source)
XLA Modules:
  0.0 114.6 jit_solution(12527171248292469879)
XLA Ops:
  2.3 9.1 %all-to-all-start = ((bf16[8,128,256]{2,1,0:T(8,128)(2,1)}), bf16[8,128,256]{2,1,0:T(8,128)(2,1)S(1)}, u32[]{:S(2)}, u32[]{:S(2)}) async-start(bf16[8,128,256]{2,1,0:T(8,128)(2,1)} %broadcast_in_dim.19), calls=%async_computation | async-start | bytes 1048576 | tf_op jit(solution)/shard_map/all_to_all | solution.py:333
  12.1 2.3 %local_state.1 = (f32[264,512]{1,0:T(8,128)S(1)}, f32[264,512]{1,0:T(8,128)S(1)}) custom-call(s32[1,128]{1,0:T(1,128)S(1)} %bitcast.10, bf16[128,1024]{1,0:T(8,128)(2,1)S(1)} %copy-done, bf16[128,256]{1,0:T(8,128)(2,1)S(1)} %copy-done.3, f32[16,128]{1,0:T(8,128)S(1)} %bitcast.5, f32[1,16]{1,0:T(1,128)S(1)} %bitcast.8), custom_call_target="tpu_custom_call" | custom-call | tf_op jit(solution)/shard_map/local_state/pallas_call | solution.py:351
  17.9 11.5 %all-to-all-done.rest_0_.rest_1_ = bf16[8,128,256]{2,1,0:T(8,128)(2,1)S(1)} async-done(((bf16[8,128,256]{2,1,0:T(8,128)(2,1)}), bf16[8,128,256]{2,1,0:T(8,128)(2,1)S(1)}, u32[]{:S(2)}, u32[]{:S(2)}) %all-to-all-start) | async-done | bytes 524320 | tf_op jit(solution)/shard_map/all_to_all | solution.py:333
  29.4 1.2 %collective-permute-start.1 = (bf16[8,128,256]{2,1,0:T(8,128)(2,1)S(1)}, bf16[8,128,256]{2,1,0:T(8,128)(2,1)S(1)}, u32[]{:S(2)}, u32[]{:S(2)}) collective-permute-start(bf16[8,128,256]{2,1,0:T(8,128)(2,1)S(1)} %all-to-all-done.rest_0_.rest_1_), channel_id=1, source_target_pairs={{0,8},{4,12},{8,0},{12,4},{16,24},{20,28},{24,16},{28,20},{32,40},... | collective-permute-start | bytes 1572872 | tf_op jit(solution)/shard_map/ppermute | solution.py:321
  30.6 1.8 %collective-permute-start.3 = (bf16[8,128,256]{2,1,0:T(8,128)(2,1)S(1)}, bf16[8,128,256]{2,1,0:T(8,128)(2,1)}, u32[]{:S(2)}, u32[]{:S(2)}) collective-permute-start(bf16[8,128,256]{2,1,0:T(8,128)(2,1)S(1)} %all-to-all-done.rest_0_.rest_1_), channel_id=1, source_target_pairs={{0,24},{4,28},{8,16},{12,20},{16,8},{20,12},{24,0},{28,4},{32,56},... | collective-permute-start | bytes 1572872 | tf_op jit(solution)/shard_map/ppermute | solution.py:321
  33.4 3.9 %all-to-all-start.1 = ((f32[32,8,640]{2,1,0:T(8,128)}), f32[32,8,640]{2,1,0:T(8,128)S(1)}, u32[]{:S(2)}, u32[]{:S(2)}) async-start(f32[32,8,640]{2,1,0:T(8,128)} %chip_state.1), calls=%async_computation.1 | async-start | bytes 1310720 | tf_op jit(solution)/shard_map/all_to_all | solution.py:360
  37.3 5.6 %collective-permute-done.1.rest_0_.rest_1_ = bf16[8,128,256]{2,1,0:T(8,128)(2,1)S(1)} collective-permute-done((bf16[8,128,256]{2,1,0:T(8,128)(2,1)S(1)}, bf16[8,128,256]{2,1,0:T(8,128)(2,1)S(1)}, u32[]{:S(2)}, u32[]{:S(2)}) %collective-permute-start.1) | collective-permute-done | bytes 524320 | tf_op jit(solution)/shard_map/ppermute | solution.py:321
  43.0 2.8 %collective-permute-start.2 = (bf16[8,128,128]{2,1,0:T(8,128)(2,1)S(1)}, bf16[8,128,128]{2,1,0:T(8,128)(2,1)}, u32[]{:S(2)}, u32[]{:S(2)}) collective-permute-start(bf16[8,128,128]{2,1,0:T(8,128)(2,1)S(1)} %slice.8), channel_id=1, source_target_pairs={{0,24},{4,28},{8,16},{12,20},{16,8},{20,12},{24,0},{28,4},{32,56},... | collective-permute-start | bytes 786440 | tf_op jit(solution)/shard_map/ppermute | solution.py:321
  47.4 5.0 %collective-permute-start.7 = (bf16[8,128,256]{2,1,0:T(8,128)(2,1)S(1)}, bf16[8,128,256]{2,1,0:T(8,128)(2,1)}, u32[]{:S(2)}, u32[]{:S(2)}) collective-permute-start(bf16[8,128,256]{2,1,0:T(8,128)(2,1)S(1)} %collective-permute-done.1.rest_0_.rest_1_), channel_id=1, source_target_pairs={{0,4},{4,0},{8,12},{12,8},{16,20},{20,16},{24,28},{28,24},{32,36},... | collective-permute-start | bytes 1572872 | tf_op jit(solution)/shard_map/ppermute | solution.py:321
  52.5 2.6 %attention_near.1.rest_8_ = f32[3,640,128]{2,1,0:T(8,128)S(1)} custom-call(s32[1,128]{1,0:T(1,128)S(1)} %bitcast.12, bf16[128,640]{1,0:T(8,128)(2,1)S(1)} %copy-done.9, s32[1,128]{1,0:T(1,128)S(1)} %bitcast.13, bf16[8,128,256]{2,1,0:T(8,128)(2,1)S(1)} %all-to-all-done.rest_0_.rest_1_, bf16[8,128,256]{2,1,0:T(8,128)(2,1)S(1)} %all-to-all-done.rest_0_.rest_1_, ...), custom_call_target="tpu_custom_call" | custom-call | flops 8999999488 | tf_op jit(solution)/shard_map/attention_near/pallas_call | solution.py:346
  56.5 2.4 %collective-permute-start.5 = (bf16[8,128,128]{2,1,0:T(8,128)(2,1)}, bf16[8,128,128]{2,1,0:T(8,128)(2,1)S(1)}, u32[]{:S(2)}, u32[]{:S(2)}) collective-permute-start(bf16[8,128,128]{2,1,0:T(8,128)(2,1)} %collective-permute-done.2.rest_0_), channel_id=1, source_target_pairs={{0,4},{4,0},{8,12},{12,8},{16,20},{20,16},{24,28},{28,24},{32,36},... | collective-permute-start | bytes 786440 | tf_op jit(solution)/shard_map/ppermute | solution.py:321
  59.7 5.5 %all-to-all-start.2 = ((f32[32,8,512]{2,1,0:T(8,128)}), f32[32,8,512]{2,1,0:T(8,128)S(1)}, u32[]{:S(2)}, u32[]{:S(2)}) async-start(f32[32,8,512]{2,1,0:T(8,128)} %prefix.1), calls=%async_computation.2 | async-start | bytes 1048576 | tf_op jit(solution)/shard_map/all_to_all | solution.py:367
  66.2 1.2 %copy-done.12 = f32[3,640,128]{2,1,0:T(8,128)S(1)} copy-done((f32[3,640,128]{2,1,0:T(8,128)S(1)}, f32[3,640,128]{2,1,0:T(8,128)}, u32[]{:S(2)}) %copy-start.12) | copy-done | bytes 983064
  67.4 3.4 %attention_sides.1.rest_4_ = f32[3,640,128]{2,1,0:T(8,128)S(1)} custom-call(s32[1,128]{1,0:T(1,128)S(1)} %bitcast.14, bf16[128,640]{1,0:T(8,128)(2,1)S(1)} %copy-done.10, s32[1,128]{1,0:T(1,128)S(1)} %bitcast.15, bf16[8,128,256]{2,1,0:T(8,128)(2,1)S(1)} %collective-permute-done.1.rest_0_.rest_1_, ...), custom_call_target="tpu_custom_call" | custom-call | flops 10000000000 | tf_op jit(solution)/shard_map/attention_sides/pallas_call | solution.py:346
  70.8 3.2 %attention_far.1 = (bf16[128,640]{1,0:T(8,128)(2,1)}, f32[16,128]{1,0:T(8,128)S(1)}) custom-call(s32[1,128]{1,0:T(1,128)S(1)} %bitcast.16, bf16[128,640]{1,0:T(8,128)(2,1)S(1)} %copy-done.10, s32[1,128]{1,0:T(1,128)S(1)} %bitcast.17, bf16[8,128,128]{2,1,0:T(8,128)(2,1)} %collective-permute-done.2.rest_0_, ...), custom_call_target="tpu_custom_call" | custom-call | flops 10000000000 | tf_op jit(solution)/shard_map/attention_far/pallas_call | solution.py:346
  74.0 8.0 %all-to-all-done.2.pre_ref = f32[32,8,512]{2,1,0:T(8,128)S(1)} async-done(((f32[32,8,512]{2,1,0:T(8,128)}), f32[32,8,512]{2,1,0:T(8,128)S(1)}, u32[]{:S(2)}, u32[]{:S(2)}) %all-to-all-start.2) | async-done | bytes 524320 | tf_op jit(solution)/shard_map/all_to_all | solution.py:367
  82.2 2.0 %collective-permute-start.10 = (f32[256,512]{1,0:T(8,128)S(1)}, f32[256,512]{1,0:T(8,128)S(1)}, u32[]{:S(2)}, u32[]{:S(2)}) collective-permute-start(f32[256,512]{1,0:T(8,128)S(1)} %get-tuple-element.36), channel_id=1, source_target_pairs={{0,4},{4,0},{8,12},{12,8},{16,20},{20,16},{24,28},{28,24},{32,36},... | collective-permute-start | bytes 1572872 | tf_op jit(solution)/shard_map/ppermute | solution.py:321
  84.1 1.5 %collective-permute-done.10.got_ref = f32[256,512]{1,0:T(8,128)S(1)} collective-permute-done((f32[256,512]{1,0:T(8,128)S(1)}, f32[256,512]{1,0:T(8,128)S(1)}, u32[]{:S(2)}, u32[]{:S(2)}) %collective-permute-start.10) | collective-permute-done | bytes 524320 | tf_op jit(solution)/shard_map/ppermute | solution.py:321
  86.7 1.3 %collective-permute-start.11 = (f32[8,128]{1,0:T(8,128)S(1)}, f32[8,128]{1,0:T(8,128)S(1)}, u32[]{:S(2)}, u32[]{:S(2)}) collective-permute-start(f32[8,128]{1,0:T(8,128)S(1)} %get-tuple-element.38.s0), channel_id=1, source_target_pairs={{0,1},{1,0},{2,3},{3,2},{4,5},{5,4},{6,7},{7,6},{8,9},{9,8},{10,11... | collective-permute-start | bytes 12296 | tf_op jit(solution)/shard_map/ppermute | solution.py:378
  88.0 2.6 %collective-permute-start.12 = (f32[8,128]{1,0:T(8,128)S(1)}, f32[8,128]{1,0:T(8,128)S(1)}, u32[]{:S(2)}, u32[]{:S(2)}) collective-permute-start(f32[8,128]{1,0:T(8,128)S(1)} %get-tuple-element.38.s0), channel_id=1, source_target_pairs={{0,2},{1,3},{2,0},{3,1},{4,6},{5,7},{6,4},{7,5},{8,10},{9,11},{10,... | collective-permute-start | bytes 12296 | tf_op jit(solution)/shard_map/ppermute | solution.py:378
  90.6 1.3 %collective-permute-done.12.s2 = f32[8,128]{1,0:T(8,128)S(1)} collective-permute-done((f32[8,128]{1,0:T(8,128)S(1)}, f32[8,128]{1,0:T(8,128)S(1)}, u32[]{:S(2)}, u32[]{:S(2)}) %collective-permute-start.12) | collective-permute-done | bytes 4128 | tf_op jit(solution)/shard_map/ppermute | solution.py:378
  92.0 2.3 %collective-permute-done.13.s3 = f32[8,128]{1,0:T(8,128)S(1)} collective-permute-done((f32[8,128]{1,0:T(8,128)S(1)}, f32[8,128]{1,0:T(8,128)S(1)}, u32[]{:S(2)}, u32[]{:S(2)}) %collective-permute-start.13) | collective-permute-done | bytes 4128 | tf_op jit(solution)/shard_map/ppermute | solution.py:378
  95.2 2.1 %collective-permute-start.14 = (bf16[32,128]{1,0:T(8,128)(2,1)S(1)}, bf16[32,128]{1,0:T(8,128)(2,1)S(1)}, u32[]{:S(2)}, u32[]{:S(2)}) collective-permute-start(bf16[32,128]{1,0:T(8,128)(2,1)S(1)} %get-tuple-element.41.own_ref), channel_id=1, source_target_pairs={{0,4},{4,0},{8,12},{12,8},{16,20},{20,16},{24,28},{28,24},{32,36},... | collective-permute-start | bytes 24584 | tf_op jit(solution)/shard_map/ppermute | solution.py:321
  98.1 15.8 %all_to_all.20.in_ref = bf16[32,32,128]{2,1,0:T(8,128)(2,1)S(1)} all-to-all(bf16[32,32,128]{2,1,0:T(8,128)(2,1)S(1)} %least.1), channel_id=1, replica_groups={{0,8,16,24,32,40,48,56,64,72,80,88,96,104,112,120,128,136,144,152,160,1..., dimensions={0} | all-to-all | bytes 524288 | tf_op jit(solution)/shard_map/all_to_all | solution.py:386
  (55 shorter events, 15.4 us)
Async XLA Ops:
  2.2 9.2 %copy-start = (bf16[128,1024]{1,0:T(8,128)(2,1)S(1)}, bf16[128,1024]{1,0:T(8,128)(2,1)}, u32[]{:S(2)}) copy-start(bf16[128,1024]{1,0:T(8,128)(2,1)} %x_ref.3) | copy-start | bytes 786436
  2.3 9.2 %copy-start.3 = (bf16[128,256]{1,0:T(8,128)(2,1)S(1)}, bf16[128,256]{1,0:T(8,128)(2,1)}, u32[]{:S(2)}) copy-start(bf16[128,256]{1,0:T(8,128)(2,1)} %b_ref.3) | copy-start | bytes 196612
  2.3 9.2 %copy-start.4 = (f32[128,16]{0,1:T(8,128)S(1)}, f32[128,16]{0,1:T(8,128)}, u32[]{:S(2)}) copy-start(f32[128,16]{0,1:T(8,128)} %param.19) | copy-start | bytes 24580
  2.3 27.1 %all-to-all-start = ((bf16[8,128,256]{2,1,0:T(8,128)(2,1)}), bf16[8,128,256]{2,1,0:T(8,128)(2,1)S(1)}, u32[]{:S(2)}, u32[]{:S(2)}) async-start(bf16[8,128,256]{2,1,0:T(8,128)(2,1)} %broadcast_in_dim.19), calls=%async_computation | async-start | bytes 1048576 | tf_op jit(solution)/shard_map/all_to_all | solution.py:333
  14.4 2.6 %collective-permute-start = (f32[264,512]{1,0:T(8,128)S(1)}, f32[264,512]{1,0:T(8,128)S(1)}, u32[]{:S(2)}, u32[]{:S(2)}) collective-permute-start(f32[264,512]{1,0:T(8,128)S(1)} %get-tuple-element.25), channel_id=1, source_target_pairs={{0,4},{4,0},{8,12},{12,8},{16,20},{20,16},{24,28},{28,24},{32,36},... | collective-permute-start | bytes 1622024 | tf_op jit(solution)/shard_map/ppermute | solution.py:321
  29.4 13.5 %collective-permute-start.1 = (bf16[8,128,256]{2,1,0:T(8,128)(2,1)S(1)}, bf16[8,128,256]{2,1,0:T(8,128)(2,1)S(1)}, u32[]{:S(2)}, u32[]{:S(2)}) collective-permute-start(bf16[8,128,256]{2,1,0:T(8,128)(2,1)S(1)} %all-to-all-done.rest_0_.rest_1_), channel_id=1, source_target_pairs={{0,8},{4,12},{8,0},{12,4},{16,24},{20,28},{24,16},{28,20},{32,40},... | collective-permute-start | bytes 1572872 | tf_op jit(solution)/shard_map/ppermute | solution.py:321
  30.6 15.7 %collective-permute-start.3 = (bf16[8,128,256]{2,1,0:T(8,128)(2,1)S(1)}, bf16[8,128,256]{2,1,0:T(8,128)(2,1)}, u32[]{:S(2)}, u32[]{:S(2)}) collective-permute-start(bf16[8,128,256]{2,1,0:T(8,128)(2,1)S(1)} %all-to-all-done.rest_0_.rest_1_), channel_id=1, source_target_pairs={{0,24},{4,28},{8,16},{12,20},{16,8},{20,12},{24,0},{28,4},{32,56},... | collective-permute-start | bytes 1572872 | tf_op jit(solution)/shard_map/ppermute | solution.py:321
  32.4 20.1 %collective-permute-start.9 = (bf16[8,128,256]{2,1,0:T(8,128)(2,1)S(1)}, bf16[8,128,256]{2,1,0:T(8,128)(2,1)}, u32[]{:S(2)}, u32[]{:S(2)}) collective-permute-start(bf16[8,128,256]{2,1,0:T(8,128)(2,1)S(1)} %all-to-all-done.rest_0_.rest_1_), channel_id=1, source_target_pairs={{0,4},{4,0},{8,12},{12,8},{16,20},{20,16},{24,28},{28,24},{32,36},... | collective-permute-start | bytes 1572872 | tf_op jit(solution)/shard_map/ppermute | solution.py:321
  33.4 25.4 %all-to-all-start.1 = ((f32[32,8,640]{2,1,0:T(8,128)}), f32[32,8,640]{2,1,0:T(8,128)S(1)}, u32[]{:S(2)}, u32[]{:S(2)}) async-start(f32[32,8,640]{2,1,0:T(8,128)} %chip_state.1), calls=%async_computation.1 | async-start | bytes 1310720 | tf_op jit(solution)/shard_map/all_to_all | solution.py:360
  43.0 9.5 %copy-start.9 = (bf16[128,640]{1,0:T(8,128)(2,1)S(1)}, bf16[128,640]{1,0:T(8,128)(2,1)}, u32[]{:S(2)}) copy-start(bf16[128,640]{1,0:T(8,128)(2,1)} %q_ref.5) | copy-start | bytes 491524
  43.0 13.5 %collective-permute-start.2 = (bf16[8,128,128]{2,1,0:T(8,128)(2,1)S(1)}, bf16[8,128,128]{2,1,0:T(8,128)(2,1)}, u32[]{:S(2)}, u32[]{:S(2)}) collective-permute-start(bf16[8,128,128]{2,1,0:T(8,128)(2,1)S(1)} %slice.8), channel_id=1, source_target_pairs={{0,24},{4,28},{8,16},{12,20},{16,8},{20,12},{24,0},{28,4},{32,56},... | collective-permute-start | bytes 786440 | tf_op jit(solution)/shard_map/ppermute | solution.py:321
  47.3 11.6 %collective-permute-start.4 = (bf16[8,128,128]{2,1,0:T(8,128)(2,1)S(1)}, bf16[8,128,128]{2,1,0:T(8,128)(2,1)}, u32[]{:S(2)}, u32[]{:S(2)}) collective-permute-start(bf16[8,128,128]{2,1,0:T(8,128)(2,1)S(1)} %slice.9), channel_id=1, source_target_pairs={{0,8},{4,12},{8,0},{12,4},{16,24},{20,28},{24,16},{28,20},{32,40},... | collective-permute-start | bytes 786440 | tf_op jit(solution)/shard_map/ppermute | solution.py:321
  47.4 17.9 %collective-permute-start.7 = (bf16[8,128,256]{2,1,0:T(8,128)(2,1)S(1)}, bf16[8,128,256]{2,1,0:T(8,128)(2,1)}, u32[]{:S(2)}, u32[]{:S(2)}) collective-permute-start(bf16[8,128,256]{2,1,0:T(8,128)(2,1)S(1)} %collective-permute-done.1.rest_0_.rest_1_), channel_id=1, source_target_pairs={{0,4},{4,0},{8,12},{12,8},{16,20},{20,16},{24,28},{28,24},{32,36},... | collective-permute-start | bytes 1572872 | tf_op jit(solution)/shard_map/ppermute | solution.py:321
  52.4 12.9 %collective-permute-start.8 = (bf16[8,128,256]{2,1,0:T(8,128)(2,1)}, bf16[8,128,256]{2,1,0:T(8,128)(2,1)}, u32[]{:S(2)}, u32[]{:S(2)}) collective-permute-start(bf16[8,128,256]{2,1,0:T(8,128)(2,1)} %collective-permute-done.3.rest_4_.rest_5_), channel_id=1, source_target_pairs={{0,4},{4,0},{8,12},{12,8},{16,20},{20,16},{24,28},{28,24},{32,36},... | collective-permute-start | bytes 1572872 | tf_op jit(solution)/shard_map/ppermute | solution.py:321
  56.5 14.3 %collective-permute-start.5 = (bf16[8,128,128]{2,1,0:T(8,128)(2,1)}, bf16[8,128,128]{2,1,0:T(8,128)(2,1)S(1)}, u32[]{:S(2)}, u32[]{:S(2)}) collective-permute-start(bf16[8,128,128]{2,1,0:T(8,128)(2,1)} %collective-permute-done.2.rest_0_), channel_id=1, source_target_pairs={{0,4},{4,0},{8,12},{12,8},{16,20},{20,16},{24,28},{28,24},{32,36},... | collective-permute-start | bytes 786440 | tf_op jit(solution)/shard_map/ppermute | solution.py:321
  58.9 11.9 %collective-permute-start.6 = (bf16[8,128,128]{2,1,0:T(8,128)(2,1)}, bf16[8,128,128]{2,1,0:T(8,128)(2,1)S(1)}, u32[]{:S(2)}, u32[]{:S(2)}) collective-permute-start(bf16[8,128,128]{2,1,0:T(8,128)(2,1)} %collective-permute-done.4.rest_1_), channel_id=1, source_target_pairs={{0,4},{4,0},{8,12},{12,8},{16,20},{20,16},{24,28},{28,24},{32,36},... | collective-permute-start | bytes 786440 | tf_op jit(solution)/shard_map/ppermute | solution.py:321
  59.7 22.3 %all-to-all-start.2 = ((f32[32,8,512]{2,1,0:T(8,128)}), f32[32,8,512]{2,1,0:T(8,128)S(1)}, u32[]{:S(2)}, u32[]{:S(2)}) async-start(f32[32,8,512]{2,1,0:T(8,128)} %prefix.1), calls=%async_computation.2 | async-start | bytes 1048576 | tf_op jit(solution)/shard_map/all_to_all | solution.py:367
  82.0 3.6 %copy-start.1 = (bf16[128,1024]{1,0:T(8,128)(2,1)S(1)}, bf16[128,1024]{1,0:T(8,128)(2,1)}, u32[]{:S(2)}) copy-start(bf16[128,1024]{1,0:T(8,128)(2,1)} %z_ref.1) | copy-start | bytes 786436
  82.2 3.5 %collective-permute-start.10 = (f32[256,512]{1,0:T(8,128)S(1)}, f32[256,512]{1,0:T(8,128)S(1)}, u32[]{:S(2)}, u32[]{:S(2)}) collective-permute-start(f32[256,512]{1,0:T(8,128)S(1)} %get-tuple-element.36), channel_id=1, source_target_pairs={{0,4},{4,0},{8,12},{12,8},{16,20},{20,16},{24,28},{28,24},{32,36},... | collective-permute-start | bytes 1572872 | tf_op jit(solution)/shard_map/ppermute | solution.py:321
  86.7 7.6 %copy-start.5 = (f32[1024]{0:T(1024)S(1)}, f32[1024]{0:T(1024)}, u32[]{:S(2)}) copy-start(f32[1024]{0:T(1024)} %param.22) | copy-start | bytes 12292
  86.7 4.0 %collective-permute-start.11 = (f32[8,128]{1,0:T(8,128)S(1)}, f32[8,128]{1,0:T(8,128)S(1)}, u32[]{:S(2)}, u32[]{:S(2)}) collective-permute-start(f32[8,128]{1,0:T(8,128)S(1)} %get-tuple-element.38.s0), channel_id=1, source_target_pairs={{0,1},{1,0},{2,3},{3,2},{4,5},{5,4},{6,7},{7,6},{8,9},{9,8},{10,11... | collective-permute-start | bytes 12296 | tf_op jit(solution)/shard_map/ppermute | solution.py:378
  88.0 4.0 %collective-permute-start.12 = (f32[8,128]{1,0:T(8,128)S(1)}, f32[8,128]{1,0:T(8,128)S(1)}, u32[]{:S(2)}, u32[]{:S(2)}) collective-permute-start(f32[8,128]{1,0:T(8,128)S(1)} %get-tuple-element.38.s0), channel_id=1, source_target_pairs={{0,2},{1,3},{2,0},{3,1},{4,6},{5,7},{6,4},{7,5},{8,10},{9,11},{10,... | collective-permute-start | bytes 12296 | tf_op jit(solution)/shard_map/ppermute | solution.py:378
  90.6 3.7 %collective-permute-start.13 = (f32[8,128]{1,0:T(8,128)S(1)}, f32[8,128]{1,0:T(8,128)S(1)}, u32[]{:S(2)}, u32[]{:S(2)}) collective-permute-start(f32[8,128]{1,0:T(8,128)S(1)} %get-tuple-element.38.s0), channel_id=1, source_target_pairs={{0,3},{1,2},{2,1},{3,0},{4,7},{5,6},{6,5},{7,4},{8,11},{9,10},{10,... | collective-permute-start | bytes 12296 | tf_op jit(solution)/shard_map/ppermute | solution.py:378
  95.2 2.9 %collective-permute-start.14 = (bf16[32,128]{1,0:T(8,128)(2,1)S(1)}, bf16[32,128]{1,0:T(8,128)(2,1)S(1)}, u32[]{:S(2)}, u32[]{:S(2)}) collective-permute-start(bf16[32,128]{1,0:T(8,128)(2,1)S(1)} %get-tuple-element.41.own_ref), channel_id=1, source_target_pairs={{0,4},{4,0},{8,12},{12,8},{16,20},{20,16},{24,28},{28,24},{32,36},... | collective-permute-start | bytes 24584 | tf_op jit(solution)/shard_map/ppermute | solution.py:321
  (7 other events, 8.8 us)

commit v5 on v4

--- a/solution.py
+++ b/solution.py
@@ -87,14 +87,17 @@
         out[NS : NS + 8, :] = wide[TOK:]
 
 
-def intra_kernel(x_ref, b_ref, c_ref, dt_ref, a_ref, skip_ref, doc_ref, y_ref, enter_ref):
+def intra_kernel(x_ref, b_ref, c_ref, dt_ref, a_ref, skip_ref, doc_ref, z_ref, y_ref, enter_ref, gate_ref):
     begin = lax.axis_index("seq") * TOK
     step_t, running_t, _, running = step_sizes(dt_ref, a_ref)
     rows, cols = iota((TOK, TOK), 0), iota((TOK, TOK), 1)
     doc = jnp.transpose(jnp.broadcast_to(doc_ref[...], (TOK, TOK)).astype(F32)).astype(jnp.int32)
     same_doc = (cols <= rows) & (begin + cols >= doc)
     earlier = same_doc & (cols < rows)
-    enter_ref[...] = jnp.where(doc[:, :HEADS] < begin, jnp.exp(running), 0.0)
+    enter = jnp.where(doc[:, :HEADS] < begin, jnp.exp(running), 0.0)
+    enter_ref[...] = mm(enter, spread_heads(0, COLS), precision=HIGH)
+    gate = z_ref[...].astype(F32)
+    gate_ref[...] = gate / (1.0 + jnp.exp(-gate))
     inner = jnp.where(same_doc, mm(c_ref[...], b_ref[...], ((1,), (1,))), 0.0)
     skip = mm(
         jnp.broadcast_to(skip_ref[...], (8, HEADS)), spread_heads(0, COLS), precision=HIGH
@@ -149,15 +152,13 @@
         send_ref[rows, :] = jnp.where(first, after, before)
 
 
-def mix_kernel(y_ref, enter_ref, c_ref, z_ref, mine_ref, got_ref, gated_ref, sq_ref):
+def mix_kernel(y_ref, enter_ref, c_ref, gate_ref, mine_ref, got_ref, gated_ref, sq_ref):
     core = lax.axis_index("seq") % 2
     squares = jnp.zeros((TOK, 128), F32)
     for half, state in ((core, mine_ref), (1 - core, got_ref)):
         at = pl.ds(pl.multiple_of(half * HALF, HALF), HALF)
-        wide = mm(enter_ref[...], spread_heads(half * HALF_HEADS, HALF), precision=HIGH)
-        mixed = y_ref[:, at] + split_mm(c_ref[...], state[...], which=1) * wide
-        gate = z_ref[:, at].astype(F32)
-        gated = mixed * (gate / (1.0 + jnp.exp(-gate)))
+        mixed = y_ref[:, at] + split_mm(c_ref[...], state[...], which=1) * enter_ref[:, at]
+        gated = mixed * gate_ref[:, at]
         gated_ref[:, at] = gated
         power = gated * gated
         for tile in range(HALF // 128):
@@ -352,9 +353,9 @@
         local_kernel, [((NS + 8, HALF), F32)] * 2, [SMEM] + [VMEM] * 4, "local_state"
     )(doc_row, x_in, b_in, dt_t, a_row)
     got = swap(send, 1)
-    y_part, enter = call(
-        intra_kernel, [((TOK, COLS), F32), ((TOK, HEADS), F32)], [VMEM] * 7, "intra"
-    )(x_in, b_in, c_in, dt_t, a_row, skip_row, doc_row)
+    y_part, enter, gate = call(
+        intra_kernel, [((TOK, COLS), F32)] * 3, [VMEM] * 8, "intra"
+    )(x_in, b_in, c_in, dt_t, a_row, skip_row, doc_row, z_in)
     (chunks,) = call(chip_kernel, [((CHIPS, 8, HALF + 128), F32)], [VMEM] * 2, "chip_state")(keep, got)
     near, chunks, y_part = lax.optimization_barrier((near, chunks, y_part))
     chunks = lax.all_to_all(chunks, "seq", 0, 0, tiled=True, axis_index_groups=same_core)
@@ -372,7 +373,7 @@
     )
     got_state = swap(theirs, 1)
     gated, square = call(mix_kernel, [((TOK, COLS), F32), ((8, TOK), F32)], [VMEM] * 6, "mix")(
-        y_part, enter, c_in, z_in, mine, got_state
+        y_part, enter, c_in, gate, mine, got_state
     )
     squares = [square] + [
         lax.ppermute(square, "head", [(i, i ^ bit) for i in range(4)]) for bit in (1, 2, 3)

time: 115 us -> 115 us (level)
  waiting for transfers between devices: 32.5 us -> 31.2 us
    ppermute x12, waiting for transfers between devices: 9.35 us -> 7.95 us  [swap(): return lax.ppermute(value, 'seq', [(i, i ^ bit) for i in range(count)])]
    unnamed x26 -> x28, local copies, waits for them, and re-layouts: 3.74 us -> 2.98 us
  transfers between devices with their start and end apart: 18 -> 18, of which waited for: 10 -> 7; matrix products, arithmetic and copies ran while one was open for 1% -> 2% of each run, Pallas kernels for 13% -> 13%
where the time goes in v5:
time: 115 us; the launch traced here: 114 us
  starting transfers between devices  42.1 us (37%)
  waiting for transfers between devices  31.2 us (27%)
  Pallas kernels  17.7 us (15%)
  blocking collectives  15.8 us (14%)
  local copies, waits for them, and re-layouts  5.73 us (5%)
    ppermute x12, starting transfers between devices, swap(): return lax.ppermute(value, 'seq', [(i, i ^ bit) for i in range(count)])  19.7 us
    all_to_all x1, blocking collectives, body(): lax.all_to_all(rng, 'seq', 0, 0, tiled=True, axis_index_groups=same_core)  15.8 us
    all_to_all x1, waiting for transfers between devices, body(): lax.all_to_all(near, 'seq', 0, 0, tiled=True, axis_index_groups=column)  11.1 us
    pallas_call x3, Pallas kernels, attend(): call(functools.partial(attn_kernel, flips, span, first, final), outs, [SM...  9.64 us
    all_to_all x1, starting transfers between devices, body(): lax.all_to_all(near, 'seq', 0, 0, tiled=True, axis_index_groups=column)  9.16 us
    all_to_all x1, waiting for transfers between devices, body(): lax.all_to_all(prefix, 'seq', 0, 0, tiled=True, axis_index_groups=same_core)  8.52 us
    ppermute x12, waiting for transfers between devices, swap(): return lax.ppermute(value, 'seq', [(i, i ^ bit) for i in range(count)])  7.95 us
    all_to_all x1, starting transfers between devices, body(): lax.all_to_all(prefix, 'seq', 0, 0, tiled=True, axis_index_groups=same_core)  5.38 us
  transfers between devices with their start and end apart: 18, of which 7 were waited for; matrix products, arithmetic and copies ran while one was open for 2% of the time, Pallas kernels for 13%

profile of v5, /device:TPU:1, one launch (start us, length us, event | category | flops | bytes accessed | tf_op | source)
XLA Modules:
  0.0 114.2 jit_solution(15102830032300511250)
XLA Ops:
  2.3 9.2 %all-to-all-start = ((bf16[8,128,256]{2,1,0:T(8,128)(2,1)}), bf16[8,128,256]{2,1,0:T(8,128)(2,1)S(1)}, u32[]{:S(2)}, u32[]{:S(2)}) async-start(bf16[8,128,256]{2,1,0:T(8,128)(2,1)} %broadcast_in_dim.19), calls=%async_computation | async-start | bytes 1048576 | tf_op jit(solution)/shard_map/all_to_all | solution.py:334
  11.5 2.3 %local_state.1 = (f32[264,512]{1,0:T(8,128)S(1)}, f32[264,512]{1,0:T(8,128)S(1)}) custom-call(s32[1,128]{1,0:T(1,128)S(1)} %bitcast.10, bf16[128,1024]{1,0:T(8,128)(2,1)S(1)} %copy-done, bf16[128,256]{1,0:T(8,128)(2,1)S(1)} %copy-done.4, f32[16,128]{1,0:T(8,128)S(1)} %bitcast.5, f32[1,16]{1,0:T(1,128)S(1)} %bitcast.8), custom_call_target="tpu_custom_call" | custom-call | tf_op jit(solution)/shard_map/local_state/pallas_call | solution.py:352
  14.8 1.7 %intra.1 = (f32[128,1024]{1,0:T(8,128)S(1)}, f32[128,1024]{1,0:T(8,128)S(1)}, f32[128,1024]{1,0:T(8,128)S(1)}) custom-call(bf16[128,1024]{1,0:T(8,128)(2,1)S(1)} %copy-done, bf16[128,256]{1,0:T(8,128)(2,1)S(1)} %copy-done.4, bf16[128,256]{1,0:T(8,128)(2,1)S(1)} %copy-done.5, f32[16,128]{1,0:T(8,128)S(1)} %bitcast.6, f32[1,16]{1,0:T(1,128)S(1)} %bitcast.9, ...), custom_call_target="tpu_custom_call" | custom-call | tf_op jit(solution)/shard_map/intra/pallas_call | solution.py:356
  18.2 11.1 %all-to-all-done.rest_0_.rest_1_ = bf16[8,128,256]{2,1,0:T(8,128)(2,1)S(1)} async-done(((bf16[8,128,256]{2,1,0:T(8,128)(2,1)}), bf16[8,128,256]{2,1,0:T(8,128)(2,1)S(1)}, u32[]{:S(2)}, u32[]{:S(2)}) %all-to-all-start) | async-done | bytes 524320 | tf_op jit(solution)/shard_map/all_to_all | solution.py:334
  29.4 1.2 %collective-permute-start.1 = (bf16[8,128,256]{2,1,0:T(8,128)(2,1)S(1)}, bf16[8,128,256]{2,1,0:T(8,128)(2,1)}, u32[]{:S(2)}, u32[]{:S(2)}) collective-permute-start(bf16[8,128,256]{2,1,0:T(8,128)(2,1)S(1)} %all-to-all-done.rest_0_.rest_1_), channel_id=1, source_target_pairs={{0,8},{4,12},{8,0},{12,4},{16,24},{20,28},{24,16},{28,20},{32,40},... | collective-permute-start | bytes 1572872 | tf_op jit(solution)/shard_map/ppermute | solution.py:322
  30.6 1.8 %collective-permute-start.3 = (bf16[8,128,256]{2,1,0:T(8,128)(2,1)S(1)}, bf16[8,128,256]{2,1,0:T(8,128)(2,1)}, u32[]{:S(2)}, u32[]{:S(2)}) collective-permute-start(bf16[8,128,256]{2,1,0:T(8,128)(2,1)S(1)} %all-to-all-done.rest_0_.rest_1_), channel_id=1, source_target_pairs={{0,24},{4,28},{8,16},{12,20},{16,8},{20,12},{24,0},{28,4},{32,56},... | collective-permute-start | bytes 1572872 | tf_op jit(solution)/shard_map/ppermute | solution.py:322
  33.5 3.9 %all-to-all-start.1 = ((f32[32,8,640]{2,1,0:T(8,128)}), f32[32,8,640]{2,1,0:T(8,128)S(1)}, u32[]{:S(2)}, u32[]{:S(2)}) async-start(f32[32,8,640]{2,1,0:T(8,128)} %chip_state.1), calls=%async_computation.1 | async-start | bytes 1310720 | tf_op jit(solution)/shard_map/all_to_all | solution.py:361
  37.4 5.6 %collective-permute-done.1.rest_0_.rest_1_ = bf16[8,128,256]{2,1,0:T(8,128)(2,1)} collective-permute-done((bf16[8,128,256]{2,1,0:T(8,128)(2,1)S(1)}, bf16[8,128,256]{2,1,0:T(8,128)(2,1)}, u32[]{:S(2)}, u32[]{:S(2)}) %collective-permute-start.1) | collective-permute-done | bytes 524320 | tf_op jit(solution)/shard_map/ppermute | solution.py:322
  43.9 2.8 %collective-permute-start.2 = (bf16[8,128,128]{2,1,0:T(8,128)(2,1)S(1)}, bf16[8,128,128]{2,1,0:T(8,128)(2,1)}, u32[]{:S(2)}, u32[]{:S(2)}) collective-permute-start(bf16[8,128,128]{2,1,0:T(8,128)(2,1)S(1)} %slice.8), channel_id=1, source_target_pairs={{0,24},{4,28},{8,16},{12,20},{16,8},{20,12},{24,0},{28,4},{32,56},... | collective-permute-start | bytes 786440 | tf_op jit(solution)/shard_map/ppermute | solution.py:322
  47.8 4.6 %collective-permute-start.7 = (bf16[8,128,256]{2,1,0:T(8,128)(2,1)}, bf16[8,128,256]{2,1,0:T(8,128)(2,1)}, u32[]{:S(2)}, u32[]{:S(2)}) collective-permute-start(bf16[8,128,256]{2,1,0:T(8,128)(2,1)} %collective-permute-done.1.rest_0_.rest_1_), channel_id=1, source_target_pairs={{0,4},{4,0},{8,12},{12,8},{16,20},{20,16},{24,28},{28,24},{32,36},... | collective-permute-start | bytes 1572872 | tf_op jit(solution)/shard_map/ppermute | solution.py:322
  52.5 2.6 %attention_near.1.rest_8_ = f32[3,640,128]{2,1,0:T(8,128)S(1)} custom-call(s32[1,128]{1,0:T(1,128)S(1)} %bitcast.12, bf16[128,640]{1,0:T(8,128)(2,1)S(1)} %copy-done.11, s32[1,128]{1,0:T(1,128)S(1)} %bitcast.13, bf16[8,128,256]{2,1,0:T(8,128)(2,1)S(1)} %all-to-all-done.rest_0_.rest_1_, bf16[8,128,256]{2,1,0:T(8,128)(2,1)S(1)} %all-to-all-done.rest_0_.rest_1_, ...), custom_call_target="tpu_custom_call" | custom-call | flops 8999999488 | tf_op jit(solution)/shard_map/attention_near/pallas_call | solution.py:347
  56.0 2.8 %collective-permute-start.5 = (bf16[8,128,128]{2,1,0:T(8,128)(2,1)}, bf16[8,128,128]{2,1,0:T(8,128)(2,1)S(1)}, u32[]{:S(2)}, u32[]{:S(2)}) collective-permute-start(bf16[8,128,128]{2,1,0:T(8,128)(2,1)} %collective-permute-done.2.rest_0_), channel_id=1, source_target_pairs={{0,4},{4,0},{8,12},{12,8},{16,20},{20,16},{24,28},{28,24},{32,36},... | collective-permute-start | bytes 786440 | tf_op jit(solution)/shard_map/ppermute | solution.py:322
  59.9 5.4 %all-to-all-start.2 = ((f32[32,8,512]{2,1,0:T(8,128)}), f32[32,8,512]{2,1,0:T(8,128)S(1)}, u32[]{:S(2)}, u32[]{:S(2)}) async-start(f32[32,8,512]{2,1,0:T(8,128)} %prefix.1), calls=%async_computation.2 | async-start | bytes 1048576 | tf_op jit(solution)/shard_map/all_to_all | solution.py:368
  66.5 3.8 %attention_sides.1.rest_4_ = f32[3,640,128]{2,1,0:T(8,128)S(1)} custom-call(s32[1,128]{1,0:T(1,128)S(1)} %bitcast.14, bf16[128,640]{1,0:T(8,128)(2,1)S(1)} %copy-done.11, s32[1,128]{1,0:T(1,128)S(1)} %bitcast.15, bf16[8,128,256]{2,1,0:T(8,128)(2,1)} %collective-permute-done.1.rest_0_.rest_1_, bf16[8,128,256]{2,1,0:T(8,128)(2,1)} %collective-permute-done.1.rest_0_.rest_1_, ...), custom_call_target="tpu_custom_call" | custom-call | flops 10000000000 | tf_op jit(solution)/shard_map/attention_sides/pallas_call | solution.py:347
  70.3 3.2 %attention_far.1 = (bf16[128,640]{1,0:T(8,128)(2,1)}, f32[16,128]{1,0:T(8,128)S(1)}) custom-call(s32[1,128]{1,0:T(1,128)S(1)} %bitcast.16, bf16[128,640]{1,0:T(8,128)(2,1)S(1)} %copy-done.11, s32[1,128]{1,0:T(1,128)S(1)} %bitcast.17, bf16[8,128,128]{2,1,0:T(8,128)(2,1)} %collective-permute-done.2.rest_0_, ...), custom_call_target="tpu_custom_call" | custom-call | flops 10000000000 | tf_op jit(solution)/shard_map/attention_far/pallas_call | solution.py:347
  73.5 8.5 %all-to-all-done.2.pre_ref = f32[32,8,512]{2,1,0:T(8,128)S(1)} async-done(((f32[32,8,512]{2,1,0:T(8,128)}), f32[32,8,512]{2,1,0:T(8,128)S(1)}, u32[]{:S(2)}, u32[]{:S(2)}) %all-to-all-start.2) | async-done | bytes 524320 | tf_op jit(solution)/shard_map/all_to_all | solution.py:368
  82.2 2.0 %collective-permute-start.10 = (f32[256,512]{1,0:T(8,128)S(1)}, f32[256,512]{1,0:T(8,128)S(1)}, u32[]{:S(2)}, u32[]{:S(2)}) collective-permute-start(f32[256,512]{1,0:T(8,128)S(1)} %get-tuple-element.38), channel_id=1, source_target_pairs={{0,4},{4,0},{8,12},{12,8},{16,20},{20,16},{24,28},{28,24},{32,36},... | collective-permute-start | bytes 1572872 | tf_op jit(solution)/shard_map/ppermute | solution.py:322
  84.1 1.5 %collective-permute-done.10.got_ref = f32[256,512]{1,0:T(8,128)S(1)} collective-permute-done((f32[256,512]{1,0:T(8,128)S(1)}, f32[256,512]{1,0:T(8,128)S(1)}, u32[]{:S(2)}, u32[]{:S(2)}) %collective-permute-start.10) | collective-permute-done | bytes 524320 | tf_op jit(solution)/shard_map/ppermute | solution.py:322
  86.3 1.3 %collective-permute-start.11 = (f32[8,128]{1,0:T(8,128)S(1)}, f32[8,128]{1,0:T(8,128)S(1)}, u32[]{:S(2)}, u32[]{:S(2)}) collective-permute-start(f32[8,128]{1,0:T(8,128)S(1)} %get-tuple-element.40.s0), channel_id=1, source_target_pairs={{0,1},{1,0},{2,3},{3,2},{4,5},{5,4},{6,7},{7,6},{8,9},{9,8},{10,11... | collective-permute-start | bytes 12296 | tf_op jit(solution)/shard_map/ppermute | solution.py:379
  87.6 2.6 %collective-permute-start.12 = (f32[8,128]{1,0:T(8,128)S(1)}, f32[8,128]{1,0:T(8,128)S(1)}, u32[]{:S(2)}, u32[]{:S(2)}) collective-permute-start(f32[8,128]{1,0:T(8,128)S(1)} %get-tuple-element.40.s0), channel_id=1, source_target_pairs={{0,2},{1,3},{2,0},{3,1},{4,6},{5,7},{6,4},{7,5},{8,10},{9,11},{10,... | collective-permute-start | bytes 12296 | tf_op jit(solution)/shard_map/ppermute | solution.py:379
  90.2 1.3 %collective-permute-done.12.s2 = f32[8,128]{1,0:T(8,128)S(1)} collective-permute-done((f32[8,128]{1,0:T(8,128)S(1)}, f32[8,128]{1,0:T(8,128)S(1)}, u32[]{:S(2)}, u32[]{:S(2)}) %collective-permute-start.12) | collective-permute-done | bytes 4128 | tf_op jit(solution)/shard_map/ppermute | solution.py:379
  91.6 2.3 %collective-permute-done.13.s3 = f32[8,128]{1,0:T(8,128)S(1)} collective-permute-done((f32[8,128]{1,0:T(8,128)S(1)}, f32[8,128]{1,0:T(8,128)S(1)}, u32[]{:S(2)}, u32[]{:S(2)}) %collective-permute-start.13) | collective-permute-done | bytes 4128 | tf_op jit(solution)/shard_map/ppermute | solution.py:379
  94.8 2.1 %collective-permute-start.14 = (bf16[32,128]{1,0:T(8,128)(2,1)S(1)}, bf16[32,128]{1,0:T(8,128)(2,1)S(1)}, u32[]{:S(2)}, u32[]{:S(2)}) collective-permute-start(bf16[32,128]{1,0:T(8,128)(2,1)S(1)} %get-tuple-element.43.own_ref), channel_id=1, source_target_pairs={{0,4},{4,0},{8,12},{12,8},{16,20},{20,16},{24,28},{28,24},{32,36},... | collective-permute-start | bytes 24584 | tf_op jit(solution)/shard_map/ppermute | solution.py:322
  97.8 15.8 %all_to_all.20.in_ref = bf16[32,32,128]{2,1,0:T(8,128)(2,1)S(1)} all-to-all(bf16[32,32,128]{2,1,0:T(8,128)(2,1)S(1)} %least.1), channel_id=1, replica_groups={{0,8,16,24,32,40,48,56,64,72,80,88,96,104,112,120,128,136,144,152,160,1..., dimensions={0} | all-to-all | bytes 524288 | tf_op jit(solution)/shard_map/all_to_all | solution.py:387
  (57 shorter events, 13.9 us)
Async XLA Ops:
  2.2 9.2 %copy-start = (bf16[128,1024]{1,0:T(8,128)(2,1)S(1)}, bf16[128,1024]{1,0:T(8,128)(2,1)}, u32[]{:S(2)}) copy-start(bf16[128,1024]{1,0:T(8,128)(2,1)} %x_ref.3) | copy-start | bytes 786436
  2.2 9.2 %copy-start.4 = (bf16[128,256]{1,0:T(8,128)(2,1)S(1)}, bf16[128,256]{1,0:T(8,128)(2,1)}, u32[]{:S(2)}) copy-start(bf16[128,256]{1,0:T(8,128)(2,1)} %b_ref.3) | copy-start | bytes 196612
  2.2 9.2 %copy-start.6 = (f32[128,16]{0,1:T(8,128)S(1)}, f32[128,16]{0,1:T(8,128)}, u32[]{:S(2)}) copy-start(f32[128,16]{0,1:T(8,128)} %param.19) | copy-start | bytes 24580
  2.2 9.2 %copy-start.8 = (f32[16]{0:T(128)S(1)}, f32[16]{0:T(128)}, u32[]{:S(2)}) copy-start(f32[16]{0:T(128)} %param.20) | copy-start | bytes 196
  2.2 9.2 %copy-start.9 = (s32[128]{0:T(128)S(1)}, s32[128]{0:T(128)}, u32[]{:S(2)}) copy-start(s32[128]{0:T(128)} %param.23) | copy-start | bytes 1540
  2.3 27.1 %all-to-all-start = ((bf16[8,128,256]{2,1,0:T(8,128)(2,1)}), bf16[8,128,256]{2,1,0:T(8,128)(2,1)S(1)}, u32[]{:S(2)}, u32[]{:S(2)}) async-start(bf16[8,128,256]{2,1,0:T(8,128)(2,1)} %broadcast_in_dim.19), calls=%async_computation | async-start | bytes 1048576 | tf_op jit(solution)/shard_map/all_to_all | solution.py:334
  13.8 3.6 %collective-permute-start = (f32[264,512]{1,0:T(8,128)S(1)}, f32[264,512]{1,0:T(8,128)S(1)}, u32[]{:S(2)}, u32[]{:S(2)}) collective-permute-start(f32[264,512]{1,0:T(8,128)S(1)} %get-tuple-element.26), channel_id=1, source_target_pairs={{0,4},{4,0},{8,12},{12,8},{16,20},{20,16},{24,28},{28,24},{32,36},... | collective-permute-start | bytes 1622024 | tf_op jit(solution)/shard_map/ppermute | solution.py:322
  29.4 13.5 %collective-permute-start.1 = (bf16[8,128,256]{2,1,0:T(8,128)(2,1)S(1)}, bf16[8,128,256]{2,1,0:T(8,128)(2,1)}, u32[]{:S(2)}, u32[]{:S(2)}) collective-permute-start(bf16[8,128,256]{2,1,0:T(8,128)(2,1)S(1)} %all-to-all-done.rest_0_.rest_1_), channel_id=1, source_target_pairs={{0,8},{4,12},{8,0},{12,4},{16,24},{20,28},{24,16},{28,20},{32,40},... | collective-permute-start | bytes 1572872 | tf_op jit(solution)/shard_map/ppermute | solution.py:322
  30.6 16.1 %collective-permute-start.3 = (bf16[8,128,256]{2,1,0:T(8,128)(2,1)S(1)}, bf16[8,128,256]{2,1,0:T(8,128)(2,1)}, u32[]{:S(2)}, u32[]{:S(2)}) collective-permute-start(bf16[8,128,256]{2,1,0:T(8,128)(2,1)S(1)} %all-to-all-done.rest_0_.rest_1_), channel_id=1, source_target_pairs={{0,24},{4,28},{8,16},{12,20},{16,8},{20,12},{24,0},{28,4},{32,56},... | collective-permute-start | bytes 1572872 | tf_op jit(solution)/shard_map/ppermute | solution.py:322
  32.4 20.1 %collective-permute-start.9 = (bf16[8,128,256]{2,1,0:T(8,128)(2,1)S(1)}, bf16[8,128,256]{2,1,0:T(8,128)(2,1)}, u32[]{:S(2)}, u32[]{:S(2)}) collective-permute-start(bf16[8,128,256]{2,1,0:T(8,128)(2,1)S(1)} %all-to-all-done.rest_0_.rest_1_), channel_id=1, source_target_pairs={{0,4},{4,0},{8,12},{12,8},{16,20},{20,16},{24,28},{28,24},{32,36},... | collective-permute-start | bytes 1572872 | tf_op jit(solution)/shard_map/ppermute | solution.py:322
  33.5 25.5 %all-to-all-start.1 = ((f32[32,8,640]{2,1,0:T(8,128)}), f32[32,8,640]{2,1,0:T(8,128)S(1)}, u32[]{:S(2)}, u32[]{:S(2)}) async-start(f32[32,8,640]{2,1,0:T(8,128)} %chip_state.1), calls=%async_computation.1 | async-start | bytes 1310720 | tf_op jit(solution)/shard_map/all_to_all | solution.py:361
  43.9 8.6 %copy-start.11 = (bf16[128,640]{1,0:T(8,128)(2,1)S(1)}, bf16[128,640]{1,0:T(8,128)(2,1)}, u32[]{:S(2)}) copy-start(bf16[128,640]{1,0:T(8,128)(2,1)} %q_ref.5) | copy-start | bytes 491524
  43.9 12.1 %collective-permute-start.2 = (bf16[8,128,128]{2,1,0:T(8,128)(2,1)S(1)}, bf16[8,128,128]{2,1,0:T(8,128)(2,1)}, u32[]{:S(2)}, u32[]{:S(2)}) collective-permute-start(bf16[8,128,128]{2,1,0:T(8,128)(2,1)S(1)} %slice.8), channel_id=1, source_target_pairs={{0,24},{4,28},{8,16},{12,20},{16,8},{20,12},{24,0},{28,4},{32,56},... | collective-permute-start | bytes 786440 | tf_op jit(solution)/shard_map/ppermute | solution.py:322
  47.7 11.2 %collective-permute-start.4 = (bf16[8,128,128]{2,1,0:T(8,128)(2,1)S(1)}, bf16[8,128,128]{2,1,0:T(8,128)(2,1)}, u32[]{:S(2)}, u32[]{:S(2)}) collective-permute-start(bf16[8,128,128]{2,1,0:T(8,128)(2,1)S(1)} %slice.9), channel_id=1, source_target_pairs={{0,8},{4,12},{8,0},{12,4},{16,24},{20,28},{24,16},{28,20},{32,40},... | collective-permute-start | bytes 786440 | tf_op jit(solution)/shard_map/ppermute | solution.py:322
  47.8 17.5 %collective-permute-start.7 = (bf16[8,128,256]{2,1,0:T(8,128)(2,1)}, bf16[8,128,256]{2,1,0:T(8,128)(2,1)}, u32[]{:S(2)}, u32[]{:S(2)}) collective-permute-start(bf16[8,128,256]{2,1,0:T(8,128)(2,1)} %collective-permute-done.1.rest_0_.rest_1_), channel_id=1, source_target_pairs={{0,4},{4,0},{8,12},{12,8},{16,20},{20,16},{24,28},{28,24},{32,36},... | collective-permute-start | bytes 1572872 | tf_op jit(solution)/shard_map/ppermute | solution.py:322
  52.4 12.9 %collective-permute-start.8 = (bf16[8,128,256]{2,1,0:T(8,128)(2,1)}, bf16[8,128,256]{2,1,0:T(8,128)(2,1)}, u32[]{:S(2)}, u32[]{:S(2)}) collective-permute-start(bf16[8,128,256]{2,1,0:T(8,128)(2,1)} %collective-permute-done.3.rest_4_.rest_5_), channel_id=1, source_target_pairs={{0,4},{4,0},{8,12},{12,8},{16,20},{20,16},{24,28},{28,24},{32,36},... | collective-permute-start | bytes 1572872 | tf_op jit(solution)/shard_map/ppermute | solution.py:322
  56.0 14.3 %collective-permute-start.5 = (bf16[8,128,128]{2,1,0:T(8,128)(2,1)}, bf16[8,128,128]{2,1,0:T(8,128)(2,1)S(1)}, u32[]{:S(2)}, u32[]{:S(2)}) collective-permute-start(bf16[8,128,128]{2,1,0:T(8,128)(2,1)} %collective-permute-done.2.rest_0_), channel_id=1, source_target_pairs={{0,4},{4,0},{8,12},{12,8},{16,20},{20,16},{24,28},{28,24},{32,36},... | collective-permute-start | bytes 786440 | tf_op jit(solution)/shard_map/ppermute | solution.py:322
  58.9 11.4 %collective-permute-start.6 = (bf16[8,128,128]{2,1,0:T(8,128)(2,1)}, bf16[8,128,128]{2,1,0:T(8,128)(2,1)S(1)}, u32[]{:S(2)}, u32[]{:S(2)}) collective-permute-start(bf16[8,128,128]{2,1,0:T(8,128)(2,1)} %collective-permute-done.4.rest_1_), channel_id=1, source_target_pairs={{0,4},{4,0},{8,12},{12,8},{16,20},{20,16},{24,28},{28,24},{32,36},... | collective-permute-start | bytes 786440 | tf_op jit(solution)/shard_map/ppermute | solution.py:322
  59.9 22.2 %all-to-all-start.2 = ((f32[32,8,512]{2,1,0:T(8,128)}), f32[32,8,512]{2,1,0:T(8,128)S(1)}, u32[]{:S(2)}, u32[]{:S(2)}) async-start(f32[32,8,512]{2,1,0:T(8,128)} %prefix.1), calls=%async_computation.2 | async-start | bytes 1048576 | tf_op jit(solution)/shard_map/all_to_all | solution.py:368
  82.2 3.5 %collective-permute-start.10 = (f32[256,512]{1,0:T(8,128)S(1)}, f32[256,512]{1,0:T(8,128)S(1)}, u32[]{:S(2)}, u32[]{:S(2)}) collective-permute-start(f32[256,512]{1,0:T(8,128)S(1)} %get-tuple-element.38), channel_id=1, source_target_pairs={{0,4},{4,0},{8,12},{12,8},{16,20},{20,16},{24,28},{28,24},{32,36},... | collective-permute-start | bytes 1572872 | tf_op jit(solution)/shard_map/ppermute | solution.py:322
  86.3 4.0 %collective-permute-start.11 = (f32[8,128]{1,0:T(8,128)S(1)}, f32[8,128]{1,0:T(8,128)S(1)}, u32[]{:S(2)}, u32[]{:S(2)}) collective-permute-start(f32[8,128]{1,0:T(8,128)S(1)} %get-tuple-element.40.s0), channel_id=1, source_target_pairs={{0,1},{1,0},{2,3},{3,2},{4,5},{5,4},{6,7},{7,6},{8,9},{9,8},{10,11... | collective-permute-start | bytes 12296 | tf_op jit(solution)/shard_map/ppermute | solution.py:379
  87.6 4.0 %collective-permute-start.12 = (f32[8,128]{1,0:T(8,128)S(1)}, f32[8,128]{1,0:T(8,128)S(1)}, u32[]{:S(2)}, u32[]{:S(2)}) collective-permute-start(f32[8,128]{1,0:T(8,128)S(1)} %get-tuple-element.40.s0), channel_id=1, source_target_pairs={{0,2},{1,3},{2,0},{3,1},{4,6},{5,7},{6,4},{7,5},{8,10},{9,11},{10,... | collective-permute-start | bytes 12296 | tf_op jit(solution)/shard_map/ppermute | solution.py:379
  90.2 3.7 %collective-permute-start.13 = (f32[8,128]{1,0:T(8,128)S(1)}, f32[8,128]{1,0:T(8,128)S(1)}, u32[]{:S(2)}, u32[]{:S(2)}) collective-permute-start(f32[8,128]{1,0:T(8,128)S(1)} %get-tuple-element.40.s0), channel_id=1, source_target_pairs={{0,3},{1,2},{2,1},{3,0},{4,7},{5,6},{6,5},{7,4},{8,11},{9,10},{10,... | collective-permute-start | bytes 12296 | tf_op jit(solution)/shard_map/ppermute | solution.py:379
  94.8 2.9 %collective-permute-start.14 = (bf16[32,128]{1,0:T(8,128)(2,1)S(1)}, bf16[32,128]{1,0:T(8,128)(2,1)S(1)}, u32[]{:S(2)}, u32[]{:S(2)}) collective-permute-start(bf16[32,128]{1,0:T(8,128)(2,1)S(1)} %get-tuple-element.43.own_ref), channel_id=1, source_target_pairs={{0,4},{4,0},{8,12},{12,8},{16,20},{20,16},{24,28},{28,24},{32,36},... | collective-permute-start | bytes 24584 | tf_op jit(solution)/shard_map/ppermute | solution.py:322
  (8 other events, 22.0 us)
